TPU v7x, 32 devices: a whole 2x2x4 slice. The times are simulated.
32 devices in a mesh: leaf: 16 (over z, y, x), panel: 2 (over core).
Axes of the slice: x: 2, y: 2, z: 4, core: 2. Of those that a mesh axis runs over, the one named last changes fastest.
Arguments:
- rhs: float32 [32768, 128], P(('leaf', 'panel')), may hold values from -6 to 6
- leaf_q: float32 [64, 512, 512], P(('leaf', 'panel')), may hold values from -0.25 to 0.25
- leaf_e: float32 [64, 384, 384], P(('leaf', 'panel')), may hold values from -0.3125 to 0.3125
- leaf_f: float32 [64, 128, 384], P(('leaf', 'panel')), may hold values from -0.15625 to 0.15625
- leaf_g: float32 [64, 384, 128], P(('leaf', 'panel')), may hold values from -0.25 to 0.25
- mid_q: float32 [32, 256, 256], P(('leaf', 'panel')), may hold values from -0.375 to 0.375
- mid_e: float32 [32, 128, 128], P(('leaf', 'panel')), may hold values from -0.5 to 0.5
- mid_f: float32 [32, 128, 128], P(('leaf', 'panel')), may hold values from -0.25 to 0.25
- mid_g: float32 [32, 128, 128], P(('leaf', 'panel')), may hold values from -0.25 to 0.25
- pair_q: float32 [16, 256, 256], P('leaf'), may hold values from -0.375 to 0.375
- pair_e: float32 [16, 128, 128], P('leaf'), may hold values from -0.5 to 0.5
- pair_f: float32 [16, 128, 128], P('leaf'), may hold values from -0.25 to 0.25
- pair_g: float32 [16, 128, 128], P('leaf'), may hold values from -0.25 to 0.25
- up_q: float32 [16, 256, 256], P('leaf'), may hold values from -0.375 to 0.375
- up_e: float32 [16, 128, 128], P('leaf'), may hold values from -0.5 to 0.5
- up_f: float32 [16, 128, 128], P('leaf'), may hold values from -0.25 to 0.25
- up_g: float32 [16, 128, 128], P('leaf'), may hold values from -0.25 to 0.25
Outputs:
- solution: float32 [32768, 128], P(('leaf', 'panel'))
All inputs are finite; a program needn't handle non-finite values.
Results may differ from a plain program's by a relative error of at most 0.0003.
Values sent between devices are 32-bit elements; how exact they have to be, the bound alone decides.
No kernel may reach another device: no remote copies, remote signals or barrier semaphores. Data moves between devices by JAX's collectives and lax.ppermute only.
A program may use at most 128 MiB of HBM per device.

v0:
```python
import jax
import jax.numpy as jnp
from jax import lax
from jax.sharding import PartitionSpec as P

highest_precision = lax.Precision.HIGHEST


def partner(value, axis, bit):
    mask = 2**bit
    pairs = [(source, source ^ mask) for source in range(lax.axis_size(axis))]
    return lax.ppermute(value, axis, pairs)


def eliminate(basis, inverse_factor, coupling_block, block_in):
    eliminated_rows = inverse_factor.shape[1]
    coefficient_rows = jnp.einsum("nij,nic->njc", basis, block_in, precision=highest_precision)
    lower_block_part = jnp.einsum(
        "gwe,gel->gwl",
        inverse_factor,
        coefficient_rows[:, :eliminated_rows],
        precision=highest_precision,
    )
    reduced_system = coefficient_rows[:, eliminated_rows:] - jnp.einsum(
        "gwe,gel->gwl", coupling_block, lower_block_part, precision=highest_precision
    )
    return (lower_block_part, reduced_system)


def substitute(basis, back_map, lower_block_part, upper_part):
    first_part = lower_block_part - jnp.einsum(
        "gwe,gel->gwl", back_map, upper_part, precision=highest_precision
    )
    stacked = jnp.concatenate([first_part, upper_part], axis=1)
    return jnp.einsum("nij,njc->nic", basis, stacked, precision=highest_precision)


def unpack_row(packed_row, rank_rows):
    square_big = 4 * rank_rows * rank_rows
    square_small = rank_rows * rank_rows
    basis = packed_row[:square_big].reshape(1, 2 * rank_rows, 2 * rank_rows)
    inverse_factor = packed_row[square_big : square_big + square_small].reshape(
        1, rank_rows, rank_rows
    )
    coupling_block = packed_row[square_big + square_small : square_big + 2 * square_small].reshape(
        1, rank_rows, rank_rows
    )
    back_map = packed_row[square_big + 2 * square_small : square_big + 3 * square_small].reshape(
        1, rank_rows, rank_rows
    )
    return (basis, inverse_factor, coupling_block, back_map)


def local(
    rhs,
    leaf_q,
    leaf_e,
    leaf_f,
    leaf_g,
    mid_q,
    mid_e,
    mid_f,
    mid_g,
    pair_q,
    pair_e,
    pair_f,
    pair_g,
    up_q,
    up_e,
    up_f,
    up_g,
):
    count_leaf = lax.axis_size("leaf")
    position = lax.axis_index("leaf")
    depth_levels = count_leaf.bit_length() - 1
    rank_rows = up_e.shape[1]
    leaf_size = leaf_q.shape[1]
    leaves_here = leaf_q.shape[0]
    columns = rhs.shape[1]
    leaf_lower, reduced_system = eliminate(
        leaf_q, leaf_e, leaf_f, rhs.reshape(leaves_here, leaf_size, columns)
    )
    offset = 0
    pairs = leaves_here // 2
    stacked = reduced_system.reshape(pairs, 2 * rank_rows, columns)
    lower_block_part, reduced_system = eliminate(mid_q, mid_e, mid_f, stacked)
    mid_saved = [(lower_block_part, offset, pairs)]
    joined = lax.all_gather(reduced_system, "panel", axis=1, tiled=True)
    pair_lower, node_out = eliminate(pair_q, pair_e, pair_f, joined)
    flat_factors = jnp.concatenate(
        [up_q.reshape(-1), up_e.reshape(-1), up_f.reshape(-1), up_g.reshape(-1)]
    )
    level_row = jnp.zeros((), jnp.int32)
    for bit in range(depth_levels):
        level_row = level_row + (position % (2 << bit) == 0).astype(jnp.int32)
    level_onehot = (jnp.arange(depth_levels + 1, dtype=jnp.int32) == level_row).astype(jnp.float32)
    packet = level_onehot[:, None] * flat_factors[None, :]
    upper_saved = []
    for bit in range(depth_levels):
        tail_rows = packet[bit:]
        node_flat = node_out.reshape(-1)
        node_len = node_flat.shape[0]
        side_index = lax.axis_index("panel")
        half_width = tail_rows.shape[1] // 2
        own_half = lax.dynamic_slice_in_dim(tail_rows, side_index * half_width, half_width, 1)
        outgoing = jnp.concatenate([node_flat, own_half.reshape(-1)])
        incoming = partner(outgoing, "leaf", bit)
        partner_half = incoming[node_len:].reshape(tail_rows.shape[0], half_width)
        partner_tail = lax.all_gather(partner_half, "panel", axis=1, tiled=True)
        packet = jnp.concatenate([packet[:bit], tail_rows + partner_tail], axis=0)
        partner_node = incoming[:node_len].reshape(node_out.shape)
        upper_side = position // (1 << bit) % 2 == 1
        first_child = jnp.where(upper_side, partner_node, node_out)
        second_child = jnp.where(upper_side, node_out, partner_node)
        basis, inverse_factor, coupling_block, back_map = unpack_row(packet[bit], rank_rows)
        lower_block_part, node_out = eliminate(
            basis,
            inverse_factor,
            coupling_block,
            jnp.concatenate([first_child, second_child], axis=1),
        )
        upper_saved.append((lower_block_part, basis, back_map))
    apex_inverse = unpack_row(packet[depth_levels], rank_rows)[1]
    upper_part = jnp.einsum("gwe,gel->gwl", apex_inverse, node_out, precision=highest_precision)
    for bit in range(depth_levels - 1, -1, -1):
        lower_block_part, basis, back_map = upper_saved[bit]
        whole_x = substitute(basis, back_map, lower_block_part, upper_part)
        upper_side = position // (1 << bit) % 2 == 1
        upper_part = jnp.where(upper_side, whole_x[:, rank_rows:], whole_x[:, :rank_rows])
    whole_x = substitute(pair_q, pair_g, pair_lower, upper_part)
    side_index = lax.axis_index("panel")
    upper_part = lax.dynamic_slice_in_dim(whole_x, side_index * rank_rows, rank_rows, 1)
    for lower_block_part, offset, pairs in reversed(mid_saved):
        whole_x = substitute(mid_q, mid_g, lower_block_part, upper_part)
        upper_part = whole_x.reshape(2 * pairs, rank_rows, columns)
    result = substitute(leaf_q, leaf_g, leaf_lower, upper_part)
    return result.reshape(leaves_here * leaf_size, columns)


def solution(mesh):
    in_specs = (
        P(("leaf", "panel"), None),
        P(("leaf", "panel"), None, None),
        P(("leaf", "panel"), None, None),
        P(("leaf", "panel"), None, None),
        P(("leaf", "panel"), None, None),
        P(("leaf", "panel"), None, None),
        P(("leaf", "panel"), None, None),
        P(("leaf", "panel"), None, None),
        P(("leaf", "panel"), None, None),
        P("leaf", None, None),
        P("leaf", None, None),
        P("leaf", None, None),
        P("leaf", None, None),
        P("leaf", None, None),
        P("leaf", None, None),
        P("leaf", None, None),
        P("leaf", None, None),
    )
    out_specs = P(("leaf", "panel"), None)
    return jax.shard_map(local, mesh=mesh, in_specs=in_specs, out_specs=out_specs, check_vma=False)
```

profile of v0, /device:TPU:0, one launch (start us, length us, event | category | flops | bytes accessed | tf_op | source)
XLA Modules:
  0.0 231.2 jit_solution(15760812993998475329)
XLA Ops:
  6.6 1.2 copy.45
  8.2 4.6 %fusion.85 = f32[2,512,128]{2,1,0:T(8,128)S(1)} fusion(f32[2,512,512]{2,1,0:T(8,128)S(1)} %copy-done, f32[2,512,128]{2,1,0:T(8,128)} %bitcast.276), kind=kOutput, calls=%fused_computation.156 | convolution fusion | flops 805306368 | bytes 3145728 | tf_op jit(solution)/shard_map/nij,nic->njc/dot_general | solution.py:17
  12.8 1.5 fusion.19
  16.8 2.0 all_gather.15
  21.3 1.4 constant_dynamic-slice_fusion.1
  22.7 2.1 reshape.382
  24.8 2.9 %collective-permute-start = (f32[303104]{0:T(1024)S(1)}, f32[303104]{0:T(1024)S(1)}, u32[]{:S(2)}, u32[]{:S(2)}) collective-permute-start(f32[303104]{0:T(1024)S(1)} %pad_maximum_fusion), channel_id=1, source_target_pairs={{0,2},{2,0},{4,6},{6,4},{8,10},{10,8},{12,14},{14,12},{16,18},{18,... | collective-permute-start | bytes 3637256 | tf_op jit(solution)/shard_map/ppermute | solution.py:12
  27.7 27.0 %collective-permute-done = f32[303104]{0:T(1024)S(1)} collective-permute-done((f32[303104]{0:T(1024)S(1)}, f32[303104]{0:T(1024)S(1)}, u32[]{:S(2)}, u32[]{:S(2)}) %collective-permute-start) | collective-permute-done | bytes 1212448 | tf_op jit(solution)/shard_map/ppermute | solution.py:12
  54.7 1.0 copy-done.8
  55.9 1.6 reshape.383
  58.7 13.4 %all-gather.4.cloned.1.call-done = f32[5,114688]{1,0:T(8,128)} async-done(((f32[5,57344]{1,0:T(8,128)}), f32[5,114688]{1,0:T(8,128)}) %all-gather.4.cloned.1.call-update) | async-done | bytes 2293776 | tf_op jit(solution)/shard_map/all_gather | solution.py:109
  72.0 2.5 %fusion.15 = f32[5,114688]{1,0:T(8,128)S(1)} fusion(f32[5,114688]{1,0:T(8,128)} %all-gather.4.cloned.1.call-done, f32[114688]{0:T(1024)S(1)} %copy-done.5, f32[5]{0:T(128)S(1)} %compare_convert_fusion), kind=kLoop, calls=%fused_computation.44 | loop fusion | flops 1146880 | bytes 5046292 | tf_op jit(solution)/shard_map/add | solution.py:110
  76.3 1.7 slice.273
  78.1 1.2 dynamic-slice_bitcast_fusion
  81.0 1.8 collective-permute-start.1
  82.8 22.2 %collective-permute-done.1 = f32[245760]{0:T(1024)S(1)} collective-permute-done((f32[245760]{0:T(1024)S(1)}, f32[245760]{0:T(1024)S(1)}, u32[]{:S(2)}, u32[]{:S(2)}) %collective-permute-start.1) | collective-permute-done | bytes 983072 | tf_op jit(solution)/shard_map/ppermute | solution.py:12
  106.0 1.4 reshape.393
  107.5 1.5 fusion.64
  109.0 9.9 %all-gather.6.cloned.1.call-done = f32[4,114688]{1,0:T(4,128)} async-done(((f32[4,57344]{1,0:T(4,128)}), f32[4,114688]{1,0:T(4,128)}) %all-gather.6.cloned.1.call-update) | async-done | bytes 1835024 | tf_op jit(solution)/shard_map/all_gather | solution.py:109
  118.9 3.3 %slice_add_fusion.2 = f32[4,114688]{1,0:T(4,128)S(1)} fusion(f32[4,114688]{1,0:T(4,128)} %all-gather.6.cloned.1.call-done, f32[5,114688]{1,0:T(8,128)} %copy-done.2), kind=kLoop, calls=%fused_computation.151 | loop fusion | flops 458752 | bytes 5505024 | tf_op jit(solution)/shard_map/add | solution.py:110
  123.9 1.7 slice.282
  125.7 1.3 constant_dynamic-slice_fusion
  127.0 1.4 reshape.401
  128.4 1.5 convolution_bitcast_fusion.8
  129.8 1.0 fusion.48
  130.9 1.1 fusion.11
  132.0 1.1 pad_maximum_fusion.2
  133.1 1.8 collective-permute-start.2
  135.0 17.3 %collective-permute-done.2 = f32[188416]{0:T(1024)S(1)} collective-permute-done((f32[188416]{0:T(1024)S(1)}, f32[188416]{0:T(1024)S(1)}, u32[]{:S(2)}, u32[]{:S(2)}) %collective-permute-start.2) | collective-permute-done | bytes 753696 | tf_op jit(solution)/shard_map/ppermute | solution.py:12
  153.2 1.3 reshape.402
  154.5 1.5 fusion.66
  156.0 10.0 %all-gather.8.cloned.1.call-done = f32[3,114688]{1,0:T(4,128)} async-done(((f32[3,57344]{1,0:T(4,128)}), f32[3,114688]{1,0:T(4,128)}) %all-gather.8.cloned.1.call-update) | async-done | bytes 1376272 | tf_op jit(solution)/shard_map/all_gather | solution.py:109
  166.0 2.8 %slice_add_fusion.1 = f32[3,114688]{1,0:T(4,128)S(1)} fusion(f32[3,114688]{1,0:T(4,128)} %all-gather.8.cloned.1.call-done, f32[4,114688]{1,0:T(4,128)} %copy-done.1), kind=kLoop, calls=%fused_computation.150 | loop fusion | flops 344064 | bytes 4128768 | tf_op jit(solution)/shard_map/add | solution.py:110
  170.4 1.4 slice.291
  172.0 1.1 dynamic-slice_bitcast_fusion.1
  173.1 1.4 convolution_bitcast_fusion.7
  175.8 2.7 %collective-permute-start.3 = (f32[131072]{0:T(1024)}, f32[131072]{0:T(1024)}, u32[]{:S(2)}, u32[]{:S(2)}) collective-permute-start(f32[131072]{0:T(1024)} %pad_maximum_fusion.3), channel_id=1, source_target_pairs={{0,16},{2,18},{4,20},{6,22},{8,24},{10,26},{12,28},{14,30},{16,0},... | collective-permute-start | bytes 1572872 | tf_op jit(solution)/shard_map/ppermute | solution.py:12
  179.2 23.2 %collective-permute-done.3 = f32[131072]{0:T(1024)} collective-permute-done((f32[131072]{0:T(1024)}, f32[131072]{0:T(1024)}, u32[]{:S(2)}, u32[]{:S(2)}) %collective-permute-start.3) | collective-permute-done | bytes 524320 | tf_op jit(solution)/shard_map/ppermute | solution.py:12
  202.4 1.0 slice.294
  203.4 1.1 reshape.412
  204.5 2.9 %all_gather.19 = f32[2,114688]{1,0:T(2,128)S(1)} all-gather(f32[2,57344]{1,0:T(2,128)} %reshape.412), channel_id=1, replica_groups=mesh['leaf'=16,'panel'=2] {'panel'}, dimensions={1}, use_global_device_ids=true | all-gather | bytes 1376256 | tf_op jit(solution)/shard_map/all_gather | solution.py:109
  207.4 2.2 slice_add_fusion
  212.8 1.1 fusion.46
  213.9 1.0 fusion.14
  214.9 1.0 fusion.86
  216.0 1.0 fusion.7
  221.4 2.2 convolution_bitcast_fusion
  223.6 1.0 copy.37
  (144 shorter events, 24.6 us)
Async XLA Ops:
  6.5 1.7 copy-start
  6.5 65.5 %all-gather.4.cloned.1.call-start = ((), (), s32[]{:S(2)}) async-start(), calls=%async_computation | async-start | bytes 5505024 | tf_op jit(solution)/shard_map/all_gather | solution.py:109
  6.5 6.2 %copy-start.9 = (f32[2,384,384]{2,1,0:T(8,128)S(1)}, f32[2,384,384]{2,1,0:T(8,128)}, u32[]{:S(2)}) copy-start(f32[2,384,384]{2,1,0:T(8,128)} %param.19) | copy-start | bytes 3538948
  8.2 7.0 %copy-start.24 = (f32[2,128,384]{2,1,0:T(8,128)S(1)}, f32[2,128,384]{2,1,0:T(8,128)}, u32[]{:S(2)}) copy-start(f32[2,128,384]{2,1,0:T(8,128)} %param.20) | copy-start | bytes 1179652
  12.8 3.1 %copy-start.12 = (f32[1,256,256]{2,1,0:T(8,128)S(1)}, f32[1,256,256]{2,1,0:T(8,128)}, u32[]{:S(2)}) copy-start(f32[1,256,256]{2,1,0:T(8,128)} %param.22) | copy-start | bytes 786436
  12.8 3.5 %copy-start.34 = (f32[1,128,128]{2,1,0:T(8,128)S(1)}, f32[1,128,128]{2,1,0:T(8,128)}, u32[]{:S(2)}) copy-start(f32[1,128,128]{2,1,0:T(8,128)} %param.23) | copy-start | bytes 196612
  12.8 3.7 %copy-start.36 = (f32[1,128,128]{2,1,0:T(8,128)S(1)}, f32[1,128,128]{2,1,0:T(8,128)}, u32[]{:S(2)}) copy-start(f32[1,128,128]{2,1,0:T(8,128)} %param.24) | copy-start | bytes 196612
  12.8 6.0 %copy-start.10 = (f32[1,256,256]{2,1,0:T(8,128)S(1)}, f32[1,256,256]{2,1,0:T(8,128)}, u32[]{:S(2)}) copy-start(f32[1,256,256]{2,1,0:T(8,128)} %param.26) | copy-start | bytes 786436
  14.4 0.8 copy-start.6
  15.2 3.9 %copy-start.35 = (f32[1,128,128]{2,1,0:T(8,128)S(1)}, f32[1,128,128]{2,1,0:T(8,128)}, u32[]{:S(2)}) copy-start(f32[1,128,128]{2,1,0:T(8,128)} %param.27) | copy-start | bytes 196612
  15.2 4.8 %copy-start.37 = (f32[1,128,128]{2,1,0:T(8,128)S(1)}, f32[1,128,128]{2,1,0:T(8,128)}, u32[]{:S(2)}) copy-start(f32[1,128,128]{2,1,0:T(8,128)} %param.28) | copy-start | bytes 196612
  15.2 5.2 %copy-start.31 = (f32[1,128,128]{2,1,0:T(8,128)S(1)}, f32[1,128,128]{2,1,0:T(8,128)}, u32[]{:S(2)}) copy-start(f32[1,128,128]{2,1,0:T(8,128)} %param.33) | copy-start | bytes 196612
  15.2 5.2 %copy-start.32 = (f32[1,128,128]{2,1,0:T(8,128)S(1)}, f32[1,128,128]{2,1,0:T(8,128)}, u32[]{:S(2)}) copy-start(f32[1,128,128]{2,1,0:T(8,128)} %param.32) | copy-start | bytes 196612
  15.2 5.2 %copy-start.33 = (f32[1,128,128]{2,1,0:T(8,128)S(1)}, f32[1,128,128]{2,1,0:T(8,128)}, u32[]{:S(2)}) copy-start(f32[1,128,128]{2,1,0:T(8,128)} %param.31) | copy-start | bytes 196612
  16.5 2.3 copy-start.18
  19.4 0.6 copy-start.16
  20.5 0.8 copy-start.4
  24.8 29.9 %collective-permute-start = (f32[303104]{0:T(1024)S(1)}, f32[303104]{0:T(1024)S(1)}, u32[]{:S(2)}, u32[]{:S(2)}) collective-permute-start(f32[303104]{0:T(1024)S(1)} %pad_maximum_fusion), channel_id=1, source_target_pairs={{0,2},{2,0},{4,6},{6,4},{8,10},{10,8},{12,14},{14,12},{16,18},{18,... | collective-permute-start | bytes 3637256 | tf_op jit(solution)/shard_map/ppermute | solution.py:12
  54.7 1.0 copy-start.8
  57.4 14.6 %copy-start.5 = (f32[114688]{0:T(1024)S(1)}, f32[114688]{0:T(1024)}, u32[]{:S(2)}) copy-start(f32[114688]{0:T(1024)} %copy-done.4) | copy-start | bytes 1376260
  57.5 61.5 %all-gather.6.cloned.1.call-start = ((), (), s32[]{:S(2)}) async-start(), calls=%async_computation.1 | async-start | bytes 2752512 | tf_op jit(solution)/shard_map/all_gather | solution.py:109
  74.5 1.8 copy-start.2
  80.3 0.6 copy-start.20
  81.0 24.0 %collective-permute-start.1 = (f32[245760]{0:T(1024)S(1)}, f32[245760]{0:T(1024)S(1)}, u32[]{:S(2)}, u32[]{:S(2)}) collective-permute-start(f32[245760]{0:T(1024)S(1)} %pad_maximum_fusion.1), channel_id=1, source_target_pairs={{0,4},{2,6},{4,0},{6,2},{8,12},{10,14},{12,8},{14,10},{16,20},{18,... | collective-permute-start | bytes 2949128 | tf_op jit(solution)/shard_map/ppermute | solution.py:12
  105.0 1.0 copy-start.14
  107.4 58.6 %all-gather.8.cloned.1.call-start = ((), (), s32[]{:S(2)}) async-start(), calls=%async_computation.2 | async-start | bytes 2752512 | tf_op jit(solution)/shard_map/all_gather | solution.py:109
  122.2 1.6 copy-start.1
  130.9 1.1 copy-start.22
  133.1 19.1 %collective-permute-start.2 = (f32[188416]{0:T(1024)S(1)}, f32[188416]{0:T(1024)S(1)}, u32[]{:S(2)}, u32[]{:S(2)}) collective-permute-start(f32[188416]{0:T(1024)S(1)} %pad_maximum_fusion.2), channel_id=1, source_target_pairs={{0,8},{2,10},{4,12},{6,14},{8,0},{10,2},{12,4},{14,6},{16,24},{18,... | collective-permute-start | bytes 2261000 | tf_op jit(solution)/shard_map/ppermute | solution.py:12
  152.3 0.9 copy-start.15
  168.8 1.6 copy-start.3
  171.9 2.8 %copy-start.30 = (f32[1,16384]{1,0:T(1,128)S(1)}, f32[1,16384]{1,0:T(1,128)}, u32[]{:S(2)}) copy-start(f32[1,16384]{1,0:T(1,128)} %get-tuple-element.12) | copy-start | bytes 196612
  172.0 6.5 %copy-start.17 = (f32[128,128]{0,1:T(8,128)S(1)}, f32[128,128]{0,1:T(8,128)}, u32[]{:S(2)}) copy-start(f32[128,128]{0,1:T(8,128)} %copy-done.16) | copy-start | bytes 196612
  175.8 26.6 %collective-permute-start.3 = (f32[131072]{0:T(1024)}, f32[131072]{0:T(1024)}, u32[]{:S(2)}, u32[]{:S(2)}) collective-permute-start(f32[131072]{0:T(1024)} %pad_maximum_fusion.3), channel_id=1, source_target_pairs={{0,16},{2,18},{4,20},{6,22},{8,24},{10,26},{12,28},{14,30},{16,0},... | collective-permute-start | bytes 1572872 | tf_op jit(solution)/shard_map/ppermute | solution.py:12
  211.2 6.2 %copy-start.29 = (f32[1,16384]{1,0:T(1,128)S(1)}, f32[1,16384]{1,0:T(1,128)}, u32[]{:S(2)}) copy-start(f32[1,16384]{1,0:T(1,128)} %get-tuple-element.11) | copy-start | bytes 196612
  211.2 6.9 %copy-start.23 = (f32[128,128]{1,0:T(8,128)S(1)}, f32[128,128]{1,0:T(8,128)}, u32[]{:S(2)}) copy-start(f32[128,128]{1,0:T(8,128)} %copy-done.22) | copy-start | bytes 196612
  211.2 6.9 %copy-start.28 = (f32[1,16384]{1,0:T(1,128)S(1)}, f32[1,16384]{1,0:T(1,128)}, u32[]{:S(2)}) copy-start(f32[1,16384]{1,0:T(1,128)} %get-tuple-element.8) | copy-start | bytes 196612
  212.8 6.0 %copy-start.21 = (f32[128,128]{1,0:T(8,128)S(1)}, f32[128,128]{1,0:T(8,128)}, u32[]{:S(2)}) copy-start(f32[128,128]{1,0:T(8,128)} %copy-done.20) | copy-start | bytes 196612
  212.8 6.0 %copy-start.27 = (f32[1,16384]{1,0:T(1,128)S(1)}, f32[1,16384]{1,0:T(1,128)}, u32[]{:S(2)}) copy-start(f32[1,16384]{1,0:T(1,128)} %get-tuple-element.5) | copy-start | bytes 196612
  217.0 2.4 %copy-start.26 = (f32[128,128]{1,0:T(8,128)S(1)}, f32[128,128]{1,0:T(8,128)}, u32[]{:S(2)}) copy-start(f32[128,128]{1,0:T(8,128)} %copy.33) | copy-start | bytes 196612
  217.0 2.4 %copy-start.38 = (f32[1,128,128]{2,1,0:T(8,128)S(1)}, f32[1,128,128]{2,1,0:T(8,128)}, u32[]{:S(2)}) copy-start(f32[1,128,128]{2,1,0:T(8,128)} %param.29) | copy-start | bytes 196612
  217.4 2.3 copy-start.11
  217.7 2.4 %copy-start.19 = (f32[128,128]{0,1:T(8,128)S(1)}, f32[128,128]{0,1:T(8,128)}, u32[]{:S(2)}) copy-start(f32[128,128]{0,1:T(8,128)} %copy-done.18) | copy-start | bytes 196612
  217.7 2.4 %copy-start.39 = (f32[1,128,128]{2,1,0:T(8,128)S(1)}, f32[1,128,128]{2,1,0:T(8,128)}, u32[]{:S(2)}) copy-start(f32[1,128,128]{2,1,0:T(8,128)} %param.25) | copy-start | bytes 196612
  217.7 2.7 %copy-start.13 = (f32[1,256,256]{2,1,0:T(8,128)S(1)}, f32[1,256,256]{2,1,0:T(8,128)}, u32[]{:S(2)}) copy-start(f32[1,256,256]{2,1,0:T(8,128)} %param.22) | copy-start | bytes 786436
  218.1 2.7 %copy-start.7 = (f32[2,128,384]{2,1,0:T(8,128)S(1)}, f32[2,128,384]{2,1,0:T(8,128)}, u32[]{:S(2)}) copy-start(f32[2,128,384]{2,1,0:T(8,128)} %copy-done.6) | copy-start | bytes 1179652
  218.1 2.7 %copy-start.25 = (f32[2,384,128]{2,1,0:T(8,128)S(1)}, f32[2,384,128]{2,1,0:T(8,128)}, u32[]{:S(2)}) copy-start(f32[2,384,128]{2,1,0:T(8,128)} %param.21) | copy-start | bytes 1179652
Sparse Core Ops, SparseCore 0:
  57.6 14.3 all-gather.3
  107.5 11.3 all-gather.5
  154.6 11.3 all-gather.7
where the time goes:
time: 232 us; the launch traced here: 231 us
  waiting for transfers between devices  123 us (53%)
  local copies, waits for them, and re-layouts  36.6 us (16%)
  matrix products  25.9 us (11%)
  other arithmetic  17.2 us (7%)
  between operations  14 us (6%)
  starting transfers between devices  9.44 us (4%)
  blocking collectives  4.88 us (2%)
    ppermute x4, waiting for transfers between devices, partner(): return lax.ppermute(value, axis, pairs)  89.7 us
    all_gather x3, waiting for transfers between devices, local(): partner_tail = lax.all_gather(partner_half, 'panel', axis=1, tiled=True)  33.3 us
    add x4, other arithmetic, local(): packet = jnp.concatenate([packet[:bit], tail_rows + partner_tail], axis=0)  10.8 us
    unnamed x85, local copies, waits for them, and re-layouts  9.62 us
    dot_general x7, matrix products, eliminate(): jnp.einsum('nij,nic->njc', basis, block_in, precision=highest_precision)  9.31 us
    ppermute x4, starting transfers between devices, partner(): return lax.ppermute(value, axis, pairs)  9.17 us
    reshape x4, local copies, waits for them, and re-layouts, local(): partner_half = incoming[node_len:].reshape(tail_rows.shape[0], half_width)  5.26 us
    slice x3, local copies, waits for them, and re-layouts, local(): tail_rows = packet[bit:]  4.86 us
  transfers between devices with their start and end apart: 7, of which 7 were waited for; matrix products, arithmetic and copies ran while one was open for 2% of the time, Pallas kernels for 0%

commit v1 on v0

v1 whole, which is shorter than its diff:
```python
import functools

import jax
import jax.numpy as jnp
from jax import lax
from jax.experimental import pallas as pl
from jax.experimental.pallas import tpu as pltpu
from jax.sharding import PartitionSpec as P

F32 = jnp.float32
VMEM = pl.BlockSpec(memory_space=pltpu.VMEM)
ANY = pl.BlockSpec(memory_space=pl.ANY)
NN = (((1,), (0,)), ((), ()))
NT = (((1,), (1,)), ((), ()))


def split(value):
    high = value.astype(jnp.bfloat16)
    return high, (value - high.astype(F32)).astype(jnp.bfloat16)


def product(left, right, dims):
    left_high, left_low = left if isinstance(left, tuple) else split(left)
    right_high, right_low = right if isinstance(right, tuple) else split(right)
    dot = functools.partial(lax.dot_general, dimension_numbers=dims, preferred_element_type=F32)
    return dot(left_high, right_high) + (dot(left_high, right_low) + dot(left_low, right_high))


def mm(left, right):
    return product(left, right, NN)


def mt(left, right):
    return product(left, right, NT)


def call(kernel, out_shapes, *operands, any_inputs=False, scratch=(), flops=0):
    outs = [jax.ShapeDtypeStruct(shape, F32) for shape in out_shapes]
    size = sum(4 * o.size for o in operands) + sum(4 * o.size for o in outs)
    return pl.pallas_call(
        kernel,
        out_shape=outs,
        in_specs=[ANY if any_inputs else VMEM] * len(operands),
        out_specs=[VMEM] * len(outs),
        scratch_shapes=list(scratch),
        compiler_params=pltpu.CompilerParams(vmem_limit_bytes=40 * 2**20),
        cost_estimate=pl.CostEstimate(flops=flops, bytes_accessed=size, transcendentals=0),
    )(*operands)


def fetch(sources, targets, sems):
    copies = [
        pltpu.make_async_copy(s, t, sems.at[i]) for i, (s, t) in enumerate(zip(sources, targets))
    ]
    for copy in copies:
        copy.start()
    return copies


def up_rows(basis, inverse_factor, coupling_block, block_rows):
    e = inverse_factor.shape[0]
    c = mm(block_rows, basis)
    y = mt(c[:, :e], inverse_factor)
    return y, c[:, e:] - mt(y, coupling_block)


def node_kernel(q_ref, e_ref, f_ref, g_ref, low_ref, high_ref):
    rank = e_ref.shape[1]
    q = q_ref[0]
    q1, q2 = split(q[:, :rank]), q[:, rank:]
    inverse = split(e_ref[0])
    fe = mm(f_ref[0], inverse)
    s = q2.T - mt(fe, q1)
    v = mm(q1, inverse)
    a = mt(v, q1)
    t = q2 - mm(q1, g_ref[0])
    for half, ref in enumerate((low_ref, high_ref)):
        rows = slice(half * rank, (half + 1) * rank)
        ref[0] = s[:, :rank]
        ref[1] = s[:, rank:]
        ref[2] = a[rows, :rank]
        ref[3] = a[rows, rank:]
        ref[4] = t[rows]
    first = lax.axis_index("leaf") == 0

    @pl.when(first)
    def _():
        low_ref[4] = e_ref[0]


def top_kernel(low_ref, high_ref, apex_ref, out_low_ref, out_high_ref):
    apex = split(apex_ref[4])
    s = [split(low_ref[0]), split(low_ref[1])]
    for ref, out in ((low_ref, out_low_ref), (high_ref, out_high_ref)):
        u = split(mm(ref[4], apex))
        out[0] = ref[2] + mm(u, s[0])
        out[1] = ref[3] + mm(u, s[1])


def leaf_kernel(
    rhs, q, e, f, mid_q, mid_e, mid_f, y_ref, mid_y_ref, z_ref,
    rhs_v, q_v, e_v, f_v, mid_q_v, mid_e_v, mid_f_v, sems,
):
    leaves = q.shape[0]
    size = q.shape[1]
    sources, targets = [], []
    for n in range(leaves):
        rows = pl.ds(n * size, size)
        sources += [rhs.at[rows], q.at[n], e.at[n], f.at[n]]
        targets += [rhs_v.at[rows], q_v.at[n], e_v.at[n], f_v.at[n]]
    sources += [mid_q, mid_e, mid_f]
    targets += [mid_q_v, mid_e_v, mid_f_v]
    copies = fetch(sources, targets, sems)
    reduced = []
    for n in range(leaves):
        copies[4 * n].wait()
        copies[4 * n + 1].wait()
        block = rhs_v[n * size : (n + 1) * size, :].T
        c = mm(block, q_v[n])
        copies[4 * n + 2].wait()
        count = e.shape[1]
        y = mt(c[:, :count], e_v[n])
        copies[4 * n + 3].wait()
        reduced.append(c[:, count:] - mt(y, f_v[n]))
        y_ref[n] = y
    for copy in copies[4 * leaves :]:
        copy.wait()
    y, z = up_rows(mid_q_v[0], mid_e_v[0], mid_f_v[0], jnp.concatenate(reduced, axis=1))
    mid_y_ref[...] = y
    z_ref[...] = z


def pair_kernel(own_ref, other_ref, q_ref, e_ref, f_ref, y_ref, z_ref):
    second = lax.axis_index("panel") == 1
    own, other = own_ref[...], other_ref[...]
    block = jnp.concatenate(
        [jnp.where(second, other, own), jnp.where(second, own, other)], axis=1
    )
    y, z = up_rows(q_ref[0], e_ref[0], f_ref[0], block)
    y_ref[...] = y
    z_ref[...] = z


def level_kernel(bit, own_ref, other_ref, packet_ref, z_ref):
    second = (lax.axis_index("leaf") >> bit) & 1 == 1
    own, other = own_ref[...], other_ref[...]
    first_z = jnp.where(second, other, own)
    second_z = jnp.where(second, own, other)
    z_ref[...] = mt(first_z, packet_ref[0]) + mt(second_z, packet_ref[1])


def own_half(ref, start, rank):
    return ref[0, pl.ds(pl.multiple_of(start * rank, rank), rank), :]


def tail_kernel(
    q, g, y_ref, mid_q_ref, mid_g_ref, mid_y_ref, pair_q_ref, pair_g_ref, pair_y_ref,
    base_ref, w_ref, q_v, g_v, sems,
):
    leaves, size = q.shape[0], q.shape[1]
    rank = pair_g_ref.shape[2]
    count = g.shape[1]
    copies = fetch(
        [a.at[n] for n in range(leaves) for a in (q, g)],
        [a.at[n] for n in range(leaves) for a in (q_v, g_v)],
        sems,
    )
    pair_q = own_half(pair_q_ref, lax.axis_index("panel"), rank)
    pair_t = split(pair_q[:, rank:] - mm(pair_q[:, :rank], pair_g_ref[0]))
    mid_w = mt(pair_y_ref[...], pair_q[:, :rank])
    mid_q = mid_q_ref[0]
    mid_q1 = split(mid_q[:, :rank])
    mid_t = split(mid_q[:, rank:] - mm(mid_q1, mid_g_ref[0]))
    leaf_w = mt(mid_y_ref[...], mid_q1) + mt(mid_w, mid_t)
    map_w = mm(mid_t, pair_t)
    for n in range(leaves):
        copies[2 * n].wait()
        q1 = split(q_v[n, :, :count])
        copies[2 * n + 1].wait()
        leaf_t = split(q_v[n, :, count:] - mm(q1, g_v[n]))
        part = slice(n * rank, (n + 1) * rank)
        rows = slice(n * size, (n + 1) * size)
        base_ref[rows] = mt(q1, y_ref[n]) + mt(leaf_t, leaf_w[:, part])
        w_ref[rows] = mm(leaf_t, map_w[part])


def fold_kernel(levels, base_ref, w_ref, *refs):
    base_out, w_out = refs[-2:]
    offset = None
    chain = None
    for bit in range(levels):
        own_ref, other_ref, packet_ref = refs[3 * bit : 3 * bit + 3]
        second = (lax.axis_index("leaf") >> bit) & 1 == 1
        own, other = own_ref[...], other_ref[...]
        first_z = jnp.where(second, other, own)
        second_z = jnp.where(second, own, other)
        u = mt(first_z, packet_ref[2]) + mt(second_z, packet_ref[3])
        if bit == 0:
            offset, chain = u, packet_ref[4]
        else:
            chain = split(chain)
            offset = offset + mt(u, chain)
            chain = mm(chain, packet_ref[4])
    w = split(w_ref[...])
    base_out[...] = base_ref[...] + mt(w, offset)
    w_out[...] = mm(w, chain)


def apex_kernel(low, levels, *refs):
    out_ref = refs[-1]
    w = None
    for bit in range(levels - 1, low - 1, -1):
        own_ref, other_ref, packet_ref = refs[3 * (bit - low) : 3 * (bit - low) + 3]
        second = (lax.axis_index("leaf") >> bit) & 1 == 1
        own, other = own_ref[...], other_ref[...]
        first_z = jnp.where(second, other, own)
        second_z = jnp.where(second, own, other)
        start = 0 if bit == levels - 1 else 2
        value = mt(first_z, packet_ref[start]) + mt(second_z, packet_ref[start + 1])
        if w is not None:
            value = value + mt(w, packet_ref[4])
        w = value
    out_ref[...] = w


def last_kernel(base_ref, w_ref, incoming_ref, out_ref):
    out_ref[...] = base_ref[...] + mt(w_ref[...], incoming_ref[...])


HOME = (0, 1, 1, 0)


def home_core(level):
    return HOME[(level - 1) % 4]


def packet_rounds(depth, low):
    rounds = []
    holders = {k: {(2 * j + 1) << (k - 1) for j in range(1 << (depth - k))} for k in range(1, depth + 1)}
    for r in range(1, depth + 2):
        moves = []
        for level in range(1, depth + 1):
            if level == depth and r == 1:
                moves.append((level, -1, [(0, 1 << (depth - 1))]))
                continue
            bit = level - r + (1 if level == depth else 0)
            if bit < (0 if level <= low else low):
                continue
            pairs = [(p, p ^ (1 << bit)) for p in sorted(holders[level])]
            holders[level] |= {target for _, target in pairs}
            moves.append((level, bit, pairs))
        if moves:
            rounds.append(moves)
    return rounds


def local(
    rhs, leaf_q, leaf_e, leaf_f, leaf_g, mid_q, mid_e, mid_f, mid_g,
    pair_q, pair_e, pair_f, pair_g, up_q, up_e, up_f, up_g,
):
    count_leaf = lax.axis_size("leaf")
    cores = lax.axis_size("panel")
    depth = count_leaf.bit_length() - 1
    low = min(2, depth - 1)
    position = lax.axis_index("leaf")
    core = lax.axis_index("panel")
    rank, columns = up_e.shape[1], rhs.shape[1]
    leaves, size = leaf_q.shape[0], leaf_q.shape[1]
    count = leaf_e.shape[1]
    tile = (columns, rank)
    dma = pltpu.SemaphoreType.DMA

    def swap_cores(value):
        return lax.ppermute(value, "panel", [(i, cores - 1 - i) for i in range(cores)])

    def exchange(value, bit, step):
        pairs = [(p, p ^ (1 << bit)) for p in range(0, count_leaf, step)]
        return lax.ppermute(value, "leaf", pairs)

    packet = (5, rank, rank)
    low_half, high_half = call(node_kernel, [packet, packet], up_q, up_e, up_f, up_g)
    held = {}

    rounds = packet_rounds(depth, low)
    full = {}

    def bit_at(level, bit):
        return position & ((1 << level) - 1) == (1 << bit)

    def start_round(index):
        moves = rounds[index]
        received = {}
        groups = {0: [m for m in moves if home_core(m[0]) == 0], 1: [m for m in moves if home_core(m[0]) == 1]}
        for i in range(max(len(groups[0]), len(groups[1]))):
            ops = [groups[c][i] for c in (0, 1) if i < len(groups[c])]
            pairs = []
            for level, _, list_of in ops:
                c = home_core(level)
                pairs += [(p * cores + c, t * cores + c) for p, t in list_of]
            if index == 0:
                operand = low_half
            else:
                values = [held[level] if bit != depth - 1 else top_low for level, bit, _ in ops]
                if len(values) == 2:
                    a, b = values
                    n = max(a.shape[0], b.shape[0])
                    a = jnp.pad(a, ((0, n - a.shape[0]), (0, 0), (0, 0)))
                    b = jnp.pad(b, ((0, n - b.shape[0]), (0, 0), (0, 0)))
                    operand = jnp.where(core == home_core(ops[0][0]), a, b)
                else:
                    operand = values[0]
            incoming = lax.ppermute(operand, ("leaf", "panel"), pairs)
            for level, _, _ in ops:
                received[level] = incoming
        return received

    def finish_round(index, received):
        nonlocal top_low
        moves = rounds[index]
        finished = []
        for level, bit, _ in moves:
            value = received[level]
            if level == depth:
                if bit < 0:
                    top_low, held[level] = call(
                        top_kernel, [(2, rank, rank)] * 2, low_half, high_half, value
                    )
                else:
                    held[level] = jnp.where(bit_at(bit + 1, bit), held[level], value[:2]) if bit == depth - 1 else jnp.where(bit_at(bit + 1, bit), value[:2], held[level])
            elif index == 0:
                owner = bit_at(level, level - 1)
                held[level] = jnp.where(owner, high_half, value)
            else:
                held[level] = jnp.where(bit_at(bit + 1, bit), value, held[level])
            if bit == (0 if level <= low else low):
                finished.append(level)
        for c0 in range(0, len(finished), 1):
            level = finished[c0]
            if level in full:
                continue
            mate = next((o for o in finished if o not in full and home_core(o) != home_core(level) and held[o].shape == held[level].shape), None)
            mine = core == home_core(level)
            if mate is None:
                other = swap_cores(held[level])
                full[level] = jnp.where(mine, held[level], other)
            else:
                other = swap_cores(jnp.where(mine, held[level], held[mate]))
                full[level] = jnp.where(mine, held[level], other)
                full[mate] = jnp.where(mine, other, held[mate])

    top_low = None
    flying = start_round(0)

    y, mid_y, z = call(
        leaf_kernel,
        [(leaves, columns, count), tile, tile],
        rhs, leaf_q, leaf_e, leaf_f, mid_q, mid_e, mid_f,
        any_inputs=True,
        scratch=[
            pltpu.VMEM(a.shape, F32) for a in (rhs, leaf_q, leaf_e, leaf_f, mid_q, mid_e, mid_f)
        ] + [dma((4 * leaves + 3,))],
    )
    other = swap_cores(z)
    pair_y, z = call(pair_kernel, [tile, tile], z, other, pair_q, pair_e, pair_f)

    exchanged = []
    base = weight = None
    for bit in range(depth):
        other = exchange(z, bit, 1 if bit < low else 1 << low)
        exchanged += [z, other]
        if bit < len(rounds):
            finish_round(bit, flying)
            if bit + 1 < len(rounds):
                flying = start_round(bit + 1)
        if bit == 0:
            base, weight = call_tail(
                leaf_q, leaf_g, y, mid_q, mid_g, mid_y, pair_q, pair_g, pair_y, rhs.shape
            )
        if bit < depth - 1:
            (z,) = call(functools.partial(level_kernel, bit), [tile], z, other, full[bit + 1])
    for index in range(depth, len(rounds)):
        finish_round(index, flying)
        if index + 1 < len(rounds):
            flying = start_round(index + 1)

    folded = []
    for bit in range(low):
        folded += [exchanged[2 * bit], exchanged[2 * bit + 1], full[bit + 1]]
    base, weight = call(
        functools.partial(fold_kernel, low), [base.shape, weight.shape], base, weight, *folded
    )

    above = []
    for bit in range(low, depth):
        above += [exchanged[2 * bit], exchanged[2 * bit + 1], full[bit + 1]]
    (w,) = call(functools.partial(apex_kernel, low, depth), [tile], *above)
    incoming = w
    for mask in range(1, 1 << low):
        pairs = [(p, p + mask) for p in range(0, count_leaf, 1 << low)]
        copy = lax.ppermute(w, "leaf", pairs)
        incoming = jnp.where(position & ((1 << low) - 1) == mask, copy, incoming)
    (result,) = call(last_kernel, [rhs.shape], base, weight, incoming)
    return result


def call_tail(leaf_q, leaf_g, y, mid_q, mid_g, mid_y, pair_q, pair_g, pair_y, shape):
    leaves = leaf_q.shape[0]
    rank = pair_g.shape[2]
    operands = (leaf_q, leaf_g, y, mid_q, mid_g, mid_y, pair_q, pair_g, pair_y)
    outs = [jax.ShapeDtypeStruct(shape, F32), jax.ShapeDtypeStruct((shape[0], rank), F32)]
    size = sum(4 * a.size for a in operands + tuple(outs))
    return pl.pallas_call(
        tail_kernel,
        out_shape=outs,
        in_specs=[ANY, ANY] + [VMEM] * 7,
        out_specs=[VMEM, VMEM],
        scratch_shapes=[
            pltpu.VMEM(leaf_q.shape, F32),
            pltpu.VMEM(leaf_g.shape, F32),
            pltpu.SemaphoreType.DMA((2 * leaves,)),
        ],
        compiler_params=pltpu.CompilerParams(vmem_limit_bytes=40 * 2**20),
        cost_estimate=pl.CostEstimate(
            flops=8 * leaf_q.size * rank, bytes_accessed=size, transcendentals=0
        ),
    )(*operands)


def solution(mesh):
    both, chip = ("leaf", "panel"), "leaf"
    in_specs = (P(both, None),) + (P(both, None, None),) * 8 + (P(chip, None, None),) * 8
    return jax.shard_map(
        local, mesh=mesh, in_specs=in_specs, out_specs=P(both, None), check_vma=False
    )
```

time: 232 us -> 82.2 us (0.35)
  waiting for transfers between devices: 123 us -> 20.4 us
  matrix products: 25.9 us -> 0 us
  local copies, waits for them, and re-layouts: 36.6 us -> 16.8 us
  Pallas kernels: 0 us -> 14.5 us
  between operations: 14 us -> 0.4 us
  starting transfers between devices: 9.44 us -> 22.4 us
  other arithmetic: 17.2 us -> 6.51 us
  blocking collectives: 4.88 us -> 0 us
    ppermute x4 -> x15, waiting for transfers between devices: 89.7 us -> 20.4 us  [the longest x4 13.3 us: exchange(): return lax.ppermute(value, 'leaf', pairs)]
    all_gather x3 -> x0, waiting for transfers between devices: 33.3 us -> none  [local(): partner_tail = lax.all_gather(partner_half, 'panel', axis=1, tiled=True)]
    dot_general x36 -> x0, matrix products: 25.9 us -> none  [the longest x7 9.31 us: eliminate(): jnp.einsum('nij,nic->njc', basis, block_in, precision=highest_precision)]
    pallas_call x0 -> x11, Pallas kernels: none -> 14.5 us  [the longest x10 11 us: call(): pl.pallas_call(kernel, out_shape=outs, in_specs=[ANY if any_inputs else V...]
    ppermute x4 -> x15, starting transfers between devices: 9.17 us -> 22.4 us  [the longest x4 10.5 us: start_round(): incoming = lax.ppermute(operand, ('leaf', 'panel'), pairs)]
    slice x15 -> x0, local copies, waits for them, and re-layouts: 12.5 us -> none  [the longest x3 4.86 us: local(): tail_rows = packet[bit:]]
    add x4 -> x0, other arithmetic: 10.8 us -> none  [local(): packet = jnp.concatenate([packet[:bit], tail_rows + partner_tail], axis=0)]
    reshape x8 -> x0, local copies, waits for them, and re-layouts: 9.65 us -> none  [the longest x4 5.26 us: local(): partner_half = incoming[node_len:].reshape(tail_rows.shape[0], half_width)]
  transfers between devices with their start and end apart: 7 -> 15, of which waited for: 7 -> 6; matrix products, arithmetic and copies ran while one was open for 2% -> 6% of each run, Pallas kernels for 0% -> 15%
where the time goes in v1:
time: 82.2 us; the launch traced here: 81.1 us
  starting transfers between devices  22.4 us (27%)
  waiting for transfers between devices  20.4 us (25%)
  local copies, waits for them, and re-layouts  16.8 us (20%)
  Pallas kernels  14.5 us (18%)
  other arithmetic  6.51 us (8%)
    unnamed x60, local copies, waits for them, and re-layouts  16.8 us
    ppermute x4, waiting for transfers between devices, exchange(): return lax.ppermute(value, 'leaf', pairs)  13.3 us
    pallas_call x10, Pallas kernels, call(): pl.pallas_call(kernel, out_shape=outs, in_specs=[ANY if any_inputs else V...  11 us
    ppermute x4, starting transfers between devices, start_round(): incoming = lax.ppermute(operand, ('leaf', 'panel'), pairs)  10.5 us
    ppermute x4, starting transfers between devices, exchange(): return lax.ppermute(value, 'leaf', pairs)  7.46 us
    ppermute x4, waiting for transfers between devices, start_round(): incoming = lax.ppermute(operand, ('leaf', 'panel'), pairs)  7.15 us
    ppermute x3, starting transfers between devices, local(): copy = lax.ppermute(w, 'leaf', pairs)  3.89 us
    pallas_call x1, Pallas kernels, call_tail(): pl.pallas_call(tail_kernel, out_shape=outs, in_specs=[ANY, ANY] + [VMEM]...  3.52 us
  transfers between devices with their start and end apart: 15, of which 6 were waited for; matrix products, arithmetic and copies ran while one was open for 6% of the time, Pallas kernels for 15%

profile of v1, /device:TPU:0, one launch (start us, length us, event | category | flops | bytes accessed | tf_op | source)
XLA Modules:
  0.0 81.1 jit_solution(5276344736823841527)
XLA Ops:
  0.0 1.1 %copy-done.11 = f32[1,256,256]{2,1,0:T(8,128)S(1)} copy-done((f32[1,256,256]{2,1,0:T(8,128)S(1)}, f32[1,256,256]{2,1,0:T(8,128)}, u32[]{:S(2)}) %copy-start.11) | copy-done | bytes 262168
  1.1 0.8 %copy-done.24 = f32[1,128,128]{2,1,0:T(8,128)S(1)} copy-done((f32[1,128,128]{2,1,0:T(8,128)S(1)}, f32[1,128,128]{2,1,0:T(8,128)}, u32[]{:S(2)}) %copy-start.24) | copy-done | bytes 65560
  1.9 0.8 %copy-done.25 = f32[1,128,128]{2,1,0:T(8,128)S(1)} copy-done((f32[1,128,128]{2,1,0:T(8,128)S(1)}, f32[1,128,128]{2,1,0:T(8,128)}, u32[]{:S(2)}) %copy-start.25) | copy-done | bytes 65560
  2.8 0.8 %copy-done.26 = f32[1,128,128]{2,1,0:T(8,128)S(1)} copy-done((f32[1,128,128]{2,1,0:T(8,128)S(1)}, f32[1,128,128]{2,1,0:T(8,128)}, u32[]{:S(2)}) %copy-start.26) | copy-done | bytes 65560
  3.6 0.6 shard_map.166
  4.2 6.0 %collective-permute-start.3 = (f32[5,128,128]{2,1,0:T(8,128)S(1)}, f32[5,128,128]{2,1,0:T(8,128)S(1)}, u32[]{:S(2)}, u32[]{:S(2)}) collective-permute-start(f32[5,128,128]{2,1,0:T(8,128)S(1)} %get-tuple-element.26.low_ref), channel_id=1, source_target_pairs={{0,16},{9,1},{25,17}} | collective-permute-start | bytes 983048 | tf_op jit(solution)/shard_map/ppermute | solution.py:312
  10.2 1.3 %collective-permute-start.2 = (f32[5,128,128]{2,1,0:T(8,128)S(1)}, f32[5,128,128]{2,1,0:T(8,128)}, u32[]{:S(2)}, u32[]{:S(2)}) collective-permute-start(f32[5,128,128]{2,1,0:T(8,128)S(1)} %get-tuple-element.26.low_ref), channel_id=1, source_target_pairs={{2,0},{6,4},{10,8},{14,12},{18,16},{22,20},{26,24},{30,28},{5,1},{... | collective-permute-start | bytes 983048 | tf_op jit(solution)/shard_map/ppermute | solution.py:312
  11.5 3.2 %collective-permute-done.3.apex_ref = f32[5,128,128]{2,1,0:T(8,128)S(1)} collective-permute-done((f32[5,128,128]{2,1,0:T(8,128)S(1)}, f32[5,128,128]{2,1,0:T(8,128)S(1)}, u32[]{:S(2)}, u32[]{:S(2)}) %collective-permute-start.3) | collective-permute-done | bytes 327712 | tf_op jit(solution)/shard_map/ppermute | solution.py:312
  14.7 0.6 shard_map.168
  15.3 3.9 %collective-permute-done.2 = f32[5,128,128]{2,1,0:T(8,128)} collective-permute-done((f32[5,128,128]{2,1,0:T(8,128)S(1)}, f32[5,128,128]{2,1,0:T(8,128)}, u32[]{:S(2)}, u32[]{:S(2)}) %collective-permute-start.2) | collective-permute-done | bytes 327712 | tf_op jit(solution)/shard_map/ppermute | solution.py:312
  19.2 1.9 %pad_select_fusion = (f32[5,128,128]{2,1,0:T(8,128)}, f32[5,128,128]{2,1,0:T(8,128)}) fusion(f32[2,128,128]{2,1,0:T(8,128)S(1)} %get-tuple-element.27, pred[]{:T(512)S(6)} %eq.29, f32[5,128,128]{2,1,0:T(8,128)S(1)} %get-tuple-element.25.high_ref, f32[5,128,128]{2,1,0:T(8,128)} %collective-permute-done.2, pred[]{:T(512)S(6)} %eq.33, ...), kind=kLoop, calls=%fused_computation | loop fusion | flops 409600 | bytes 1769476 | tf_op jit(solution)/shard_map/jit(_where)/select_n | solution.py:309
  21.1 1.3 %collective-permute-start.6 = (f32[5,128,128]{2,1,0:T(8,128)}, f32[5,128,128]{2,1,0:T(8,128)S(1)}, u32[]{:S(2)}, u32[]{:S(2)}) collective-permute-start(f32[5,128,128]{2,1,0:T(8,128)} %get-tuple-element.34), channel_id=1, source_target_pairs={{16,0},{1,3},{5,7},{9,11},{13,15},{17,19},{21,23},{25,27},{29,31}} | collective-permute-start | bytes 983048 | tf_op jit(solution)/shard_map/ppermute | solution.py:312
  22.6 1.3 %copy-done.1 = f32[2,384,384]{2,1,0:T(8,128)S(1)} copy-done((f32[2,384,384]{2,1,0:T(8,128)S(1)}, f32[2,384,384]{2,1,0:T(8,128)}, u32[]{:S(2)}) %copy-start.1) | copy-done | bytes 1179672
  23.8 1.0 %copy-done.7 = f32[2,128,384]{2,1,0:T(8,128)S(1)} copy-done((f32[2,128,384]{2,1,0:T(8,128)S(1)}, f32[2,128,384]{2,1,0:T(8,128)}, u32[]{:S(2)}) %copy-start.7) | copy-done | bytes 393240
  24.8 4.9 %shard_map.163 = (f32[2,128,384]{2,1,0:T(8,128)S(1)}, f32[128,128]{1,0:T(8,128)S(1)}, f32[128,128]{1,0:T(8,128)}) custom-call(f32[1024,128]{1,0:T(8,128)S(1)} %copy-done.6, f32[2,512,512]{2,1,0:T(8,128)S(1)} %copy-done, f32[2,384,384]{2,1,0:T(8,128)S(1)} %copy-done.1, f32[2,128,384]{2,1,0:T(8,128)S(1)} %copy-done.7, f32[1,256,256]{2,1,0:T(8,128)S(1)} %copy-done.2, ...), custom_call_target="tpu_custom_call" | custom-call | bytes 5111808 | tf_op jit(solution)/shard_map/pallas_call | solution.py:40
  29.7 0.7 copy-done.9
  30.5 0.6 copy-done.20
  31.1 0.5 collective-permute-start
  31.6 0.7 slice_select_fusion
  32.3 1.9 %collective-permute-start.10 = (f32[2,128,128]{2,1,0:T(8,128)}, f32[2,128,128]{2,1,0:T(8,128)}, u32[]{:S(2)}, u32[]{:S(2)}) collective-permute-start(f32[2,128,128]{2,1,0:T(8,128)} %slice_select_fusion), channel_id=1, source_target_pairs={{0,8},{16,24}} | collective-permute-start | bytes 393224 | tf_op jit(solution)/shard_map/ppermute | solution.py:312
  34.2 1.9 %broadcast_select_fusion.5 = (f32[5,128,128]{2,1,0:T(8,128)S(1)}, f32[5,128,128]{2,1,0:T(8,128)S(1)}, f32[5,128,128]{2,1,0:T(8,128)}) fusion(f32[5,128,128]{2,1,0:T(8,128)} %collective-permute-done.4, pred[]{:T(512)S(6)} %eq.29, f32[5,128,128]{2,1,0:T(8,128)S(1)} %get-tuple-element.25.high_ref, f32[5,128,128]{2,1,0:T(8,128)S(1)} %collective-permute-done.3.apex_ref, ...), kind=kLoop, calls=%fused_computation.6 | loop fusion | flops 491520 | bytes 2621444 | tf_op jit(solution)/shard_map/jit(_where)/select_n | solution.py:349
  36.1 0.9 %copy-done.4 = f32[1,256,256]{2,1,0:T(8,128)S(1)} copy-done((f32[1,256,256]{2,1,0:T(8,128)S(1)}, f32[1,256,256]{2,1,0:T(8,128)}, u32[]{:S(2)}) %copy-start.4) | copy-done | bytes 262168
  37.1 0.8 %copy-done.27 = f32[1,128,128]{2,1,0:T(8,128)S(1)} copy-done((f32[1,128,128]{2,1,0:T(8,128)S(1)}, f32[1,128,128]{2,1,0:T(8,128)}, u32[]{:S(2)}) %copy-start.27) | copy-done | bytes 65560
  37.9 0.8 %copy-done.28 = f32[1,128,128]{2,1,0:T(8,128)S(1)} copy-done((f32[1,128,128]{2,1,0:T(8,128)S(1)}, f32[1,128,128]{2,1,0:T(8,128)}, u32[]{:S(2)}) %copy-start.28) | copy-done | bytes 65560
  38.8 1.4 %shard_map.164 = (f32[128,128]{1,0:T(8,128)S(1)}, f32[128,128]{1,0:T(8,128)S(1)}) custom-call(f32[128,128]{1,0:T(8,128)} %get-tuple-element.20.own_ref, f32[128,128]{1,0:T(8,128)} %collective-permute-done.other_ref, f32[1,256,256]{2,1,0:T(8,128)S(1)} %copy-done.4, f32[1,128,128]{2,1,0:T(8,128)S(1)} %copy-done.27, f32[1,128,128]{2,1,0:T(8,128)S(1)} %copy-done.28), custom_call_target="tpu_custom_call" | custom-call | bytes 655360 | tf_op jit(solution)/shard_map/pallas_call | solution.py:40
  40.2 0.6 copy-done.22
  40.9 4.5 %collective-permute-done.1.other_ref.refs_1_ = f32[128,128]{1,0:T(8,128)S(1)} collective-permute-done((f32[128,128]{1,0:T(8,128)S(1)}, f32[128,128]{1,0:T(8,128)S(1)}, u32[]{:S(2)}, u32[]{:S(2)}) %collective-permute-start.1) | collective-permute-done | bytes 65568 | tf_op jit(solution)/shard_map/ppermute | solution.py:278
  45.7 0.9 %broadcast_select_fusion.8 = f32[2,128,128]{2,1,0:T(8,128)S(1)} fusion(f32[2,128,128]{2,1,0:T(8,128)} %collective-permute-done.10, f32[2,128,128]{2,1,0:T(8,128)} %slice_select_fusion, pred[]{:T(512)S(6)} %eq.31), kind=kLoop, calls=%fused_computation.11 | loop fusion | flops 32768 | bytes 393217 | tf_op jit(solution)/shard_map/jit(_where)/select_n | solution.py:329
  46.7 1.0 %broadcast_select_fusion.1.refs_5_.packet_ref = f32[5,128,128]{2,1,0:T(8,128)S(1)} fusion(f32[5,128,128]{2,1,0:T(8,128)} %get-tuple-element.33, f32[5,128,128]{2,1,0:T(8,128)} %collective-permute-done.7, pred[]{:T(512)S(6)} %eq.32), kind=kLoop, calls=%fused_computation.2 | loop fusion | flops 81920 | bytes 983041 | tf_op jit(solution)/shard_map/jit(_where)/select_n | solution.py:345
  47.8 2.2 %collective-permute-done.5.refs_4_.other_ref = f32[128,128]{1,0:T(8,128)S(1)} collective-permute-done((f32[128,128]{1,0:T(8,128)S(1)}, f32[128,128]{1,0:T(8,128)S(1)}, u32[]{:S(2)}, u32[]{:S(2)}) %collective-permute-start.5) | collective-permute-done | bytes 65568 | tf_op jit(solution)/shard_map/ppermute | solution.py:278
  50.2 1.9 %collective-permute-start.8 = (f32[128,128]{1,0:T(8,128)S(1)}, f32[128,128]{1,0:T(8,128)S(1)}, u32[]{:S(2)}, u32[]{:S(2)}) collective-permute-start(f32[128,128]{1,0:T(8,128)S(1)} %shard_map.170.own_ref.refs_0_), channel_id=1, source_target_pairs={{0,8},{8,0},{16,24},{24,16},{1,9},{9,1},{17,25},{25,17}} | collective-permute-start | bytes 196616 | tf_op jit(solution)/shard_map/ppermute | solution.py:278
  52.1 4.2 %collective-permute-done.8.other_ref.refs_1_ = f32[128,128]{1,0:T(8,128)S(1)} collective-permute-done((f32[128,128]{1,0:T(8,128)S(1)}, f32[128,128]{1,0:T(8,128)S(1)}, u32[]{:S(2)}, u32[]{:S(2)}) %collective-permute-start.8) | collective-permute-done | bytes 65568 | tf_op jit(solution)/shard_map/ppermute | solution.py:278
  56.6 5.5 %collective-permute-start.9 = (f32[128,128]{1,0:T(8,128)S(1)}, f32[128,128]{1,0:T(8,128)S(1)}, u32[]{:S(2)}, u32[]{:S(2)}) collective-permute-start(f32[128,128]{1,0:T(8,128)S(1)} %shard_map.171.refs_3_), channel_id=1, source_target_pairs={{0,16},{8,24},{16,0},{24,8},{1,17},{9,25},{17,1},{25,9}} | collective-permute-start | bytes 196616 | tf_op jit(solution)/shard_map/ppermute | solution.py:278
  62.2 2.3 %collective-permute-done.9.refs_4_ = f32[128,128]{1,0:T(8,128)S(1)} collective-permute-done((f32[128,128]{1,0:T(8,128)S(1)}, f32[128,128]{1,0:T(8,128)S(1)}, u32[]{:S(2)}, u32[]{:S(2)}) %collective-permute-start.9) | collective-permute-done | bytes 65568 | tf_op jit(solution)/shard_map/ppermute | solution.py:278
  64.5 0.5 shard_map.172
  65.0 1.3 %collective-permute-start.12 = (f32[128,128]{1,0:T(8,128)S(1)}, f32[128,128]{1,0:T(8,128)S(1)}, u32[]{:S(2)}, u32[]{:S(2)}) collective-permute-start(f32[128,128]{1,0:T(8,128)S(1)} %shard_map.172), channel_id=1, source_target_pairs={{0,6},{8,14},{16,22},{24,30},{1,7},{9,15},{17,23},{25,31}} | collective-permute-start | bytes 196616 | tf_op jit(solution)/shard_map/ppermute | solution.py:400
  66.3 1.3 %collective-permute-start.13 = (f32[128,128]{1,0:T(8,128)S(1)}, f32[128,128]{1,0:T(8,128)S(1)}, u32[]{:S(2)}, u32[]{:S(2)}) collective-permute-start(f32[128,128]{1,0:T(8,128)S(1)} %shard_map.172), channel_id=1, source_target_pairs={{0,4},{8,12},{16,20},{24,28},{1,5},{9,13},{17,21},{25,29}} | collective-permute-start | bytes 196616 | tf_op jit(solution)/shard_map/ppermute | solution.py:400
  67.6 1.3 %collective-permute-start.14 = (f32[128,128]{1,0:T(8,128)S(1)}, f32[128,128]{1,0:T(8,128)S(1)}, u32[]{:S(2)}, u32[]{:S(2)}) collective-permute-start(f32[128,128]{1,0:T(8,128)S(1)} %shard_map.172), channel_id=1, source_target_pairs={{0,2},{8,10},{16,18},{24,26},{1,3},{9,11},{17,19},{25,27}} | collective-permute-start | bytes 196616 | tf_op jit(solution)/shard_map/ppermute | solution.py:400
  69.0 0.9 %copy-done.5 = f32[1,256,256]{2,1,0:T(8,128)S(1)} copy-done((f32[1,256,256]{2,1,0:T(8,128)S(1)}, f32[1,256,256]{2,1,0:T(8,128)}, u32[]{:S(2)}) %copy-start.5) | copy-done | bytes 262168
  69.9 1.0 %copy-done.8 = f32[2,384,128]{2,1,0:T(8,128)S(1)} copy-done((f32[2,384,128]{2,1,0:T(8,128)S(1)}, f32[2,384,128]{2,1,0:T(8,128)}, u32[]{:S(2)}) %copy-start.8) | copy-done | bytes 393240
  70.9 1.0 %copy-done.10 = f32[2,128,384]{2,1,0:T(8,128)S(1)} copy-done((f32[2,128,384]{2,1,0:T(8,128)S(1)}, f32[2,128,384]{2,1,0:T(8,128)}, u32[]{:S(2)}) %copy-start.10) | copy-done | bytes 393240
  71.9 0.8 %copy-done.18 = f32[1,128,128]{2,1,0:T(8,128)S(1)} copy-done((f32[1,128,128]{2,1,0:T(8,128)S(1)}, f32[1,128,128]{2,1,0:T(8,128)}, u32[]{:S(2)}) %copy-start.18) | copy-done | bytes 65560
  72.7 0.8 %copy-done.19 = f32[1,128,128]{2,1,0:T(8,128)S(1)} copy-done((f32[1,128,128]{2,1,0:T(8,128)S(1)}, f32[1,128,128]{2,1,0:T(8,128)}, u32[]{:S(2)}) %copy-start.19) | copy-done | bytes 65560
  73.6 0.8 %copy-done.21 = f32[128,128]{1,0:T(8,128)S(1)} copy-done((f32[128,128]{1,0:T(8,128)S(1)}, f32[128,128]{1,0:T(8,128)}, u32[]{:S(2)}) %copy-start.21) | copy-done | bytes 65560
  74.4 0.8 %copy-done.23 = f32[128,128]{1,0:T(8,128)S(1)} copy-done((f32[128,128]{1,0:T(8,128)S(1)}, f32[128,128]{1,0:T(8,128)}, u32[]{:S(2)}) %copy-start.23) | copy-done | bytes 65560
  75.3 3.5 %shard_map.165 = (f32[1024,128]{1,0:T(8,128)S(1)}, f32[1024,128]{1,0:T(8,128)S(1)}) custom-call(f32[2,512,512]{2,1,0:T(8,128)S(1)} %copy-done, f32[2,384,128]{2,1,0:T(8,128)S(1)} %copy-done.8, f32[2,128,384]{2,1,0:T(8,128)S(1)} %copy-done.10, f32[1,256,256]{2,1,0:T(8,128)S(1)} %copy-done.3, f32[1,128,128]{2,1,0:T(8,128)S(1)} %copy-done.18, ...), custom_call_target="tpu_custom_call" | custom-call | flops 536870912 | bytes 4718592 | tf_op jit(solution)/shard_map/pallas_call | solution.py:412
  78.8 1.1 %shard_map.169 = (f32[1024,128]{1,0:T(8,128)S(1)}, f32[1024,128]{1,0:T(8,128)S(1)}) custom-call(f32[1024,128]{1,0:T(8,128)S(1)} %get-tuple-element.22.base_ref, f32[1024,128]{1,0:T(8,128)S(1)} %get-tuple-element.23.w_ref, f32[128,128]{1,0:T(8,128)S(1)} %get-tuple-element.24.own_ref.refs_0_, f32[128,128]{1,0:T(8,128)S(1)} %copy-done.13, ...), custom_call_target="tpu_custom_call" | custom-call | bytes 3014656 | tf_op jit(solution)/shard_map/pallas_call | solution.py:40
  80.0 1.2 %shard_map.173 = f32[1024,128]{1,0:T(8,128)} custom-call(f32[1024,128]{1,0:T(8,128)S(1)} %get-tuple-element.28.base_ref, f32[1024,128]{1,0:T(8,128)S(1)} %get-tuple-element.29.w_ref, f32[128,128]{1,0:T(8,128)S(1)} %select_select_fusion.incoming_ref), custom_call_target="tpu_custom_call" | custom-call | bytes 1638400 | tf_op jit(solution)/shard_map/pallas_call | solution.py:40
  (60 shorter events, 1.1 us)
Async XLA Ops:
  0.0 22.5 %copy-start = (f32[2,512,512]{2,1,0:T(8,128)S(1)}, f32[2,512,512]{2,1,0:T(8,128)}, u32[]{:S(2)}) copy-start(f32[2,512,512]{2,1,0:T(8,128)} %q.3) | copy-start | bytes 6291460
  0.0 22.5 %copy-start.2 = (f32[1,256,256]{2,1,0:T(8,128)S(1)}, f32[1,256,256]{2,1,0:T(8,128)}, u32[]{:S(2)}) copy-start(f32[1,256,256]{2,1,0:T(8,128)} %mid_q_ref.1) | copy-start | bytes 786436
  0.0 1.1 %copy-start.11 = (f32[1,256,256]{2,1,0:T(8,128)S(1)}, f32[1,256,256]{2,1,0:T(8,128)}, u32[]{:S(2)}) copy-start(f32[1,256,256]{2,1,0:T(8,128)} %q_ref.3) | copy-start | bytes 786436
  1.1 0.8 %copy-start.24 = (f32[1,128,128]{2,1,0:T(8,128)S(1)}, f32[1,128,128]{2,1,0:T(8,128)}, u32[]{:S(2)}) copy-start(f32[1,128,128]{2,1,0:T(8,128)} %e_ref.3) | copy-start | bytes 196612
  1.9 0.8 %copy-start.25 = (f32[1,128,128]{2,1,0:T(8,128)S(1)}, f32[1,128,128]{2,1,0:T(8,128)}, u32[]{:S(2)}) copy-start(f32[1,128,128]{2,1,0:T(8,128)} %f_ref.3) | copy-start | bytes 196612
  2.8 0.8 %copy-start.26 = (f32[1,128,128]{2,1,0:T(8,128)S(1)}, f32[1,128,128]{2,1,0:T(8,128)}, u32[]{:S(2)}) copy-start(f32[1,128,128]{2,1,0:T(8,128)} %g_ref.1) | copy-start | bytes 196612
  3.6 18.9 %copy-start.16 = (f32[1,128,128]{2,1,0:T(8,128)S(1)}, f32[1,128,128]{2,1,0:T(8,128)}, u32[]{:S(2)}) copy-start(f32[1,128,128]{2,1,0:T(8,128)} %mid_e.1) | copy-start | bytes 196612
  4.2 10.5 %collective-permute-start.3 = (f32[5,128,128]{2,1,0:T(8,128)S(1)}, f32[5,128,128]{2,1,0:T(8,128)S(1)}, u32[]{:S(2)}, u32[]{:S(2)}) collective-permute-start(f32[5,128,128]{2,1,0:T(8,128)S(1)} %get-tuple-element.26.low_ref), channel_id=1, source_target_pairs={{0,16},{9,1},{25,17}} | collective-permute-start | bytes 983048 | tf_op jit(solution)/shard_map/ppermute | solution.py:312
  10.2 9.1 %collective-permute-start.2 = (f32[5,128,128]{2,1,0:T(8,128)S(1)}, f32[5,128,128]{2,1,0:T(8,128)}, u32[]{:S(2)}, u32[]{:S(2)}) collective-permute-start(f32[5,128,128]{2,1,0:T(8,128)S(1)} %get-tuple-element.26.low_ref), channel_id=1, source_target_pairs={{2,0},{6,4},{10,8},{14,12},{18,16},{22,20},{26,24},{30,28},{5,1},{... | collective-permute-start | bytes 983048 | tf_op jit(solution)/shard_map/ppermute | solution.py:312
  11.5 11.1 %copy-start.6 = (f32[1024,128]{1,0:T(8,128)S(1)}, f32[1024,128]{1,0:T(8,128)}, u32[]{:S(2)}) copy-start(f32[1024,128]{1,0:T(8,128)} %rhs.1) | copy-start | bytes 1572868
  11.5 11.1 %copy-start.17 = (f32[1,128,128]{2,1,0:T(8,128)S(1)}, f32[1,128,128]{2,1,0:T(8,128)}, u32[]{:S(2)}) copy-start(f32[1,128,128]{2,1,0:T(8,128)} %mid_f.1) | copy-start | bytes 196612
  21.1 10.4 %collective-permute-start.6 = (f32[5,128,128]{2,1,0:T(8,128)}, f32[5,128,128]{2,1,0:T(8,128)S(1)}, u32[]{:S(2)}, u32[]{:S(2)}) collective-permute-start(f32[5,128,128]{2,1,0:T(8,128)} %get-tuple-element.34), channel_id=1, source_target_pairs={{16,0},{1,3},{5,7},{9,11},{13,15},{17,19},{21,23},{25,27},{29,31}} | collective-permute-start | bytes 983048 | tf_op jit(solution)/shard_map/ppermute | solution.py:312
  22.4 11.8 %collective-permute-start.4 = (f32[5,128,128]{2,1,0:T(8,128)}, f32[5,128,128]{2,1,0:T(8,128)}, u32[]{:S(2)}, u32[]{:S(2)}) collective-permute-start(f32[5,128,128]{2,1,0:T(8,128)} %get-tuple-element.35), channel_id=1, source_target_pairs={{0,1},{1,0},{2,3},{3,2},{4,5},{5,4},{6,7},{7,6},{8,9},{9,8},{10,11... | collective-permute-start | bytes 983048 | tf_op jit(solution)/shard_map/ppermute | solution.py:274
  22.5 1.3 %copy-start.1 = (f32[2,384,384]{2,1,0:T(8,128)S(1)}, f32[2,384,384]{2,1,0:T(8,128)}, u32[]{:S(2)}) copy-start(f32[2,384,384]{2,1,0:T(8,128)} %e.1) | copy-start | bytes 3538948
  23.8 1.0 %copy-start.7 = (f32[2,128,384]{2,1,0:T(8,128)S(1)}, f32[2,128,384]{2,1,0:T(8,128)}, u32[]{:S(2)}) copy-start(f32[2,128,384]{2,1,0:T(8,128)} %f.1) | copy-start | bytes 1179652
  29.7 0.7 copy-start.9
  30.5 0.6 copy-start.20
  31.1 5.0 %collective-permute-start = (f32[128,128]{1,0:T(8,128)}, f32[128,128]{1,0:T(8,128)}, u32[]{:S(2)}, u32[]{:S(2)}) collective-permute-start(f32[128,128]{1,0:T(8,128)} %get-tuple-element.20.own_ref), channel_id=1, source_target_pairs={{0,1},{1,0},{2,3},{3,2},{4,5},{5,4},{6,7},{7,6},{8,9},{9,8},{10,11... | collective-permute-start | bytes 196616 | tf_op jit(solution)/shard_map/ppermute | solution.py:274
  31.6 2.7 %copy-start.29 = (f32[5,128,128]{2,1,0:T(8,128)}, f32[5,128,128]{2,1,0:T(8,128)S(1)}, u32[]{:S(2)}) copy-start(f32[5,128,128]{2,1,0:T(8,128)S(1)} %collective-permute-done.6) | copy-start | bytes 983044
  32.3 13.4 %collective-permute-start.10 = (f32[2,128,128]{2,1,0:T(8,128)}, f32[2,128,128]{2,1,0:T(8,128)}, u32[]{:S(2)}, u32[]{:S(2)}) collective-permute-start(f32[2,128,128]{2,1,0:T(8,128)} %slice_select_fusion), channel_id=1, source_target_pairs={{0,8},{16,24}} | collective-permute-start | bytes 393224 | tf_op jit(solution)/shard_map/ppermute | solution.py:312
  36.1 10.6 %collective-permute-start.7 = (f32[5,128,128]{2,1,0:T(8,128)}, f32[5,128,128]{2,1,0:T(8,128)}, u32[]{:S(2)}, u32[]{:S(2)}) collective-permute-start(f32[5,128,128]{2,1,0:T(8,128)} %get-tuple-element.33), channel_id=1, source_target_pairs={{0,1},{1,0},{2,3},{3,2},{4,5},{5,4},{6,7},{7,6},{8,9},{9,8},{10,11... | collective-permute-start | bytes 983048 | tf_op jit(solution)/shard_map/ppermute | solution.py:274
  36.1 1.0 %copy-start.4 = (f32[1,256,256]{2,1,0:T(8,128)S(1)}, f32[1,256,256]{2,1,0:T(8,128)}, u32[]{:S(2)}) copy-start(f32[1,256,256]{2,1,0:T(8,128)} %pair_q_ref.1) | copy-start | bytes 786436
  37.1 0.8 %copy-start.27 = (f32[1,128,128]{2,1,0:T(8,128)S(1)}, f32[1,128,128]{2,1,0:T(8,128)}, u32[]{:S(2)}) copy-start(f32[1,128,128]{2,1,0:T(8,128)} %e_ref.2) | copy-start | bytes 196612
  37.9 0.8 %copy-start.28 = (f32[1,128,128]{2,1,0:T(8,128)S(1)}, f32[1,128,128]{2,1,0:T(8,128)}, u32[]{:S(2)}) copy-start(f32[1,128,128]{2,1,0:T(8,128)} %f_ref.2) | copy-start | bytes 196612
  40.2 0.6 copy-start.22
  40.9 28.1 %copy-start.3 = (f32[1,256,256]{2,1,0:T(8,128)S(1)}, f32[1,256,256]{2,1,0:T(8,128)}, u32[]{:S(2)}) copy-start(f32[1,256,256]{2,1,0:T(8,128)} %mid_q_ref.1) | copy-start | bytes 786436
  40.9 4.5 %collective-permute-start.1 = (f32[128,128]{1,0:T(8,128)S(1)}, f32[128,128]{1,0:T(8,128)S(1)}, u32[]{:S(2)}, u32[]{:S(2)}) collective-permute-start(f32[128,128]{1,0:T(8,128)S(1)} %get-tuple-element.24.own_ref.refs_0_), channel_id=1, source_target_pairs={{0,2},{2,0},{4,6},{6,4},{8,10},{10,8},{12,14},{14,12},{16,18},{18,... | collective-permute-start | bytes 196616 | tf_op jit(solution)/shard_map/ppermute | solution.py:278
  45.4 16.8 %copy-start.12 = (f32[128,128]{1,0:T(8,128)}, f32[128,128]{1,0:T(8,128)S(1)}, u32[]{:S(2)}) copy-start(f32[128,128]{1,0:T(8,128)S(1)} %collective-permute-done.1.other_ref.refs_1_) | copy-start | bytes 196612
  45.6 4.3 %collective-permute-start.5 = (f32[128,128]{1,0:T(8,128)S(1)}, f32[128,128]{1,0:T(8,128)S(1)}, u32[]{:S(2)}, u32[]{:S(2)}) collective-permute-start(f32[128,128]{1,0:T(8,128)S(1)} %shard_map.167.refs_3_.own_ref), channel_id=1, source_target_pairs={{0,4},{2,6},{4,0},{6,2},{8,12},{10,14},{12,8},{14,10},{16,20},{18,... | collective-permute-start | bytes 196616 | tf_op jit(solution)/shard_map/ppermute | solution.py:278
  46.7 15.5 %collective-permute-start.11 = (f32[2,128,128]{2,1,0:T(8,128)S(1)}, f32[2,128,128]{2,1,0:T(8,128)S(1)}, u32[]{:S(2)}, u32[]{:S(2)}) collective-permute-start(f32[2,128,128]{2,1,0:T(8,128)S(1)} %broadcast_select_fusion.8), channel_id=1, source_target_pairs={{0,1},{1,0},{2,3},{3,2},{4,5},{5,4},{6,7},{7,6},{8,9},{9,8},{10,11... | collective-permute-start | bytes 393224 | tf_op jit(solution)/shard_map/ppermute | solution.py:274
  50.0 16.4 %copy-start.14 = (f32[128,128]{1,0:T(8,128)}, f32[128,128]{1,0:T(8,128)S(1)}, u32[]{:S(2)}) copy-start(f32[128,128]{1,0:T(8,128)S(1)} %collective-permute-done.5.refs_4_.other_ref) | copy-start | bytes 196612
  50.2 6.2 %collective-permute-start.8 = (f32[128,128]{1,0:T(8,128)S(1)}, f32[128,128]{1,0:T(8,128)S(1)}, u32[]{:S(2)}, u32[]{:S(2)}) collective-permute-start(f32[128,128]{1,0:T(8,128)S(1)} %shard_map.170.own_ref.refs_0_), channel_id=1, source_target_pairs={{0,8},{8,0},{16,24},{24,16},{1,9},{9,1},{17,25},{25,17}} | collective-permute-start | bytes 196616 | tf_op jit(solution)/shard_map/ppermute | solution.py:278
  56.6 7.8 %collective-permute-start.9 = (f32[128,128]{1,0:T(8,128)S(1)}, f32[128,128]{1,0:T(8,128)S(1)}, u32[]{:S(2)}, u32[]{:S(2)}) collective-permute-start(f32[128,128]{1,0:T(8,128)S(1)} %shard_map.171.refs_3_), channel_id=1, source_target_pairs={{0,16},{8,24},{16,0},{24,8},{1,17},{9,25},{17,1},{25,9}} | collective-permute-start | bytes 196616 | tf_op jit(solution)/shard_map/ppermute | solution.py:278
  65.0 14.9 %collective-permute-start.12 = (f32[128,128]{1,0:T(8,128)S(1)}, f32[128,128]{1,0:T(8,128)S(1)}, u32[]{:S(2)}, u32[]{:S(2)}) collective-permute-start(f32[128,128]{1,0:T(8,128)S(1)} %shard_map.172), channel_id=1, source_target_pairs={{0,6},{8,14},{16,22},{24,30},{1,7},{9,15},{17,23},{25,31}} | collective-permute-start | bytes 196616 | tf_op jit(solution)/shard_map/ppermute | solution.py:400
  66.3 13.6 %collective-permute-start.13 = (f32[128,128]{1,0:T(8,128)S(1)}, f32[128,128]{1,0:T(8,128)S(1)}, u32[]{:S(2)}, u32[]{:S(2)}) collective-permute-start(f32[128,128]{1,0:T(8,128)S(1)} %shard_map.172), channel_id=1, source_target_pairs={{0,4},{8,12},{16,20},{24,28},{1,5},{9,13},{17,21},{25,29}} | collective-permute-start | bytes 196616 | tf_op jit(solution)/shard_map/ppermute | solution.py:400
  67.6 12.3 %collective-permute-start.14 = (f32[128,128]{1,0:T(8,128)S(1)}, f32[128,128]{1,0:T(8,128)S(1)}, u32[]{:S(2)}, u32[]{:S(2)}) collective-permute-start(f32[128,128]{1,0:T(8,128)S(1)} %shard_map.172), channel_id=1, source_target_pairs={{0,2},{8,10},{16,18},{24,26},{1,3},{9,11},{17,19},{25,27}} | collective-permute-start | bytes 196616 | tf_op jit(solution)/shard_map/ppermute | solution.py:400
  68.9 1.0 %copy-start.5 = (f32[1,256,256]{2,1,0:T(8,128)S(1)}, f32[1,256,256]{2,1,0:T(8,128)}, u32[]{:S(2)}) copy-start(f32[1,256,256]{2,1,0:T(8,128)} %pair_q_ref.1) | copy-start | bytes 786436
  69.9 1.0 %copy-start.8 = (f32[2,384,128]{2,1,0:T(8,128)S(1)}, f32[2,384,128]{2,1,0:T(8,128)}, u32[]{:S(2)}) copy-start(f32[2,384,128]{2,1,0:T(8,128)} %g.1) | copy-start | bytes 1179652
  70.9 1.0 %copy-start.10 = (f32[2,128,384]{2,1,0:T(8,128)S(1)}, f32[2,128,384]{2,1,0:T(8,128)}, u32[]{:S(2)}) copy-start(f32[2,128,384]{2,1,0:T(8,128)} %copy-done.9) | copy-start | bytes 1179652
  71.9 0.8 %copy-start.18 = (f32[1,128,128]{2,1,0:T(8,128)S(1)}, f32[1,128,128]{2,1,0:T(8,128)}, u32[]{:S(2)}) copy-start(f32[1,128,128]{2,1,0:T(8,128)} %mid_g_ref.1) | copy-start | bytes 196612
  72.7 0.8 %copy-start.19 = (f32[1,128,128]{2,1,0:T(8,128)S(1)}, f32[1,128,128]{2,1,0:T(8,128)}, u32[]{:S(2)}) copy-start(f32[1,128,128]{2,1,0:T(8,128)} %pair_g_ref.1) | copy-start | bytes 196612
  73.6 0.8 %copy-start.21 = (f32[128,128]{1,0:T(8,128)S(1)}, f32[128,128]{1,0:T(8,128)}, u32[]{:S(2)}) copy-start(f32[128,128]{1,0:T(8,128)} %copy-done.20) | copy-start | bytes 196612
  74.4 0.8 %copy-start.23 = (f32[128,128]{1,0:T(8,128)S(1)}, f32[128,128]{1,0:T(8,128)}, u32[]{:S(2)}) copy-start(f32[128,128]{1,0:T(8,128)} %copy-done.22) | copy-start | bytes 196612
  75.3 3.5 %copy-start.13 = (f32[128,128]{1,0:T(8,128)S(1)}, f32[128,128]{1,0:T(8,128)}, u32[]{:S(2)}) copy-start(f32[128,128]{1,0:T(8,128)} %copy-done.12) | copy-start | bytes 196612
  75.3 3.5 %copy-start.15 = (f32[128,128]{1,0:T(8,128)S(1)}, f32[128,128]{1,0:T(8,128)}, u32[]{:S(2)}) copy-start(f32[128,128]{1,0:T(8,128)} %copy-done.14) | copy-start | bytes 196612

commit v2 on v1

v2 whole, which is shorter than its diff:
```python
import functools

import jax
import jax.numpy as jnp
from jax import lax
from jax.experimental import pallas as pl
from jax.experimental.pallas import tpu as pltpu
from jax.sharding import PartitionSpec as P

F32 = jnp.float32
VMEM = pl.BlockSpec(memory_space=pltpu.VMEM)
ANY = pl.BlockSpec(memory_space=pl.ANY)
HBM = pl.BlockSpec(memory_space=pltpu.HBM)
NN = (((1,), (0,)), ((), ()))
NT = (((1,), (1,)), ((), ()))


def split(value):
    high = value.astype(jnp.bfloat16)
    return high, (value - high.astype(F32)).astype(jnp.bfloat16)


def product(left, right, dims):
    left_high, left_low = left if isinstance(left, tuple) else split(left)
    right_high, right_low = right if isinstance(right, tuple) else split(right)
    dot = functools.partial(lax.dot_general, dimension_numbers=dims, preferred_element_type=F32)
    return dot(left_high, right_high) + (dot(left_high, right_low) + dot(left_low, right_high))


def mm(left, right):
    return product(left, right, NN)


def mt(left, right):
    return product(left, right, NT)


STEP = 1 << 25


def call(kernel, outs, *operands, after=(), wait_in=(), alias=None, scratch=(), ahead=0):
    outs = [jax.ShapeDtypeStruct(shape, F32) for shape in outs]
    out_specs = [VMEM] * len(outs)
    aliases = {}
    wait_in = [pltpu.with_memory_space_constraint(a, pltpu.HBM) for a in wait_in]
    every = [*wait_in, *operands, *after]
    in_specs = [HBM] * len(wait_in) + [VMEM] * len(operands) + [ANY] * len(after)
    used = len(wait_in) + len(operands)
    if alias is not None:
        aliases[len(every)] = len(outs)
        every.append(alias)
        in_specs.append(ANY)
        outs.append(jax.ShapeDtypeStruct(alias.shape, F32))
        out_specs.append(ANY)
    n_in, n_out = len(every), len(outs) - len(aliases)

    def body(*refs):
        kernel(*refs[:used], *refs[n_in : n_in + n_out], *refs[n_in + len(outs) :])

    return pl.pallas_call(
        body,
        out_shape=outs,
        in_specs=in_specs,
        out_specs=out_specs,
        scratch_shapes=list(scratch),
        input_output_aliases=aliases,
        compiler_params=pltpu.CompilerParams(vmem_limit_bytes=20 * 2**20),
        cost_estimate=pl.CostEstimate(flops=0, bytes_accessed=ahead, transcendentals=0),
    )(*every)


def fetch(sources, targets, sems):
    copies = [
        pltpu.make_async_copy(s, t, sems.at[i]) for i, (s, t) in enumerate(zip(sources, targets))
    ]
    for copy in copies:
        copy.start()
    return copies


def up_rows(basis, inverse_factor, coupling_block, block_rows):
    e = inverse_factor.shape[0]
    c = mm(block_rows, basis)
    y = mt(c[:, :e], inverse_factor)
    return y, c[:, e:] - mt(y, coupling_block)


def node_kernel(q_h, e_h, f_h, g_h, low_ref, again_ref, high_ref, q_v, e_v, f_v, g_v, sems):
    rank = e_h.shape[1]
    copies = fetch(
        [f_h.at[0], e_h.at[0], q_h.at[0], g_h.at[0]], [f_v, e_v, q_v, g_v], sems
    )
    copies[0].wait()
    copies[1].wait()
    inverse = split(e_v[...])
    fe = mm(f_v[...], inverse)
    copies[2].wait()
    q = q_v[...]
    q1, q2 = split(q[:, :rank]), q[:, rank:]
    s = q2.T - mt(fe, q1)
    v = mm(q1, inverse)
    a = mt(v, q1)
    copies[3].wait()
    t = q2 - mm(q1, g_v[...])
    for half, ref in enumerate((low_ref, high_ref)):
        rows = slice(half * rank, (half + 1) * rank)
        ref[0] = s[:, :rank]
        ref[1] = s[:, rank:]
        ref[2] = a[rows, :rank]
        ref[3] = a[rows, rank:]
        ref[4] = t[rows]
    again_ref[...] = low_ref[...]

    @pl.when(lax.axis_index("leaf") == 0)
    def _():
        again_ref[4] = e_v[...]


def top_kernel(which, low_ref, high_ref, apex_ref, *out_refs):
    apex = split(apex_ref[4])
    s = [split(low_ref[0]), split(low_ref[1])]
    for half, out in zip(which, out_refs):
        ref = (low_ref, high_ref)[half]
        u = split(mm(ref[4], apex))
        out[0] = ref[2] + mm(u, s[0])
        out[1] = ref[3] + mm(u, s[1])


def choose(shape, choices, after=()):
    def kernel(*refs):
        position, core = lax.axis_index("leaf"), lax.axis_index("panel")
        out = refs[-1]
        for ref, (at_core, condition, _, start, count) in zip(refs, choices):
            here = condition(position)
            if at_core is not None:
                here = here & (core == at_core)

            def fill(ref=ref, start=start, count=count):
                out[0:count] = ref[start : start + count]

            pl.when(here)(fill)

    return call(kernel, [shape], *[c[2] for c in choices], after=after)[0]


def leaf_kernel(
    rhs, q, e, f, g, mid_q, mid_e, mid_f, mid_g, pair_q, pair_e, pair_f, pair_g,
    y_ref, mid_y_ref, z_ref, q_v, g_v, mid_q_v, mid_g_v,
    pair_q_v, pair_e_v, pair_f_v, pair_g_v, rhs_v, e_v, f_v, mid_e_v, mid_f_v, sems, later,
):
    leaves, size = q.shape[0], q.shape[1]
    sources, targets = [], []
    for n in range(leaves):
        rows = pl.ds(n * size, size)
        sources += [rhs.at[rows], q.at[n], e.at[n], f.at[n]]
        targets += [rhs_v.at[rows], q_v.at[n], e_v.at[n], f_v.at[n]]
    sources += [mid_q, mid_e, mid_f]
    targets += [mid_q_v, mid_e_v, mid_f_v]
    copies = fetch(sources, targets, sems)
    ahead = fetch(
        [pair_q, pair_e, pair_f, pair_g, mid_g, g],
        [pair_q_v, pair_e_v, pair_f_v, pair_g_v, mid_g_v, g_v],
        later,
    )
    reduced = []
    count = e.shape[1]
    for n in range(leaves):
        copies[4 * n].wait()
        block = rhs_v[n * size : (n + 1) * size, :].T
        copies[4 * n + 1].wait()
        c = mm(block, q_v[n])
        copies[4 * n + 2].wait()
        y = mt(c[:, :count], e_v[n])
        copies[4 * n + 3].wait()
        reduced.append(c[:, count:] - mt(y, f_v[n]))
        y_ref[n] = y
    for copy in copies[4 * leaves :]:
        copy.wait()
    y, z = up_rows(mid_q_v[0], mid_e_v[0], mid_f_v[0], jnp.concatenate(reduced, axis=1))
    mid_y_ref[...] = y
    z_ref[...] = z
    for copy in ahead:
        copy.wait()


def pair_kernel(own_ref, other_ref, q_ref, e_ref, f_ref, y_ref, z_ref):
    second = lax.axis_index("panel") == 1
    own, other = own_ref[...], other_ref[...]
    block = jnp.concatenate(
        [jnp.where(second, other, own), jnp.where(second, own, other)], axis=1
    )
    y, z = up_rows(q_ref[0], e_ref[0], f_ref[0], block)
    y_ref[...] = y
    z_ref[...] = z


def in_order(bit, own_ref, other_ref):
    second = (lax.axis_index("leaf") >> bit) & 1 == 1
    own, other = own_ref[...], other_ref[...]
    return jnp.where(second, other, own), jnp.where(second, own, other)


def level_kernel(bit, own_ref, other_ref, packet_ref, z_ref):
    first_z, second_z = in_order(bit, own_ref, other_ref)
    z_ref[...] = mt(first_z, packet_ref[0]) + mt(second_z, packet_ref[1])


def leaf_maps_kernel(q_ref, g_ref, y_ref, base_ref, t_ref):
    leaves, size = q_ref.shape[0], q_ref.shape[1]
    count = g_ref.shape[1]
    for n in range(leaves):
        q1 = split(q_ref[n, :, :count])
        rows = slice(n * size, (n + 1) * size)
        t_ref[rows] = q_ref[n, :, count:] - mm(q1, g_ref[n])
        base_ref[rows] = mt(q1, y_ref[n])


def fold_kernel(
    levels, base_ref, t_ref, mid_q_ref, mid_g_ref, mid_y_ref, pair_q_ref, pair_g_ref, pair_y_ref, *refs
):
    base_out, w_out = refs[-2:]
    rank = pair_g_ref.shape[2]
    start = lax.axis_index("panel") * rank
    pair_q = pair_q_ref[0, pl.ds(pl.multiple_of(start, rank), rank), :]
    pair_q1 = split(pair_q[:, :rank])
    pair_t = split(pair_q[:, rank:] - mm(pair_q1, pair_g_ref[0]))
    mid_q = mid_q_ref[0]
    mid_q1 = split(mid_q[:, :rank])
    mid_t = split(mid_q[:, rank:] - mm(mid_q1, mid_g_ref[0]))
    offset = chain = None
    for bit in range(levels):
        packet_ref = refs[3 * bit + 2]
        first_z, second_z = in_order(bit, *refs[3 * bit : 3 * bit + 2])
        u = mt(first_z, packet_ref[2]) + mt(second_z, packet_ref[3])
        if bit == 0:
            offset, chain = u, split(packet_ref[4])
        else:
            offset = offset + mt(u, chain)
            chain = split(mm(chain, packet_ref[4]))
    mid_w = mt(pair_y_ref[...], pair_q1)
    if chain is not None:
        mid_w = mid_w + mt(offset, pair_t)
        pair_t = split(mm(pair_t, chain))
    leaf_w = mt(mid_y_ref[...], mid_q1) + mt(mid_w, mid_t)
    map_w = mm(mid_t, pair_t)
    leaves = map_w.shape[0] // rank
    size = base_ref.shape[0] // leaves
    for n in range(leaves):
        rows = slice(n * size, (n + 1) * size)
        part = slice(n * rank, (n + 1) * rank)
        t = split(t_ref[rows])
        base_out[rows] = base_ref[rows] + mt(t, leaf_w[:, part])
        w_out[rows] = mm(t, map_w[part])


def apex_kernel(low, levels, *refs):
    out_ref = refs[-1]
    w = None
    for bit in range(levels - 1, low - 1, -1):
        packet_ref = refs[3 * (bit - low) + 2]
        first_z, second_z = in_order(bit, *refs[3 * (bit - low) : 3 * (bit - low) + 2])
        start = 0 if bit == levels - 1 else 2
        value = mt(first_z, packet_ref[start]) + mt(second_z, packet_ref[start + 1])
        if w is not None:
            value = value + mt(w, packet_ref[4])
        w = value
    out_ref[...] = w


def last_kernel(base_ref, w_ref, *refs):
    *incoming, out_ref = refs
    place = lax.axis_index("leaf") & (len(incoming) - 1)
    w = incoming[0][...]
    for mask in range(1, len(incoming)):
        w = jnp.where(place == mask, incoming[mask][...], w)
    out_ref[...] = base_ref[...] + mt(w_ref[...], w)


def home_core(level):
    return (0, 1, 1, 0)[(level - 1) % 4]


def lowest(bit):
    return lambda position: position & ((2 << bit) - 1) == 1 << bit


def clear(bits):
    return lambda position: position & ((1 << bits) - 1) == 0


def packet_rounds(depth, low):
    holders = {
        k: {(2 * j + 1) << (k - 1) for j in range(1 << (depth - k))} for k in range(1, depth + 1)
    }
    rounds = []
    for r in range(depth + 1):
        moves = []
        for level in range(1, depth + 1):
            bit = level - 1 - r + (level == depth)
            if bit == depth:
                moves.append((level, bit, [(0, 1 << (depth - 1))]))
            elif bit >= (0 if level <= low else low):
                pairs = [(p, p ^ (1 << bit)) for p in sorted(holders[level])]
                holders[level] |= {target for _, target in pairs}
                moves.append((level, bit, pairs))
        if moves:
            rounds.append(moves)
    return rounds


def local(
    rhs, leaf_q, leaf_e, leaf_f, leaf_g, mid_q, mid_e, mid_f, mid_g,
    pair_q, pair_e, pair_f, pair_g, up_q, up_e, up_f, up_g,
):
    count_leaf = lax.axis_size("leaf")
    cores = lax.axis_size("panel")
    depth = count_leaf.bit_length() - 1
    low = min(2, depth - 1)
    rank, columns = up_e.shape[1], rhs.shape[1]
    leaves, count = leaf_e.shape[0], leaf_e.shape[1]
    tile, packet = (columns, rank), (5, rank, rank)
    dma = pltpu.SemaphoreType.DMA

    def swap_cores(value):
        return lax.ppermute(value, "panel", [(i, cores - 1 - i) for i in range(cores)])

    def exchange(value, bit, step):
        pairs = [(p, p ^ (1 << bit)) for p in range(0, count_leaf, step)]
        return lax.ppermute(value, "leaf", pairs)

    low_half, low_again, high_half = call(
        node_kernel,
        [packet] * 3,
        wait_in=(up_q, up_e, up_f, up_g),
        scratch=[pltpu.VMEM(a.shape[1:], F32) for a in (up_q, up_e, up_f, up_g)] + [dma((4,))],
    )
    rounds = packet_rounds(depth, low)
    places = {k: [(lowest(k - 1), high_half, high_half, 0, 5)] for k in range(1, depth)}
    places[depth] = []
    top = {}

    def groups_of(index):
        lists = [[m for m in rounds[index] if home_core(m[0]) == c] for c in (0, 1)]
        longest = max(len(a) for a in lists)
        return [[a[i] for a in lists if i < len(a)] for i in range(longest)]

    def send(index, group, operand):
        pairs = []
        for level, _, moves in groups_of(index)[group]:
            c = home_core(level)
            pairs += [(p * cores + c, t * cores + c) for p, t in moves]
        return lax.ppermute(operand, ("leaf", "panel"), pairs)

    def blocks(level, index):
        return 2 if level == depth else 3 if level <= low and index > 0 else 5

    def operand_of(index, group):
        moves = groups_of(index)[group]
        choices = []
        for level, bit, _ in moves:
            c, n = home_core(level), blocks(level, index)
            if level == depth and bit == depth - 1:
                choices.append((c, lowest(bit), top["low"], 0, n))
                continue
            for condition, mine, _, start, held in places[level]:
                choices.append((c, condition, mine, start + held - n, n))
        size = max(blocks(level, index) for level, _, _ in moves)
        return choose((size, rank, rank), choices)

    def receive(index, group, incoming, after):
        incoming, _ = lax.optimization_barrier((incoming, after))
        other = swap_cores(incoming)
        for level, bit, _ in groups_of(index)[group]:
            if level == depth and bit == depth:
                top["mine"], top["other"] = incoming, other
                top["low"], top["high"] = call(
                    functools.partial(top_kernel, (0, 1)), [(2, rank, rank)] * 2,
                    low_half, high_half, incoming,
                )
                continue
            n = blocks(level, index)
            if index == 0 or (level == depth and bit == depth - 1):
                condition = clear(bit + 1)
            else:
                condition = lowest(bit)
            places[level].append((condition, incoming, other, 0, n))
        if any(level == depth and bit == depth for level, bit, _ in groups_of(index)[group]):
            places[depth].append((lowest(depth - 1), top["high"], None, 0, 2))

    def settle(level, after=()):
        c = home_core(level)
        choices = []
        size = packet if level < depth else (2, rank, rank)
        for condition, mine, other, start, n in places[level]:
            offset = size[0] - n if level < depth else 0
            if other is mine:
                choices.append((None, condition, mine, start, n, offset))
                continue
            choices.append((c, condition, mine, start, n, offset))
            if other is None:
                (other,) = call(
                    functools.partial(top_kernel, (1,)), [size], low_half, high_half, top["other"]
                )
            choices.append((cores - 1 - c, condition, other, start, n, offset))
        return place_blocks(size, choices, after)

    early = send(0, 0, low_half)

    wait_in = (
        rhs, leaf_q, leaf_e, leaf_f, leaf_g, mid_q, mid_e, mid_f, mid_g, pair_q, pair_e, pair_f, pair_g
    )
    kept = (leaf_q, leaf_g, mid_q, mid_g, pair_q, pair_e, pair_f, pair_g)
    y, mid_y, z, *kept = call(
        leaf_kernel,
        [(leaves, columns, count), tile, tile] + [a.shape for a in kept],
        wait_in=wait_in,
        ahead=STEP,
        scratch=[pltpu.VMEM(a.shape, F32) for a in (rhs, leaf_e, leaf_f, mid_e, mid_f)]
        + [dma((4 * leaves + 3,)), dma((6,))],
    )
    leaf_q, leaf_g, mid_q, mid_g, pair_q, pair_e, pair_f, pair_g = kept
    other = swap_cores(z)
    pair_y, z, low_again = call(
        pair_kernel, [tile, tile], z, other, pair_q, pair_e, pair_f, alias=low_again, ahead=STEP
    )
    flying = [(i, send(0, i, low_again)) for i in range(1, len(groups_of(0)))]

    exchanged, full = [], {}
    base = leaf_t = None

    def next_round(index, gate):
        for group, incoming in flying:
            receive(index, group, incoming, gate)
        flying.clear()
        if index + 1 < len(rounds):
            for group in range(len(groups_of(index + 1))):
                flying.append((group, send(index + 1, group, operand_of(index + 1, group))))

    for bit in range(depth):
        if bit == 0:
            receive(0, 0, early, z)
            full.update({level: settle(level) for level in range(1, low + 1)})
        else:
            next_round(bit - 1, z)
        if bit == 1:
            base, leaf_t = call(
                leaf_maps_kernel, [rhs.shape, (rhs.shape[0], rank)], leaf_q, leaf_g, y,
                after=(z,),
            )
        other = exchange(z, bit, 1 if bit < low else 1 << low)
        exchanged += [z, other]
        if bit < depth - 1:
            if bit >= low:
                full[bit + 1] = settle(bit + 1)
            (z,) = call(
                functools.partial(level_kernel, bit), [tile], z, other, full[bit + 1],
                after=(base,) if bit == 1 else (), ahead=STEP,
            )
    for index in range(depth - 1, len(rounds)):
        next_round(index, z)
    full[depth] = settle(depth)

    folded = []
    for bit in range(low):
        folded += [exchanged[2 * bit], exchanged[2 * bit + 1], settle(bit + 1) if bit else full[1]]
    base, weight = call(
        functools.partial(fold_kernel, low), [base.shape, leaf_t.shape], base, leaf_t,
        mid_q, mid_g, mid_y, pair_q, pair_g, pair_y, *folded,
    )

    above = []
    for bit in range(low, depth):
        above += [exchanged[2 * bit], exchanged[2 * bit + 1], full[bit + 1]]
    (w,) = call(
        functools.partial(apex_kernel, low, depth), [tile], *above, after=(base,), ahead=STEP
    )
    incoming = [w]
    for mask in range(1, 1 << low):
        pairs = [(p, p + mask) for p in range(0, count_leaf, 1 << low)]
        incoming.append(lax.ppermute(w, "leaf", pairs))
    (result,) = call(last_kernel, [rhs.shape], base, weight, *incoming)
    return result


def place_blocks(shape, choices, after):
    def kernel(*refs):
        position, core = lax.axis_index("leaf"), lax.axis_index("panel")
        out = refs[-1]
        for ref, (at_core, condition, _, start, count, offset) in zip(refs, choices):
            here = condition(position)
            if at_core is not None:
                here = here & (core == at_core)

            def fill(ref=ref, start=start, count=count, offset=offset):
                out[offset : offset + count] = ref[start : start + count]

            pl.when(here)(fill)

    return call(kernel, [shape], *[c[2] for c in choices], after=after)[0]


def solution(mesh):
    both, chip = ("leaf", "panel"), "leaf"
    in_specs = (P(both, None),) + (P(both, None, None),) * 8 + (P(chip, None, None),) * 8
    return jax.shard_map(
        local, mesh=mesh, in_specs=in_specs, out_specs=P(both, None), check_vma=False
    )
```

time: 82.2 us -> 54.8 us (0.67)
  local copies, waits for them, and re-layouts: 16.8 us -> 0 us
  other arithmetic: 6.51 us -> 0 us
  starting transfers between devices: 22.4 us -> 19.4 us
    unnamed x60 -> x0, local copies, waits for them, and re-layouts: 16.8 us -> none
    select_n x7 -> x0, other arithmetic: 6.51 us -> none  [the longest x1 1.9 us: start_round(): operand = jnp.where(core == home_core(ops[0][0]), a, b)]
    ppermute x4, starting transfers between devices: 7.46 us -> 5.23 us  [exchange(): return lax.ppermute(value, 'leaf', pairs)]
    ppermute x7, waiting for transfers between devices: 7.16 us -> 5.51 us  [the longest x4 3.63 us: send(): return lax.ppermute(operand, ('leaf', 'panel'), pairs)]
    ppermute x4, waiting for transfers between devices: 13.3 us -> 14.7 us  [exchange(): return lax.ppermute(value, 'leaf', pairs)]
    ppermute x7, starting transfers between devices: 14.4 us -> 13.4 us  [the longest x4 9.53 us: send(): return lax.ppermute(operand, ('leaf', 'panel'), pairs)]
    ppermute x4 -> x5, waiting for transfers between devices: 0.01 us -> 0.91 us  [swap_cores(): lax.ppermute(value, 'panel', [(i, cores - 1 - i) for i in range(cores)])]
    pallas_call x11 -> x19, Pallas kernels: 14.5 us -> 13.8 us  [call(): pl.pallas_call(body, out_shape=outs, in_specs=in_specs, out_specs=out_spe...]
  transfers between devices with their start and end apart: 15 -> 16, of which waited for: 6 -> 9; matrix products, arithmetic and copies ran while one was open for 6% -> 0% of each run, Pallas kernels for 15% -> 18%
where the time goes in v2:
time: 54.8 us; the launch traced here: 54.5 us
  waiting for transfers between devices  21.1 us (39%)
  starting transfers between devices  19.4 us (35%)
  Pallas kernels  13.8 us (25%)
    ppermute x4, waiting for transfers between devices, exchange(): return lax.ppermute(value, 'leaf', pairs)  14.7 us
    pallas_call x19, Pallas kernels, call(): pl.pallas_call(body, out_shape=outs, in_specs=in_specs, out_specs=out_spe...  13.8 us
    ppermute x4, starting transfers between devices, send(): return lax.ppermute(operand, ('leaf', 'panel'), pairs)  9.53 us
    ppermute x4, starting transfers between devices, exchange(): return lax.ppermute(value, 'leaf', pairs)  5.23 us
    ppermute x3, starting transfers between devices, local(): incoming.append(lax.ppermute(w, 'leaf', pairs))  3.89 us
    ppermute x4, waiting for transfers between devices, send(): return lax.ppermute(operand, ('leaf', 'panel'), pairs)  3.63 us
    ppermute x3, waiting for transfers between devices, local(): incoming.append(lax.ppermute(w, 'leaf', pairs))  1.88 us
  transfers between devices with their start and end apart: 16, of which 9 were waited for; matrix products, arithmetic and copies ran while one was open for 0% of the time, Pallas kernels for 18%

profile of v2, /device:TPU:0, one launch (start us, length us, event | category | flops | bytes accessed | tf_op | source)
XLA Modules:
  0.0 54.5 jit_solution(12745952676765615315)
XLA Ops:
  0.0 1.9 %shard_map.164 = (f32[5,128,128]{2,1,0:T(8,128)S(1)}, f32[5,128,128]{2,1,0:T(8,128)S(1)}, f32[5,128,128]{2,1,0:T(8,128)S(1)}) custom-call(f32[1,256,256]{2,1,0:T(8,128)} %refs_0_.3, f32[1,128,128]{2,1,0:T(8,128)} %refs_1_.3, f32[1,128,128]{2,1,0:T(8,128)} %refs_2_.3, f32[1,128,128]{2,1,0:T(8,128)} %refs_3_.3), custom_call_target="tpu_custom_call" | custom-call | tf_op jit(solution)/shard_map/pallas_call | solution.py:60
  1.9 1.3 %collective-permute-start.2 = (f32[5,128,128]{2,1,0:T(8,128)S(1)}, f32[5,128,128]{2,1,0:T(8,128)S(1)}, u32[]{:S(2)}, u32[]{:S(2)}) collective-permute-start(f32[5,128,128]{2,1,0:T(8,128)S(1)} %get-tuple-element.42.refs_0_), channel_id=1, source_target_pairs={{2,0},{6,4},{10,8},{14,12},{18,16},{22,20},{26,24},{30,28},{5,1},{... | collective-permute-start | bytes 983048 | tf_op jit(solution)/shard_map/ppermute | solution.py:352
  3.2 4.7 %shard_map.163 = (f32[2,128,384]{2,1,0:T(8,128)S(1)}, f32[128,128]{1,0:T(8,128)S(1)}, f32[128,128]{1,0:T(8,128)S(1)}, f32[2,512,512]{2,1,0:T(8,128)S(1)}, f32[2,...) custom-call(f32[1024,128]{1,0:T(8,128)} %refs_0_.2, ...), custom_call_target="tpu_custom_call" | custom-call | bytes 33554432 | tf_op jit(solution)/shard_map/pallas_call | solution.py:60
  7.8 0.5 collective-permute-start
  8.4 0.9 %collective-permute-done.refs_1_ = f32[128,128]{1,0:T(8,128)S(1)} collective-permute-done((f32[128,128]{1,0:T(8,128)S(1)}, f32[128,128]{1,0:T(8,128)S(1)}, u32[]{:S(2)}, u32[]{:S(2)}) %collective-permute-start) | collective-permute-done | bytes 65568 | tf_op jit(solution)/shard_map/ppermute | solution.py:325
  9.3 0.6 %shard_map.165 = (f32[128,128]{1,0:T(8,128)S(1)}, f32[128,128]{1,0:T(8,128)S(1)}, f32[5,128,128]{2,1,0:T(8,128)S(1)}) custom-call(f32[128,128]{1,0:T(8,128)S(1)} %get-tuple-element.35.refs_0_, f32[128,128]{1,0:T(8,128)S(1)} %collective-permute-done.refs_1_, f32[1,256,256]{2,1,0:T(8,128)S(1)} %get-tuple-element.36.refs_2_.refs_5_, ...), custom_call_target="tpu_custom_call", output_to_operand_aliasing={{2}: (5, {})} | custom-call | bytes 33554432 | tf_op jit(solution)/shard_map/pallas_call | solution.py:60
  9.8 1.3 %collective-permute-done.2.refs_1_.refs_2_ = f32[5,128,128]{2,1,0:T(8,128)S(1)} collective-permute-done((f32[5,128,128]{2,1,0:T(8,128)S(1)}, f32[5,128,128]{2,1,0:T(8,128)S(1)}, u32[]{:S(2)}, u32[]{:S(2)}) %collective-permute-start.2) | collective-permute-done | bytes 327712 | tf_op jit(solution)/shard_map/ppermute | solution.py:352
  11.2 0.0 collective-permute-start.3
  11.2 5.7 %collective-permute-start.5 = (f32[5,128,128]{2,1,0:T(8,128)S(1)}, f32[5,128,128]{2,1,0:T(8,128)S(1)}, u32[]{:S(2)}, u32[]{:S(2)}) collective-permute-start(f32[5,128,128]{2,1,0:T(8,128)S(1)} %get-tuple-element.51), channel_id=1, source_target_pairs={{0,16},{9,1},{25,17}} | collective-permute-start | bytes 983048 | tf_op jit(solution)/shard_map/ppermute | solution.py:352
  16.8 0.1 collective-permute-start.1
  16.9 0.0 collective-permute-done.3.refs_2_
  17.0 4.2 %collective-permute-done.1.refs_1_.refs_9_ = f32[128,128]{1,0:T(8,128)S(1)} collective-permute-done((f32[128,128]{1,0:T(8,128)S(1)}, f32[128,128]{1,0:T(8,128)S(1)}, u32[]{:S(2)}, u32[]{:S(2)}) %collective-permute-start.1) | collective-permute-done | bytes 65568 | tf_op jit(solution)/shard_map/ppermute | solution.py:329
  21.2 0.2 shard_map.167.refs_3_.refs_0_.refs_11_
  21.4 0.0 collective-permute-done.5.refs_2_.refs_1_
  21.4 0.6 %shard_map.169 = (f32[2,128,128]{2,1,0:T(8,128)S(1)}, f32[2,128,128]{2,1,0:T(8,128)S(1)}) custom-call(f32[5,128,128]{2,1,0:T(8,128)S(1)} %get-tuple-element.42.refs_0_, f32[5,128,128]{2,1,0:T(8,128)S(1)} %get-tuple-element.41.refs_0_.refs_1_, f32[5,128,128]{2,1,0:T(8,128)S(1)} %collective-permute-done.5.refs_2_.refs_1_), custom_call_target="tpu_custom_call" | custom-call | tf_op jit(solution)/shard_map/pallas_call | solution.py:60
  22.0 1.3 %collective-permute-start.6 = (f32[3,128,128]{2,1,0:T(8,128)S(1)}, f32[3,128,128]{2,1,0:T(8,128)S(1)}, u32[]{:S(2)}, u32[]{:S(2)}) collective-permute-start(f32[3,128,128]{2,1,0:T(8,128)S(1)} %shard_map.170), channel_id=1, source_target_pairs={{16,0},{1,3},{5,7},{9,11},{13,15},{17,19},{21,23},{25,27},{29,31}} | collective-permute-start | bytes 589832 | tf_op jit(solution)/shard_map/ppermute | solution.py:352
  23.3 0.1 collective-permute-start.9
  23.4 0.1 collective-permute-start.4
  23.5 1.4 %shard_map.168 = (f32[1024,128]{1,0:T(8,128)S(1)}, f32[1024,128]{1,0:T(8,128)S(1)}) custom-call(f32[2,512,512]{2,1,0:T(8,128)S(1)} %get-tuple-element.32.refs_0_, f32[2,384,128]{2,1,0:T(8,128)S(1)} %get-tuple-element.33.refs_1_, f32[2,128,384]{2,1,0:T(8,128)S(1)} %get-tuple-element.34.refs_2_, f32[128,128]{1,0:T(8,128)S(1)} %shard_map.167.refs_3_.refs_0_.refs_11_), custom_call_target="tpu_custom_call" | custom-call | tf_op jit(solution)/shard_map/pallas_call | solution.py:60
  25.0 3.0 %collective-permute-done.4.refs_1_.refs_12_ = f32[128,128]{1,0:T(8,128)S(1)} collective-permute-done((f32[128,128]{1,0:T(8,128)S(1)}, f32[128,128]{1,0:T(8,128)S(1)}, u32[]{:S(2)}, u32[]{:S(2)}) %collective-permute-start.4) | collective-permute-done | bytes 65568 | tf_op jit(solution)/shard_map/ppermute | solution.py:329
  27.9 0.3 shard_map.172.refs_0_
  28.2 2.3 %collective-permute-done.6.refs_3_.refs_1_.refs_2_ = f32[3,128,128]{2,1,0:T(8,128)S(1)} collective-permute-done((f32[3,128,128]{2,1,0:T(8,128)S(1)}, f32[3,128,128]{2,1,0:T(8,128)S(1)}, u32[]{:S(2)}, u32[]{:S(2)}) %collective-permute-start.6) | collective-permute-done | bytes 196640 | tf_op jit(solution)/shard_map/ppermute | solution.py:352
  30.5 1.3 %collective-permute-start.11 = (f32[2,128,128]{2,1,0:T(8,128)S(1)}, f32[2,128,128]{2,1,0:T(8,128)S(1)}, u32[]{:S(2)}, u32[]{:S(2)}) collective-permute-start(f32[2,128,128]{2,1,0:T(8,128)S(1)} %shard_map.178), channel_id=1, source_target_pairs={{0,8},{16,24}} | collective-permute-start | bytes 393224 | tf_op jit(solution)/shard_map/ppermute | solution.py:352
  31.8 0.1 collective-permute-start.7
  31.9 1.9 %collective-permute-start.8 = (f32[128,128]{1,0:T(8,128)S(1)}, f32[128,128]{1,0:T(8,128)S(1)}, u32[]{:S(2)}, u32[]{:S(2)}) collective-permute-start(f32[128,128]{1,0:T(8,128)S(1)} %shard_map.172.refs_0_), channel_id=1, source_target_pairs={{0,8},{8,0},{16,24},{24,16},{1,9},{9,1},{17,25},{25,17}} | collective-permute-start | bytes 196616 | tf_op jit(solution)/shard_map/ppermute | solution.py:329
  33.8 0.0 collective-permute-done.9.refs_2_
  33.9 4.4 %collective-permute-done.8.refs_1_ = f32[128,128]{1,0:T(8,128)S(1)} collective-permute-done((f32[128,128]{1,0:T(8,128)S(1)}, f32[128,128]{1,0:T(8,128)S(1)}, u32[]{:S(2)}, u32[]{:S(2)}) %collective-permute-start.8) | collective-permute-done | bytes 65568 | tf_op jit(solution)/shard_map/ppermute | solution.py:329
  38.3 0.3 shard_map.176.refs_3_
  38.5 0.0 collective-permute-done.11.refs_4_
  38.6 0.1 collective-permute-start.12
  38.6 3.2 %collective-permute-start.10 = (f32[128,128]{1,0:T(8,128)S(1)}, f32[128,128]{1,0:T(8,128)S(1)}, u32[]{:S(2)}, u32[]{:S(2)}) collective-permute-start(f32[128,128]{1,0:T(8,128)S(1)} %shard_map.176.refs_3_), channel_id=1, source_target_pairs={{0,16},{8,24},{16,0},{24,8},{1,17},{9,25},{17,1},{25,9}} | collective-permute-start | bytes 196616 | tf_op jit(solution)/shard_map/ppermute | solution.py:329
  41.8 0.4 shard_map.177.refs_1_
  42.2 0.0 collective-permute-done.7.refs_4_.refs_3_
  42.2 0.1 shard_map.173.refs_13_
  42.3 1.6 %shard_map.174 = (f32[1024,128]{1,0:T(8,128)S(1)}, f32[1024,128]{1,0:T(8,128)S(1)}) custom-call(f32[1024,128]{1,0:T(8,128)S(1)} %get-tuple-element.44.refs_3_.refs_0_, f32[1024,128]{1,0:T(8,128)S(1)} %get-tuple-element.45.refs_1_, f32[1,256,256]{2,1,0:T(8,128)S(1)} %get-tuple-element.46.refs_2_, f32[1,128,128]{2,1,0:T(8,128)S(1)} %get-tuple-element.47.refs_3_, ...), custom_call_target="tpu_custom_call" | custom-call | tf_op jit(solution)/shard_map/pallas_call | solution.py:60
  43.9 0.0 collective-permute-done.12.refs_5_
  43.9 3.1 %collective-permute-done.10.refs_4_ = f32[128,128]{1,0:T(8,128)S(1)} collective-permute-done((f32[128,128]{1,0:T(8,128)S(1)}, f32[128,128]{1,0:T(8,128)S(1)}, u32[]{:S(2)}, u32[]{:S(2)}) %collective-permute-start.10) | collective-permute-done | bytes 65568 | tf_op jit(solution)/shard_map/ppermute | solution.py:329
  47.0 0.5 shard_map.180.refs_2_
  47.6 1.3 %collective-permute-start.15 = (f32[128,128]{1,0:T(8,128)S(1)}, f32[128,128]{1,0:T(8,128)S(1)}, u32[]{:S(2)}, u32[]{:S(2)}) collective-permute-start(f32[128,128]{1,0:T(8,128)S(1)} %shard_map.180.refs_2_), channel_id=1, source_target_pairs={{0,6},{8,14},{16,22},{24,30},{1,7},{9,15},{17,23},{25,31}} | collective-permute-start | bytes 196616 | tf_op jit(solution)/shard_map/ppermute | solution.py:480
  48.9 1.3 %collective-permute-start.14 = (f32[128,128]{1,0:T(8,128)S(1)}, f32[128,128]{1,0:T(8,128)S(1)}, u32[]{:S(2)}, u32[]{:S(2)}) collective-permute-start(f32[128,128]{1,0:T(8,128)S(1)} %shard_map.180.refs_2_), channel_id=1, source_target_pairs={{0,4},{8,12},{16,20},{24,28},{1,5},{9,13},{17,21},{25,29}} | collective-permute-start | bytes 196616 | tf_op jit(solution)/shard_map/ppermute | solution.py:480
  50.2 1.3 %collective-permute-start.13 = (f32[128,128]{1,0:T(8,128)S(1)}, f32[128,128]{1,0:T(8,128)S(1)}, u32[]{:S(2)}, u32[]{:S(2)}) collective-permute-start(f32[128,128]{1,0:T(8,128)S(1)} %shard_map.180.refs_2_), channel_id=1, source_target_pairs={{0,2},{8,10},{16,18},{24,26},{1,3},{9,11},{17,19},{25,27}} | collective-permute-start | bytes 196616 | tf_op jit(solution)/shard_map/ppermute | solution.py:480
  51.5 0.0 collective-permute-done.15.refs_5_
  51.5 0.6 %collective-permute-done.14.refs_4_ = f32[128,128]{1,0:T(8,128)S(1)} collective-permute-done((f32[128,128]{1,0:T(8,128)S(1)}, f32[128,128]{1,0:T(8,128)S(1)}, u32[]{:S(2)}, u32[]{:S(2)}) %collective-permute-start.14) | collective-permute-done | bytes 65568 | tf_op jit(solution)/shard_map/ppermute | solution.py:480
  52.1 1.3 %collective-permute-done.13.refs_3_ = f32[128,128]{1,0:T(8,128)S(1)} collective-permute-done((f32[128,128]{1,0:T(8,128)S(1)}, f32[128,128]{1,0:T(8,128)S(1)}, u32[]{:S(2)}, u32[]{:S(2)}) %collective-permute-start.13) | collective-permute-done | bytes 65568 | tf_op jit(solution)/shard_map/ppermute | solution.py:480
  53.4 1.2 %shard_map.181 = f32[1024,128]{1,0:T(8,128)} custom-call(f32[1024,128]{1,0:T(8,128)S(1)} %get-tuple-element.55.refs_6_.refs_0_, f32[1024,128]{1,0:T(8,128)S(1)} %get-tuple-element.56.refs_1_, f32[128,128]{1,0:T(8,128)S(1)} %shard_map.180.refs_2_, f32[128,128]{1,0:T(8,128)S(1)} %collective-permute-done.13.refs_3_, ...), custom_call_target="tpu_custom_call" | custom-call | tf_op jit(solution)/shard_map/pallas_call | solution.py:60
  (6 shorter events, 0.2 us)
Async XLA Ops:
  1.9 9.3 %collective-permute-start.2 = (f32[5,128,128]{2,1,0:T(8,128)S(1)}, f32[5,128,128]{2,1,0:T(8,128)S(1)}, u32[]{:S(2)}, u32[]{:S(2)}) collective-permute-start(f32[5,128,128]{2,1,0:T(8,128)S(1)} %get-tuple-element.42.refs_0_), channel_id=1, source_target_pairs={{2,0},{6,4},{10,8},{14,12},{18,16},{22,20},{26,24},{30,28},{5,1},{... | collective-permute-start | bytes 983048 | tf_op jit(solution)/shard_map/ppermute | solution.py:352
  7.8 1.4 %collective-permute-start = (f32[128,128]{1,0:T(8,128)S(1)}, f32[128,128]{1,0:T(8,128)S(1)}, u32[]{:S(2)}, u32[]{:S(2)}) collective-permute-start(f32[128,128]{1,0:T(8,128)S(1)} %get-tuple-element.35.refs_0_), channel_id=1, source_target_pairs={{0,1},{1,0},{2,3},{3,2},{4,5},{5,4},{6,7},{7,6},{8,9},{9,8},{10,11... | collective-permute-start | bytes 196616 | tf_op jit(solution)/shard_map/ppermute | solution.py:325
  11.2 5.7 %collective-permute-start.3 = (f32[5,128,128]{2,1,0:T(8,128)S(1)}, f32[5,128,128]{2,1,0:T(8,128)S(1)}, u32[]{:S(2)}, u32[]{:S(2)}) collective-permute-start(f32[5,128,128]{2,1,0:T(8,128)S(1)} %collective-permute-done.2.refs_1_.refs_2_), channel_id=1, source_target_pairs={{0,1},{1,0},{2,3},{3,2},{4,5},{5,4},{6,7},{7,6},{8,9},{9,8},{10,11... | collective-permute-start | bytes 983048 | tf_op jit(solution)/shard_map/ppermute | solution.py:325
  11.2 10.3 %collective-permute-start.5 = (f32[5,128,128]{2,1,0:T(8,128)S(1)}, f32[5,128,128]{2,1,0:T(8,128)S(1)}, u32[]{:S(2)}, u32[]{:S(2)}) collective-permute-start(f32[5,128,128]{2,1,0:T(8,128)S(1)} %get-tuple-element.51), channel_id=1, source_target_pairs={{0,16},{9,1},{25,17}} | collective-permute-start | bytes 983048 | tf_op jit(solution)/shard_map/ppermute | solution.py:352
  16.8 4.3 %collective-permute-start.1 = (f32[128,128]{1,0:T(8,128)S(1)}, f32[128,128]{1,0:T(8,128)S(1)}, u32[]{:S(2)}, u32[]{:S(2)}) collective-permute-start(f32[128,128]{1,0:T(8,128)S(1)} %get-tuple-element.40.refs_0_.refs_8_), channel_id=1, source_target_pairs={{0,2},{2,0},{4,6},{6,4},{8,10},{10,8},{12,14},{14,12},{16,18},{18,... | collective-permute-start | bytes 196616 | tf_op jit(solution)/shard_map/ppermute | solution.py:329
  22.0 8.5 %collective-permute-start.6 = (f32[3,128,128]{2,1,0:T(8,128)S(1)}, f32[3,128,128]{2,1,0:T(8,128)S(1)}, u32[]{:S(2)}, u32[]{:S(2)}) collective-permute-start(f32[3,128,128]{2,1,0:T(8,128)S(1)} %shard_map.170), channel_id=1, source_target_pairs={{16,0},{1,3},{5,7},{9,11},{13,15},{17,19},{21,23},{25,27},{29,31}} | collective-permute-start | bytes 589832 | tf_op jit(solution)/shard_map/ppermute | solution.py:352
  23.3 10.5 %collective-permute-start.9 = (f32[5,128,128]{2,1,0:T(8,128)S(1)}, f32[5,128,128]{2,1,0:T(8,128)S(1)}, u32[]{:S(2)}, u32[]{:S(2)}) collective-permute-start(f32[5,128,128]{2,1,0:T(8,128)S(1)} %collective-permute-done.5.refs_2_.refs_1_), channel_id=1, source_target_pairs={{0,1},{1,0},{2,3},{3,2},{4,5},{5,4},{6,7},{7,6},{8,9},{9,8},{10,11... | collective-permute-start | bytes 983048 | tf_op jit(solution)/shard_map/ppermute | solution.py:325
  23.4 4.5 %collective-permute-start.4 = (f32[128,128]{1,0:T(8,128)S(1)}, f32[128,128]{1,0:T(8,128)S(1)}, u32[]{:S(2)}, u32[]{:S(2)}) collective-permute-start(f32[128,128]{1,0:T(8,128)S(1)} %shard_map.167.refs_3_.refs_0_.refs_11_), channel_id=1, source_target_pairs={{0,4},{2,6},{4,0},{6,2},{8,12},{10,14},{12,8},{14,10},{16,20},{18,... | collective-permute-start | bytes 196616 | tf_op jit(solution)/shard_map/ppermute | solution.py:329
  30.5 8.0 %collective-permute-start.11 = (f32[2,128,128]{2,1,0:T(8,128)S(1)}, f32[2,128,128]{2,1,0:T(8,128)S(1)}, u32[]{:S(2)}, u32[]{:S(2)}) collective-permute-start(f32[2,128,128]{2,1,0:T(8,128)S(1)} %shard_map.178), channel_id=1, source_target_pairs={{0,8},{16,24}} | collective-permute-start | bytes 393224 | tf_op jit(solution)/shard_map/ppermute | solution.py:352
  31.8 10.4 %collective-permute-start.7 = (f32[3,128,128]{2,1,0:T(8,128)S(1)}, f32[3,128,128]{2,1,0:T(8,128)S(1)}, u32[]{:S(2)}, u32[]{:S(2)}) collective-permute-start(f32[3,128,128]{2,1,0:T(8,128)S(1)} %collective-permute-done.6.refs_3_.refs_1_.refs_2_), channel_id=1, source_target_pairs={{0,1},{1,0},{2,3},{3,2},{4,5},{5,4},{6,7},{7,6},{8,9},{9,8},{10,11... | collective-permute-start | bytes 589832 | tf_op jit(solution)/shard_map/ppermute | solution.py:325
  31.9 6.4 %collective-permute-start.8 = (f32[128,128]{1,0:T(8,128)S(1)}, f32[128,128]{1,0:T(8,128)S(1)}, u32[]{:S(2)}, u32[]{:S(2)}) collective-permute-start(f32[128,128]{1,0:T(8,128)S(1)} %shard_map.172.refs_0_), channel_id=1, source_target_pairs={{0,8},{8,0},{16,24},{24,16},{1,9},{9,1},{17,25},{25,17}} | collective-permute-start | bytes 196616 | tf_op jit(solution)/shard_map/ppermute | solution.py:329
  38.6 5.3 %collective-permute-start.12 = (f32[2,128,128]{2,1,0:T(8,128)S(1)}, f32[2,128,128]{2,1,0:T(8,128)S(1)}, u32[]{:S(2)}, u32[]{:S(2)}) collective-permute-start(f32[2,128,128]{2,1,0:T(8,128)S(1)} %collective-permute-done.11.refs_4_), channel_id=1, source_target_pairs={{0,1},{1,0},{2,3},{3,2},{4,5},{5,4},{6,7},{7,6},{8,9},{9,8},{10,11... | collective-permute-start | bytes 393224 | tf_op jit(solution)/shard_map/ppermute | solution.py:325
  38.6 8.4 %collective-permute-start.10 = (f32[128,128]{1,0:T(8,128)S(1)}, f32[128,128]{1,0:T(8,128)S(1)}, u32[]{:S(2)}, u32[]{:S(2)}) collective-permute-start(f32[128,128]{1,0:T(8,128)S(1)} %shard_map.176.refs_3_), channel_id=1, source_target_pairs={{0,16},{8,24},{16,0},{24,8},{1,17},{9,25},{17,1},{25,9}} | collective-permute-start | bytes 196616 | tf_op jit(solution)/shard_map/ppermute | solution.py:329
  47.6 3.9 %collective-permute-start.15 = (f32[128,128]{1,0:T(8,128)S(1)}, f32[128,128]{1,0:T(8,128)S(1)}, u32[]{:S(2)}, u32[]{:S(2)}) collective-permute-start(f32[128,128]{1,0:T(8,128)S(1)} %shard_map.180.refs_2_), channel_id=1, source_target_pairs={{0,6},{8,14},{16,22},{24,30},{1,7},{9,15},{17,23},{25,31}} | collective-permute-start | bytes 196616 | tf_op jit(solution)/shard_map/ppermute | solution.py:480
  48.9 3.2 %collective-permute-start.14 = (f32[128,128]{1,0:T(8,128)S(1)}, f32[128,128]{1,0:T(8,128)S(1)}, u32[]{:S(2)}, u32[]{:S(2)}) collective-permute-start(f32[128,128]{1,0:T(8,128)S(1)} %shard_map.180.refs_2_), channel_id=1, source_target_pairs={{0,4},{8,12},{16,20},{24,28},{1,5},{9,13},{17,21},{25,29}} | collective-permute-start | bytes 196616 | tf_op jit(solution)/shard_map/ppermute | solution.py:480
  50.2 3.2 %collective-permute-start.13 = (f32[128,128]{1,0:T(8,128)S(1)}, f32[128,128]{1,0:T(8,128)S(1)}, u32[]{:S(2)}, u32[]{:S(2)}) collective-permute-start(f32[128,128]{1,0:T(8,128)S(1)} %shard_map.180.refs_2_), channel_id=1, source_target_pairs={{0,2},{8,10},{16,18},{24,26},{1,3},{9,11},{17,19},{25,27}} | collective-permute-start | bytes 196616 | tf_op jit(solution)/shard_map/ppermute | solution.py:480

commit v3 on v2

v3 whole, which is shorter than its diff:
```python
import functools

import jax
import jax.numpy as jnp
from jax import lax
from jax.experimental import pallas as pl
from jax.experimental.pallas import tpu as pltpu
from jax.sharding import PartitionSpec as P

F32 = jnp.float32
VMEM = pl.BlockSpec(memory_space=pltpu.VMEM)
ANY = pl.BlockSpec(memory_space=pl.ANY)
HBM = pl.BlockSpec(memory_space=pltpu.HBM)
NN = (((1,), (0,)), ((), ()))
NT = (((1,), (1,)), ((), ()))


def split(value):
    high = value.astype(jnp.bfloat16)
    return high, (value - high.astype(F32)).astype(jnp.bfloat16)


def product(left, right, dims):
    left_high, left_low = left if isinstance(left, tuple) else split(left)
    right_high, right_low = right if isinstance(right, tuple) else split(right)
    dot = functools.partial(lax.dot_general, dimension_numbers=dims, preferred_element_type=F32)
    return dot(left_high, right_high) + (dot(left_high, right_low) + dot(left_low, right_high))


def mm(left, right):
    return product(left, right, NN)


def mt(left, right):
    return product(left, right, NT)


def call(kernel, outs, *operands, after=(), wait_in=(), through=(), scratch=(), cost=0):
    wait_in = [pltpu.with_memory_space_constraint(a, pltpu.HBM) for a in wait_in]
    used = len(wait_in) + len(operands)
    every = [*wait_in, *operands, *after, *through]
    out_shape = [jax.ShapeDtypeStruct(shape, F32) for shape in outs]
    out_shape += [jax.ShapeDtypeStruct(a.shape, F32) for a in through]
    n_in, n_out = len(every), len(outs)

    def body(*refs):
        kernel(*refs[:used], *refs[n_in : n_in + n_out], *refs[n_in + len(out_shape) :])

    return pl.pallas_call(
        body,
        out_shape=out_shape,
        in_specs=[HBM] * len(wait_in) + [VMEM] * len(operands) + [ANY] * (n_in - used),
        out_specs=[VMEM] * n_out + [ANY] * len(through),
        scratch_shapes=list(scratch),
        input_output_aliases={n_in - len(through) + i: n_out + i for i in range(len(through))},
        compiler_params=pltpu.CompilerParams(vmem_limit_bytes=20 * 2**20),
        cost_estimate=pl.CostEstimate(flops=cost, bytes_accessed=1000, transcendentals=0) if cost else None,
    )(*every)


def fetch(sources, targets, sems):
    copies = [
        pltpu.make_async_copy(s, t, sems.at[i]) for i, (s, t) in enumerate(zip(sources, targets))
    ]
    for copy in copies:
        copy.start()
    return copies


def up_rows(basis, inverse_factor, coupling_block, block_rows):
    e = inverse_factor.shape[0]
    c = mm(block_rows, basis)
    y = mt(c[:, :e], inverse_factor)
    return y, c[:, e:] - mt(y, coupling_block)


def node_maps(q, inverse, coupling, back, low_ref, high_ref):
    rank = back.shape[0]
    apex = inverse
    inverse = split(inverse)
    q1, q2 = split(q[:, :rank]), q[:, rank:]
    s = q2.T - mt(mm(coupling, inverse), q1)
    a = mt(mm(q1, inverse), q1)
    t = q2 - mm(q1, back)
    for half, ref in enumerate((low_ref, high_ref)):
        rows = slice(half * rank, (half + 1) * rank)
        ref[0] = s[:, :rank]
        ref[1] = s[:, rank:]
        ref[2] = a[rows, :rank]
        ref[3] = a[rows, rank:]
        ref[4] = t[rows]

    @pl.when(lax.axis_index("leaf") == 0)
    def _():
        low_ref[0] = apex


def node_kernel(
    up_q, up_e, up_f, up_g, low_ref, high_ref, up_q_v, up_e_v, up_f_v, up_g_v, sems
):
    for copy in fetch([up_q, up_e, up_f, up_g], [up_q_v, up_e_v, up_f_v, up_g_v], sems):
        copy.wait()
    node_maps(up_q_v[0], up_e_v[0], up_f_v[0], up_g_v[0], low_ref, high_ref)


def top_kernel(low_ref, high_ref, incoming_ref, out_ref):
    first = lax.axis_index("leaf") == 0
    apex = split(jnp.where(first, low_ref[0], incoming_ref[0]))

    def part(block):
        return jnp.where(first, incoming_ref[block], high_ref[block])

    u = split(mm(part(4), apex))
    out_ref[0] = part(2) + mm(u, part(0))
    out_ref[1] = part(3) + mm(u, part(1))


def choose(size, choices, after=()):
    def kernel(*refs):
        position, core = lax.axis_index("leaf"), lax.axis_index("panel")
        out = refs[-1]
        for ref, (at_core, condition, _, start, to, count) in zip(refs, choices):
            here = jnp.bool_(True) if condition is None else condition(position)
            if at_core is not None:
                here = here & (core == at_core)

            def fill(ref=ref, start=start, to=to, count=count):
                out[to : to + count] = ref[start : start + count]

            pl.when(here)(fill)

    shape = (size,) + choices[0][2].shape[1:]
    return call(kernel, [shape], *[c[2] for c in choices], after=after)[0]


def leaf_kernel(
    rhs, q, e, f, g, mid_q, mid_e, mid_f, mid_g, pair_q, pair_e, pair_f, pair_g,
    y_ref, mid_y_ref, z_ref, q_v, g_v, mid_q_v, mid_g_v, pair_q_v, pair_e_v, pair_f_v, pair_g_v,
    rhs_v, e_v, f_v, mid_e_v, mid_f_v, sems, later,
):
    leaves, size = q.shape[0], q.shape[1]
    sources, targets = [], []
    for n in range(leaves):
        rows = pl.ds(n * size, size)
        sources += [rhs.at[rows], q.at[n], e.at[n], f.at[n]]
        targets += [rhs_v.at[rows], q_v.at[n], e_v.at[n], f_v.at[n]]
    sources += [mid_q, mid_e, mid_f]
    targets += [mid_q_v, mid_e_v, mid_f_v]
    copies = fetch(sources, targets, sems)
    ahead = fetch(
        [pair_q, pair_e, pair_f, pair_g, mid_g, g],
        [pair_q_v, pair_e_v, pair_f_v, pair_g_v, mid_g_v, g_v],
        later,
    )
    reduced = []
    count = e.shape[1]
    for n in range(leaves):
        copies[4 * n].wait()
        block = rhs_v[n * size : (n + 1) * size, :].T
        copies[4 * n + 1].wait()
        c = mm(block, q_v[n])
        copies[4 * n + 2].wait()
        y = mt(c[:, :count], e_v[n])
        copies[4 * n + 3].wait()
        reduced.append(c[:, count:] - mt(y, f_v[n]))
        y_ref[n] = y
    for copy in copies[4 * leaves :]:
        copy.wait()
    y, z = up_rows(mid_q_v[0], mid_e_v[0], mid_f_v[0], jnp.concatenate(reduced, axis=1))
    mid_y_ref[...] = y
    z_ref[...] = z
    for copy in ahead:
        copy.wait()


def pair_kernel(own_ref, other_ref, q_ref, e_ref, f_ref, y_ref, z_ref):
    second = lax.axis_index("panel") == 1
    own, other = own_ref[...], other_ref[...]
    block = jnp.concatenate(
        [jnp.where(second, other, own), jnp.where(second, own, other)], axis=1
    )
    y, z = up_rows(q_ref[0], e_ref[0], f_ref[0], block)
    y_ref[...] = y
    z_ref[...] = z


def in_order(bit, own_ref, other_ref):
    second = (lax.axis_index("leaf") >> bit) & 1 == 1
    own, other = own_ref[...], other_ref[...]
    return jnp.where(second, other, own), jnp.where(second, own, other)


def level_kernel(bit, own_ref, other_ref, packet_ref, z_ref):
    first_z, second_z = in_order(bit, own_ref, other_ref)
    z_ref[...] = mt(first_z, packet_ref[0]) + mt(second_z, packet_ref[1])


def leaf_maps_kernel(q_ref, g_ref, y_ref, base_ref, t_ref):
    leaves, size = q_ref.shape[0], q_ref.shape[1]
    count = g_ref.shape[1]
    for n in range(leaves):
        q1 = split(q_ref[n, :, :count])
        rows = slice(n * size, (n + 1) * size)
        t_ref[rows] = q_ref[n, :, count:] - mm(q1, g_ref[n])
        base_ref[rows] = mt(q1, y_ref[n])


def fold_kernel(
    base_ref, t_ref, mid_q_ref, mid_g_ref, mid_y_ref, pair_q_ref, pair_g_ref, pair_y_ref, *refs
):
    *refs, base_out, w_out = refs
    rank = pair_g_ref.shape[2]
    start = lax.axis_index("panel") * rank
    pair_q = pair_q_ref[0, pl.ds(pl.multiple_of(start, rank), rank), :]
    pair_q1 = split(pair_q[:, :rank])
    pair_t = split(pair_q[:, rank:] - mm(pair_q1, pair_g_ref[0]))
    mid_q = mid_q_ref[0]
    mid_q1 = split(mid_q[:, :rank])
    mid_t = split(mid_q[:, rank:] - mm(mid_q1, mid_g_ref[0]))
    offset = chain = None
    for bit in range(len(refs) // 3):
        packet_ref = refs[3 * bit + 2]
        first_z, second_z = in_order(bit, *refs[3 * bit : 3 * bit + 2])
        u = mt(first_z, packet_ref[2]) + mt(second_z, packet_ref[3])
        if bit == 0:
            offset, chain = u, split(packet_ref[4])
        else:
            offset = offset + mt(u, chain)
            chain = split(mm(chain, packet_ref[4]))
    mid_w = mt(pair_y_ref[...], pair_q1) + mt(offset, pair_t)
    leaf_w = mt(mid_y_ref[...], mid_q1) + mt(mid_w, mid_t)
    map_w = mm(mid_t, mm(pair_t, chain))
    leaves = map_w.shape[0] // rank
    size = base_ref.shape[0] // leaves
    for n in range(leaves):
        rows = slice(n * size, (n + 1) * size)
        part = slice(n * rank, (n + 1) * rank)
        t = split(t_ref[rows])
        base_out[rows] = base_ref[rows] + mt(t, leaf_w[:, part])
        w_out[rows] = mm(t, map_w[part])


def last_kernel(low, levels, chunks, base_ref, weight_ref, *refs):
    *refs, out_ref, result, sems = refs
    w = None
    for bit in range(levels - 1, low - 1, -1):
        packet_ref = refs[3 * (bit - low) + 2]
        first_z, second_z = in_order(bit, *refs[3 * (bit - low) : 3 * (bit - low) + 2])
        start = 0 if bit == levels - 1 else 2
        value = mt(first_z, packet_ref[start]) + mt(second_z, packet_ref[start + 1])
        if w is not None:
            value = value + mt(w, packet_ref[4])
        w = value
    w = split(w)
    rows = result.shape[0] // chunks
    copies = []
    for i in range(chunks):
        part = pl.ds(i * rows, rows)
        result[part] = base_ref[part] + mt(weight_ref[part], w)
        copies.append(pltpu.make_async_copy(result.at[part], out_ref.at[part], sems.at[i]))
        copies[-1].start()
    for copy in copies:
        copy.wait()


def lowest(bit):
    return lambda position: position & ((2 << bit) - 1) == 1 << bit


def clear(bits):
    return lambda position: position & ((1 << bits) - 1) == 0


def local(
    rhs, leaf_q, leaf_e, leaf_f, leaf_g, mid_q, mid_e, mid_f, mid_g,
    pair_q, pair_e, pair_f, pair_g, up_q, up_e, up_f, up_g,
):
    count_leaf, cores = lax.axis_size("leaf"), lax.axis_size("panel")
    depth = count_leaf.bit_length() - 1
    assert depth > 2 and cores == 2
    folded = 2
    rank, columns = up_e.shape[1], rhs.shape[1]
    leaves, count = leaf_e.shape[0], leaf_e.shape[1]
    tile, packet, top_shape = (columns, rank), (5, rank, rank), (2, rank, rank)
    dma = pltpu.SemaphoreType.DMA

    def swap_cores(value):
        return lax.ppermute(value, "panel", [(i, cores - 1 - i) for i in range(cores)])

    def across(value, *masks):
        pairs = []
        for p in range(count_leaf):
            for c in range(cores):
                pairs.append((p * cores + c, (p ^ masks[c % len(masks)]) * cores + c))
        return lax.ppermute(value, ("leaf", "panel"), pairs)

    ups = (up_q, up_e, up_f, up_g)
    low_half, high_half = call(
        node_kernel,
        [packet] * 2,
        wait_in=ups,
        scratch=[pltpu.VMEM(a.shape, F32) for a in ups] + [dma((4,))],
    )

    def home(level):
        return (level - 1) % cores

    first_round = []
    for level in range(1, depth + 1, cores):
        masks = [1 << (k - 1) for k in range(level, min(level + cores, depth + 1))]
        first_round.append(across(low_half, *masks))

    wait_in = (
        rhs, leaf_q, leaf_e, leaf_f, leaf_g, mid_q, mid_e, mid_f, mid_g, pair_q, pair_e, pair_f, pair_g
    )
    kept = (leaf_q, leaf_g, mid_q, mid_g, pair_q, pair_e, pair_f, pair_g)
    y, mid_y, z, *kept = call(
        leaf_kernel,
        [(leaves, columns, count), tile, tile] + [a.shape for a in kept],
        wait_in=wait_in,
        scratch=[pltpu.VMEM(a.shape, F32) for a in (rhs, leaf_e, leaf_f, mid_e, mid_f)]
        + [dma((4 * leaves + 3,)), dma((6,))],
    )
    leaf_q, leaf_g, mid_q, mid_g, pair_q, pair_e, pair_f, pair_g = kept
    other = swap_cores(z)
    pair_y, z = call(pair_kernel, [tile, tile], z, other, pair_q, pair_e, pair_f)

    held, full = {}, {}

    def finish(level):
        c = home(level)
        swapped = swap_cores(held[level])
        n = held[level].shape[0]
        full[level] = choose(n, [(c, None, held[level], 0, 0, n), (1 - c, None, swapped, 0, 0, n)])

    def receive_first(gate):
        for level in range(1, depth + 1):
            incoming, _ = lax.optimization_barrier((first_round[(level - 1) // cores], gate))
            if level == depth:
                (held[level],) = call(top_kernel, [top_shape], low_half, high_half, incoming)
                continue
            held[level] = choose(
                5,
                [(None, lowest(level - 1), high_half, 0, 0, 5), (None, clear(level), incoming, 0, 0, 5)],
            )
        finish(1)

    def start_round(r):
        moves = [[], []]
        for level in range(max(r, 2), depth + 1):
            moves[home(level)].append((level, level - r))
        groups = []
        for i in range(max(len(side) for side in moves)):
            group = [side[i] for side in moves if i < len(side)]
            masks = [1 << group[0][1]] * cores
            size = max(held[level].shape[0] for level, _ in group)
            choices = []
            for level, bit in group:
                masks[home(level)] = 1 << bit
                choices.append((home(level), None, held[level], 0, 0, held[level].shape[0]))
            operand = held[group[0][0]] if len(group) == 1 else choose(size, choices)
            groups.append((group, across(operand, *masks)))
        return groups

    def receive(r, groups, gate):
        for group, incoming in groups:
            incoming, _ = lax.optimization_barrier((incoming, gate))
            for level, bit in group:
                before = held[level]
                n = before.shape[0]

                def stays(position, bit=bit):
                    return position & ((2 << bit) - 1) != 1 << bit

                value = choose(
                    n, [(None, stays, before, 0, 0, n), (None, lowest(bit), incoming, 0, 0, n)]
                )
                held[level] = value
                if bit == 0:
                    finish(level)

    exchanged = []
    flying = None
    base = weight = None
    for bit in range(depth):
        other = across(z, 1 << bit)
        exchanged += [(z, other)]
        if bit == 0:
            receive_first(z)
        else:
            receive(bit + 1, flying, z)
        if bit + 2 <= depth:
            flying = start_round(bit + 2)
        if bit == 1:
            base, leaf_t = call(
                leaf_maps_kernel, [rhs.shape, (rhs.shape[0], rank)], leaf_q, leaf_g, y, after=(z,)
            )
        if bit == depth - 1:
            lowest_levels = []
            for level in range(1, folded + 1):
                lowest_levels += [*exchanged[level - 1], full[level]]
            base, weight = call(
                fold_kernel, [base.shape, leaf_t.shape], base, leaf_t,
                mid_q, mid_g, mid_y, pair_q, pair_g, pair_y, *lowest_levels, after=(z,),
            )
            break
        (z,) = call(
            functools.partial(level_kernel, bit), [tile], z, other, full[bit + 1],
            after=() if bit != 1 else (base,), cost=500000000,
        )

    above = []
    for level in range(folded + 1, depth + 1):
        above += [*exchanged[level - 1], full[level]]
    chunks = 2 * leaves
    return last_step(
        functools.partial(last_kernel, folded, depth, chunks), rhs.shape, chunks, base, weight, *above
    )


def last_step(kernel, shape, chunks, *operands):
    return pl.pallas_call(
        kernel,
        out_shape=jax.ShapeDtypeStruct(shape, F32),
        in_specs=[VMEM] * len(operands),
        out_specs=HBM,
        scratch_shapes=[pltpu.VMEM(shape, F32), pltpu.SemaphoreType.DMA((chunks,))],
        compiler_params=pltpu.CompilerParams(vmem_limit_bytes=20 * 2**20),
    )(*operands)


def solution(mesh):
    both, chip = ("leaf", "panel"), "leaf"
    in_specs = (P(both, None),) + (P(both, None, None),) * 8 + (P(chip, None, None),) * 8
    return jax.shard_map(
        local, mesh=mesh, in_specs=in_specs, out_specs=P(both, None), check_vma=False
    )
```

time: 54.8 us -> 43.6 us (0.80)
  waiting for transfers between devices: 21.1 us -> 11.4 us
  Pallas kernels: 13.8 us -> 13 us
  starting transfers between devices: 19.4 us -> 18.6 us
    ppermute x11 -> x10, waiting for transfers between devices: 20.2 us -> 10.4 us  [across(): return lax.ppermute(value, ('leaf', 'panel'), pairs)]
    ppermute x11 -> x10, starting transfers between devices: 18.7 us -> 16.2 us  [across(): return lax.ppermute(value, ('leaf', 'panel'), pairs)]
    ppermute x5, starting transfers between devices: 0.73 us -> 2.43 us  [swap_cores(): lax.ppermute(value, 'panel', [(i, cores - 1 - i) for i in range(cores)])]
    pallas_call x19 -> x25, Pallas kernels: 13.8 us -> 13 us  [the longest x24 11.4 us: call(): pl.pallas_call(body, out_shape=out_shape, in_specs=[HBM] * len(wait_in) +...]
  transfers between devices with their start and end apart: 16 -> 15, of which waited for: 9 -> 8; matrix products, arithmetic and copies ran while one was open for 0% -> 0% of each run, Pallas kernels for 18% -> 23%
where the time goes in v3:
time: 43.6 us; the launch traced here: 43.3 us
  starting transfers between devices  18.6 us (43%)
  Pallas kernels  13 us (30%)
  waiting for transfers between devices  11.4 us (26%)
    ppermute x10, starting transfers between devices, across(): return lax.ppermute(value, ('leaf', 'panel'), pairs)  16.2 us
    pallas_call x24, Pallas kernels, call(): pl.pallas_call(body, out_shape=out_shape, in_specs=[HBM] * len(wait_in) +...  11.4 us
    ppermute x10, waiting for transfers between devices, across(): return lax.ppermute(value, ('leaf', 'panel'), pairs)  10.4 us
    ppermute x5, starting transfers between devices, swap_cores(): lax.ppermute(value, 'panel', [(i, cores - 1 - i) for i in range(cores)])  2.43 us
    pallas_call x1, Pallas kernels, last_step(): pl.pallas_call(kernel, out_shape=jax.ShapeDtypeStruct(shape, F32), in_spe...  1.67 us
    ppermute x5, waiting for transfers between devices, swap_cores(): lax.ppermute(value, 'panel', [(i, cores - 1 - i) for i in range(cores)])  0.95 us
  transfers between devices with their start and end apart: 15, of which 8 were waited for; matrix products, arithmetic and copies ran while one was open for 0% of the time, Pallas kernels for 23%

profile of v3, /device:TPU:0, one launch (start us, length us, event | category | flops | bytes accessed | tf_op | source)
XLA Modules:
  0.0 43.3 jit_solution(13680672405801098860)
XLA Ops:
  0.0 1.6 %shard_map.165 = (f32[5,128,128]{2,1,0:T(8,128)S(1)}, f32[5,128,128]{2,1,0:T(8,128)S(1)}) custom-call(f32[1,256,256]{2,1,0:T(8,128)} %refs_0_.3, f32[1,128,128]{2,1,0:T(8,128)} %refs_1_.3, f32[1,128,128]{2,1,0:T(8,128)} %refs_2_.3, f32[1,128,128]{2,1,0:T(8,128)} %refs_3_.3), custom_call_target="tpu_custom_call" | custom-call | tf_op jit(solution)/shard_map/pallas_call | solution.py:49
  1.6 3.0 %collective-permute-start.2 = (f32[5,128,128]{2,1,0:T(8,128)S(1)}, f32[5,128,128]{2,1,0:T(8,128)S(1)}, u32[]{:S(2)}, u32[]{:S(2)}) collective-permute-start(f32[5,128,128]{2,1,0:T(8,128)S(1)} %get-tuple-element.39.refs_0_), channel_id=1, source_target_pairs={{0,2},{1,5},{2,0},{3,7},{4,6},{5,1},{6,4},{7,3},{8,10},{9,13},{10,... | collective-permute-start | bytes 983048 | tf_op jit(solution)/shard_map/ppermute | solution.py:295
  4.6 1.6 %collective-permute-start.5 = (f32[5,128,128]{2,1,0:T(8,128)S(1)}, f32[5,128,128]{2,1,0:T(8,128)S(1)}, u32[]{:S(2)}, u32[]{:S(2)}) collective-permute-start(f32[5,128,128]{2,1,0:T(8,128)S(1)} %get-tuple-element.39.refs_0_), channel_id=1, source_target_pairs={{0,8},{1,17},{2,10},{3,19},{4,12},{5,21},{6,14},{7,23},{8,0},{9,25... | collective-permute-start | bytes 983048 | tf_op jit(solution)/shard_map/ppermute | solution.py:295
  6.2 4.6 %shard_map.163 = (f32[2,128,384]{2,1,0:T(8,128)S(1)}, f32[128,128]{1,0:T(8,128)S(1)}, f32[128,128]{1,0:T(8,128)S(1)}, f32[2,512,512]{2,1,0:T(8,128)S(1)}, f32[2,...) custom-call(f32[1024,128]{1,0:T(8,128)} %refs_0_.2, ...), custom_call_target="tpu_custom_call" | custom-call | tf_op jit(solution)/shard_map/pallas_call | solution.py:49
  10.8 0.4 collective-permute-start
  11.2 0.9 %collective-permute-done.refs_1_ = f32[128,128]{1,0:T(8,128)S(1)} collective-permute-done((f32[128,128]{1,0:T(8,128)S(1)}, f32[128,128]{1,0:T(8,128)S(1)}, u32[]{:S(2)}, u32[]{:S(2)}) %collective-permute-start) | collective-permute-done | bytes 65568 | tf_op jit(solution)/shard_map/ppermute | solution.py:288
  12.1 0.6 %shard_map.164 = (f32[128,128]{1,0:T(8,128)S(1)}, f32[128,128]{1,0:T(8,128)S(1)}) custom-call(f32[128,128]{1,0:T(8,128)S(1)} %get-tuple-element.33.refs_0_, f32[128,128]{1,0:T(8,128)S(1)} %collective-permute-done.refs_1_, f32[1,256,256]{2,1,0:T(8,128)S(1)} %get-tuple-element.34.refs_2_.refs_5_, f32[1,128,128]{2,1,0:T(8,128)S(1)} %get-tuple-element.35.refs_3_, ...), custom_call_target="tpu_custom_call" | custom-call | tf_op jit(solution)/shard_map/pallas_call | solution.py:49
  12.7 0.0 collective-permute-done.2.refs_1_
  12.8 0.4 collective-permute-start.3
  13.2 1.0 %collective-permute-done.5.refs_1_.refs_2_ = f32[5,128,128]{2,1,0:T(8,128)S(1)} collective-permute-done((f32[5,128,128]{2,1,0:T(8,128)S(1)}, f32[5,128,128]{2,1,0:T(8,128)S(1)}, u32[]{:S(2)}, u32[]{:S(2)}) %collective-permute-start.5) | collective-permute-done | bytes 327712 | tf_op jit(solution)/shard_map/ppermute | solution.py:295
  14.3 1.3 %collective-permute-start.6 = (f32[5,128,128]{2,1,0:T(8,128)S(1)}, f32[5,128,128]{2,1,0:T(8,128)S(1)}, u32[]{:S(2)}, u32[]{:S(2)}) collective-permute-start(f32[5,128,128]{2,1,0:T(8,128)S(1)} %shard_map.172), channel_id=1, source_target_pairs={{0,4},{1,3},{2,6},{3,1},{4,0},{5,7},{6,2},{7,5},{8,12},{9,11},{10,... | collective-permute-start | bytes 983048 | tf_op jit(solution)/shard_map/ppermute | solution.py:295
  15.6 0.6 %collective-permute-start.1 = (f32[128,128]{1,0:T(8,128)S(1)}, f32[128,128]{1,0:T(8,128)S(1)}, u32[]{:S(2)}, u32[]{:S(2)}) collective-permute-start(f32[128,128]{1,0:T(8,128)S(1)} %get-tuple-element.37.refs_0_.refs_8_), channel_id=1, source_target_pairs={{0,2},{1,3},{2,0},{3,1},{4,6},{5,7},{6,4},{7,5},{8,10},{9,11},{10,... | collective-permute-start | bytes 196616 | tf_op jit(solution)/shard_map/ppermute | solution.py:295
  16.3 0.4 shard_map.177.refs_0_
  16.6 2.3 %collective-permute-start.9 = (f32[2,128,128]{2,1,0:T(8,128)S(1)}, f32[2,128,128]{2,1,0:T(8,128)S(1)}, u32[]{:S(2)}, u32[]{:S(2)}) collective-permute-start(f32[2,128,128]{2,1,0:T(8,128)S(1)} %shard_map.177.refs_0_), channel_id=1, source_target_pairs={{0,8},{1,9},{2,10},{3,11},{4,12},{5,13},{6,14},{7,15},{8,0},{9,1},... | collective-permute-start | bytes 393224 | tf_op jit(solution)/shard_map/ppermute | solution.py:295
  18.9 0.0 collective-permute-done.3.refs_1_
  18.9 1.7 %collective-permute-done.1.refs_1_.refs_9_ = f32[128,128]{1,0:T(8,128)S(1)} collective-permute-done((f32[128,128]{1,0:T(8,128)S(1)}, f32[128,128]{1,0:T(8,128)S(1)}, u32[]{:S(2)}, u32[]{:S(2)}) %collective-permute-start.1) | collective-permute-done | bytes 65568 | tf_op jit(solution)/shard_map/ppermute | solution.py:295
  20.7 0.3 shard_map.168.refs_3_.refs_0_.refs_11_
  20.9 0.5 %collective-permute-done.6.refs_1_ = f32[5,128,128]{2,1,0:T(8,128)S(1)} collective-permute-done((f32[5,128,128]{2,1,0:T(8,128)S(1)}, f32[5,128,128]{2,1,0:T(8,128)S(1)}, u32[]{:S(2)}, u32[]{:S(2)}) %collective-permute-start.6) | collective-permute-done | bytes 327712 | tf_op jit(solution)/shard_map/ppermute | solution.py:295
  21.5 1.0 %collective-permute-start.7 = (f32[5,128,128]{2,1,0:T(8,128)S(1)}, f32[5,128,128]{2,1,0:T(8,128)S(1)}, u32[]{:S(2)}, u32[]{:S(2)}) collective-permute-start(f32[5,128,128]{2,1,0:T(8,128)S(1)} %shard_map.173.refs_0_), channel_id=1, source_target_pairs={{0,1},{1,0},{2,3},{3,2},{4,5},{5,4},{6,7},{7,6},{8,9},{9,8},{10,11... | collective-permute-start | bytes 983048 | tf_op jit(solution)/shard_map/ppermute | solution.py:288
  22.5 0.0 collective-permute-done.9.refs_1_
  22.6 1.2 %collective-permute-start.10 = (f32[5,128,128]{2,1,0:T(8,128)S(1)}, f32[5,128,128]{2,1,0:T(8,128)S(1)}, u32[]{:S(2)}, u32[]{:S(2)}) collective-permute-start(f32[5,128,128]{2,1,0:T(8,128)S(1)} %shard_map.179), channel_id=1, source_target_pairs={{0,2},{1,5},{2,0},{3,7},{4,6},{5,1},{6,4},{7,3},{8,10},{9,13},{10,... | collective-permute-start | bytes 983048 | tf_op jit(solution)/shard_map/ppermute | solution.py:295
  23.7 0.9 %collective-permute-start.4 = (f32[128,128]{1,0:T(8,128)S(1)}, f32[128,128]{1,0:T(8,128)S(1)}, u32[]{:S(2)}, u32[]{:S(2)}) collective-permute-start(f32[128,128]{1,0:T(8,128)S(1)} %shard_map.168.refs_3_.refs_0_.refs_11_), channel_id=1, source_target_pairs={{0,4},{1,5},{2,6},{3,7},{4,0},{5,1},{6,2},{7,3},{8,12},{9,13},{10,... | collective-permute-start | bytes 196616 | tf_op jit(solution)/shard_map/ppermute | solution.py:295
  24.6 1.4 %shard_map.169 = (f32[1024,128]{1,0:T(8,128)S(1)}, f32[1024,128]{1,0:T(8,128)S(1)}) custom-call(f32[2,512,512]{2,1,0:T(8,128)S(1)} %get-tuple-element.30.refs_0_, f32[2,384,128]{2,1,0:T(8,128)S(1)} %get-tuple-element.31.refs_1_, f32[2,128,384]{2,1,0:T(8,128)S(1)} %get-tuple-element.32.refs_2_, f32[128,128]{1,0:T(8,128)S(1)} %shard_map.168.refs_3_.refs_0_.refs_11_), custom_call_target="tpu_custom_call" | custom-call | tf_op jit(solution)/shard_map/pallas_call | solution.py:49
  26.0 0.0 collective-permute-done.7.refs_1_
  26.1 2.7 %collective-permute-done.4.refs_1_.refs_12_ = f32[128,128]{1,0:T(8,128)S(1)} collective-permute-done((f32[128,128]{1,0:T(8,128)S(1)}, f32[128,128]{1,0:T(8,128)S(1)}, u32[]{:S(2)}, u32[]{:S(2)}) %collective-permute-start.4) | collective-permute-done | bytes 65568 | tf_op jit(solution)/shard_map/ppermute | solution.py:295
  28.8 0.2 shard_map.175.refs_0_
  29.0 0.7 %collective-permute-done.10.refs_1_ = f32[5,128,128]{2,1,0:T(8,128)S(1)} collective-permute-done((f32[5,128,128]{2,1,0:T(8,128)S(1)}, f32[5,128,128]{2,1,0:T(8,128)S(1)}, u32[]{:S(2)}, u32[]{:S(2)}) %collective-permute-start.10) | collective-permute-done | bytes 327712 | tf_op jit(solution)/shard_map/ppermute | solution.py:295
  29.7 0.6 %collective-permute-start.11 = (f32[5,128,128]{2,1,0:T(8,128)S(1)}, f32[5,128,128]{2,1,0:T(8,128)S(1)}, u32[]{:S(2)}, u32[]{:S(2)}) collective-permute-start(f32[5,128,128]{2,1,0:T(8,128)S(1)} %shard_map.180.refs_0_), channel_id=1, source_target_pairs={{0,1},{1,0},{2,3},{3,2},{4,5},{5,4},{6,7},{7,6},{8,9},{9,8},{10,11... | collective-permute-start | bytes 983048 | tf_op jit(solution)/shard_map/ppermute | solution.py:288
  30.4 1.2 %collective-permute-start.13 = (f32[2,128,128]{2,1,0:T(8,128)S(1)}, f32[2,128,128]{2,1,0:T(8,128)S(1)}, u32[]{:S(2)}, u32[]{:S(2)}) collective-permute-start(f32[2,128,128]{2,1,0:T(8,128)S(1)} %shard_map.184.refs_0_), channel_id=1, source_target_pairs={{0,2},{1,3},{2,0},{3,1},{4,6},{5,7},{6,4},{7,5},{8,10},{9,11},{10,... | collective-permute-start | bytes 393224 | tf_op jit(solution)/shard_map/ppermute | solution.py:295
  31.5 1.4 %collective-permute-start.8 = (f32[128,128]{1,0:T(8,128)S(1)}, f32[128,128]{1,0:T(8,128)S(1)}, u32[]{:S(2)}, u32[]{:S(2)}) collective-permute-start(f32[128,128]{1,0:T(8,128)S(1)} %shard_map.175.refs_0_), channel_id=1, source_target_pairs={{0,8},{1,9},{2,10},{3,11},{4,12},{5,13},{6,14},{7,15},{8,0},{9,1},... | collective-permute-start | bytes 196616 | tf_op jit(solution)/shard_map/ppermute | solution.py:295
  33.0 0.0 collective-permute-done.11.refs_1_
  33.0 2.8 %collective-permute-done.8.refs_1_ = f32[128,128]{1,0:T(8,128)S(1)} collective-permute-done((f32[128,128]{1,0:T(8,128)S(1)}, f32[128,128]{1,0:T(8,128)S(1)}, u32[]{:S(2)}, u32[]{:S(2)}) %collective-permute-start.8) | collective-permute-done | bytes 65568 | tf_op jit(solution)/shard_map/ppermute | solution.py:295
  35.8 0.3 shard_map.182.refs_14_.refs_3_
  36.1 0.0 collective-permute-done.13.refs_1_
  36.1 0.1 collective-permute-start.14
  36.2 2.7 %collective-permute-start.12 = (f32[128,128]{1,0:T(8,128)S(1)}, f32[128,128]{1,0:T(8,128)S(1)}, u32[]{:S(2)}, u32[]{:S(2)}) collective-permute-start(f32[128,128]{1,0:T(8,128)S(1)} %shard_map.182.refs_14_.refs_3_), channel_id=1, source_target_pairs={{0,16},{1,17},{2,18},{3,19},{4,20},{5,21},{6,22},{7,23},{8,24},{9,... | collective-permute-start | bytes 196616 | tf_op jit(solution)/shard_map/ppermute | solution.py:295
  38.9 1.7 %shard_map.183 = (f32[1024,128]{1,0:T(8,128)S(1)}, f32[1024,128]{1,0:T(8,128)S(1)}) custom-call(f32[1024,128]{1,0:T(8,128)S(1)} %get-tuple-element.41.refs_3_.refs_0_, f32[1024,128]{1,0:T(8,128)S(1)} %get-tuple-element.42.refs_1_, f32[1,256,256]{2,1,0:T(8,128)S(1)} %get-tuple-element.43.refs_2_, f32[1,128,128]{2,1,0:T(8,128)S(1)} %get-tuple-element.44.refs_3_, ...), custom_call_target="tpu_custom_call" | custom-call | tf_op jit(solution)/shard_map/pallas_call | solution.py:49
  40.6 0.0 collective-permute-done.14.refs_1_
  40.6 1.0 %collective-permute-done.12.refs_4_ = f32[128,128]{1,0:T(8,128)S(1)} collective-permute-done((f32[128,128]{1,0:T(8,128)S(1)}, f32[128,128]{1,0:T(8,128)S(1)}, u32[]{:S(2)}, u32[]{:S(2)}) %collective-permute-start.12) | collective-permute-done | bytes 65568 | tf_op jit(solution)/shard_map/ppermute | solution.py:295
  41.6 1.7 %shard_map.187 = f32[1024,128]{1,0:T(8,128)} custom-call(f32[1024,128]{1,0:T(8,128)S(1)} %get-tuple-element.52.base_ref, f32[1024,128]{1,0:T(8,128)S(1)} %get-tuple-element.53.weight_ref, f32[128,128]{1,0:T(8,128)S(1)} %shard_map.175.refs_0_, f32[128,128]{1,0:T(8,128)S(1)} %collective-permute-done.8.refs_1_, f32[5,128,128]{2,1,0:T(8,128)S(1)} %shard_map.181.refs_2_, ...), custom_call_target="tpu_custom_call" | custom-call | tf_op jit(solution)/shard_map/pallas_call | solution.py:422
  (15 shorter events, 0.4 us)
Async XLA Ops:
  1.6 11.1 %collective-permute-start.2 = (f32[5,128,128]{2,1,0:T(8,128)S(1)}, f32[5,128,128]{2,1,0:T(8,128)S(1)}, u32[]{:S(2)}, u32[]{:S(2)}) collective-permute-start(f32[5,128,128]{2,1,0:T(8,128)S(1)} %get-tuple-element.39.refs_0_), channel_id=1, source_target_pairs={{0,2},{1,5},{2,0},{3,7},{4,6},{5,1},{6,4},{7,3},{8,10},{9,13},{10,... | collective-permute-start | bytes 983048 | tf_op jit(solution)/shard_map/ppermute | solution.py:295
  4.6 9.6 %collective-permute-start.5 = (f32[5,128,128]{2,1,0:T(8,128)S(1)}, f32[5,128,128]{2,1,0:T(8,128)S(1)}, u32[]{:S(2)}, u32[]{:S(2)}) collective-permute-start(f32[5,128,128]{2,1,0:T(8,128)S(1)} %get-tuple-element.39.refs_0_), channel_id=1, source_target_pairs={{0,8},{1,17},{2,10},{3,19},{4,12},{5,21},{6,14},{7,23},{8,0},{9,25... | collective-permute-start | bytes 983048 | tf_op jit(solution)/shard_map/ppermute | solution.py:295
  10.8 1.3 %collective-permute-start = (f32[128,128]{1,0:T(8,128)S(1)}, f32[128,128]{1,0:T(8,128)S(1)}, u32[]{:S(2)}, u32[]{:S(2)}) collective-permute-start(f32[128,128]{1,0:T(8,128)S(1)} %get-tuple-element.33.refs_0_), channel_id=1, source_target_pairs={{0,1},{1,0},{2,3},{3,2},{4,5},{5,4},{6,7},{7,6},{8,9},{9,8},{10,11... | collective-permute-start | bytes 196616 | tf_op jit(solution)/shard_map/ppermute | solution.py:288
  12.8 6.1 %collective-permute-start.3 = (f32[5,128,128]{2,1,0:T(8,128)S(1)}, f32[5,128,128]{2,1,0:T(8,128)S(1)}, u32[]{:S(2)}, u32[]{:S(2)}) collective-permute-start(f32[5,128,128]{2,1,0:T(8,128)S(1)} %shard_map.166.refs_0_), channel_id=1, source_target_pairs={{0,1},{1,0},{2,3},{3,2},{4,5},{5,4},{6,7},{7,6},{8,9},{9,8},{10,11... | collective-permute-start | bytes 983048 | tf_op jit(solution)/shard_map/ppermute | solution.py:288
  14.3 7.1 %collective-permute-start.6 = (f32[5,128,128]{2,1,0:T(8,128)S(1)}, f32[5,128,128]{2,1,0:T(8,128)S(1)}, u32[]{:S(2)}, u32[]{:S(2)}) collective-permute-start(f32[5,128,128]{2,1,0:T(8,128)S(1)} %shard_map.172), channel_id=1, source_target_pairs={{0,4},{1,3},{2,6},{3,1},{4,0},{5,7},{6,2},{7,5},{8,12},{9,11},{10,... | collective-permute-start | bytes 983048 | tf_op jit(solution)/shard_map/ppermute | solution.py:295
  15.6 5.0 %collective-permute-start.1 = (f32[128,128]{1,0:T(8,128)S(1)}, f32[128,128]{1,0:T(8,128)S(1)}, u32[]{:S(2)}, u32[]{:S(2)}) collective-permute-start(f32[128,128]{1,0:T(8,128)S(1)} %get-tuple-element.37.refs_0_.refs_8_), channel_id=1, source_target_pairs={{0,2},{1,3},{2,0},{3,1},{4,6},{5,7},{6,4},{7,5},{8,10},{9,11},{10,... | collective-permute-start | bytes 196616 | tf_op jit(solution)/shard_map/ppermute | solution.py:295
  16.6 5.8 %collective-permute-start.9 = (f32[2,128,128]{2,1,0:T(8,128)S(1)}, f32[2,128,128]{2,1,0:T(8,128)S(1)}, u32[]{:S(2)}, u32[]{:S(2)}) collective-permute-start(f32[2,128,128]{2,1,0:T(8,128)S(1)} %shard_map.177.refs_0_), channel_id=1, source_target_pairs={{0,8},{1,9},{2,10},{3,11},{4,12},{5,13},{6,14},{7,15},{8,0},{9,1},... | collective-permute-start | bytes 393224 | tf_op jit(solution)/shard_map/ppermute | solution.py:295
  21.5 4.6 %collective-permute-start.7 = (f32[5,128,128]{2,1,0:T(8,128)S(1)}, f32[5,128,128]{2,1,0:T(8,128)S(1)}, u32[]{:S(2)}, u32[]{:S(2)}) collective-permute-start(f32[5,128,128]{2,1,0:T(8,128)S(1)} %shard_map.173.refs_0_), channel_id=1, source_target_pairs={{0,1},{1,0},{2,3},{3,2},{4,5},{5,4},{6,7},{7,6},{8,9},{9,8},{10,11... | collective-permute-start | bytes 983048 | tf_op jit(solution)/shard_map/ppermute | solution.py:288
  22.6 7.1 %collective-permute-start.10 = (f32[5,128,128]{2,1,0:T(8,128)S(1)}, f32[5,128,128]{2,1,0:T(8,128)S(1)}, u32[]{:S(2)}, u32[]{:S(2)}) collective-permute-start(f32[5,128,128]{2,1,0:T(8,128)S(1)} %shard_map.179), channel_id=1, source_target_pairs={{0,2},{1,5},{2,0},{3,7},{4,6},{5,1},{6,4},{7,3},{8,10},{9,13},{10,... | collective-permute-start | bytes 983048 | tf_op jit(solution)/shard_map/ppermute | solution.py:295
  23.7 5.0 %collective-permute-start.4 = (f32[128,128]{1,0:T(8,128)S(1)}, f32[128,128]{1,0:T(8,128)S(1)}, u32[]{:S(2)}, u32[]{:S(2)}) collective-permute-start(f32[128,128]{1,0:T(8,128)S(1)} %shard_map.168.refs_3_.refs_0_.refs_11_), channel_id=1, source_target_pairs={{0,4},{1,5},{2,6},{3,7},{4,0},{5,1},{6,2},{7,3},{8,12},{9,13},{10,... | collective-permute-start | bytes 196616 | tf_op jit(solution)/shard_map/ppermute | solution.py:295
  29.7 3.2 %collective-permute-start.11 = (f32[5,128,128]{2,1,0:T(8,128)S(1)}, f32[5,128,128]{2,1,0:T(8,128)S(1)}, u32[]{:S(2)}, u32[]{:S(2)}) collective-permute-start(f32[5,128,128]{2,1,0:T(8,128)S(1)} %shard_map.180.refs_0_), channel_id=1, source_target_pairs={{0,1},{1,0},{2,3},{3,2},{4,5},{5,4},{6,7},{7,6},{8,9},{9,8},{10,11... | collective-permute-start | bytes 983048 | tf_op jit(solution)/shard_map/ppermute | solution.py:288
  30.4 5.7 %collective-permute-start.13 = (f32[2,128,128]{2,1,0:T(8,128)S(1)}, f32[2,128,128]{2,1,0:T(8,128)S(1)}, u32[]{:S(2)}, u32[]{:S(2)}) collective-permute-start(f32[2,128,128]{2,1,0:T(8,128)S(1)} %shard_map.184.refs_0_), channel_id=1, source_target_pairs={{0,2},{1,3},{2,0},{3,1},{4,6},{5,7},{6,4},{7,5},{8,10},{9,11},{10,... | collective-permute-start | bytes 393224 | tf_op jit(solution)/shard_map/ppermute | solution.py:295
  31.5 4.3 %collective-permute-start.8 = (f32[128,128]{1,0:T(8,128)S(1)}, f32[128,128]{1,0:T(8,128)S(1)}, u32[]{:S(2)}, u32[]{:S(2)}) collective-permute-start(f32[128,128]{1,0:T(8,128)S(1)} %shard_map.175.refs_0_), channel_id=1, source_target_pairs={{0,8},{1,9},{2,10},{3,11},{4,12},{5,13},{6,14},{7,15},{8,0},{9,1},... | collective-permute-start | bytes 196616 | tf_op jit(solution)/shard_map/ppermute | solution.py:295
  36.1 4.5 %collective-permute-start.14 = (f32[2,128,128]{2,1,0:T(8,128)S(1)}, f32[2,128,128]{2,1,0:T(8,128)S(1)}, u32[]{:S(2)}, u32[]{:S(2)}) collective-permute-start(f32[2,128,128]{2,1,0:T(8,128)S(1)} %shard_map.185.refs_0_), channel_id=1, source_target_pairs={{0,1},{1,0},{2,3},{3,2},{4,5},{5,4},{6,7},{7,6},{8,9},{9,8},{10,11... | collective-permute-start | bytes 393224 | tf_op jit(solution)/shard_map/ppermute | solution.py:288
  36.2 5.4 %collective-permute-start.12 = (f32[128,128]{1,0:T(8,128)S(1)}, f32[128,128]{1,0:T(8,128)S(1)}, u32[]{:S(2)}, u32[]{:S(2)}) collective-permute-start(f32[128,128]{1,0:T(8,128)S(1)} %shard_map.182.refs_14_.refs_3_), channel_id=1, source_target_pairs={{0,16},{1,17},{2,18},{3,19},{4,20},{5,21},{6,22},{7,23},{8,24},{9,... | collective-permute-start | bytes 196616 | tf_op jit(solution)/shard_map/ppermute | solution.py:295

commit v4 on v3

--- a/solution.py
+++ b/solution.py
@@ -8,6 +8,7 @@
 from jax.sharding import PartitionSpec as P
 
 F32 = jnp.float32
+LV = (4000000000,4000000000,4000000000)+(500000000,)*9
 VMEM = pl.BlockSpec(memory_space=pltpu.VMEM)
 ANY = pl.BlockSpec(memory_space=pl.ANY)
 HBM = pl.BlockSpec(memory_space=pltpu.HBM)
@@ -48,6 +49,7 @@
 
     return pl.pallas_call(
         body,
+        name=getattr(kernel, "func", kernel).__name__,
         out_shape=out_shape,
         in_specs=[HBM] * len(wait_in) + [VMEM] * len(operands) + [ANY] * (n_in - used),
         out_specs=[VMEM] * n_out + [ANY] * len(through),
@@ -130,7 +132,7 @@
             pl.when(here)(fill)
 
     shape = (size,) + choices[0][2].shape[1:]
-    return call(kernel, [shape], *[c[2] for c in choices], after=after)[0]
+    return call(kernel, [shape], *[c[2] for c in choices], after=after, cost=1000)[0]
 
 
 def leaf_kernel(
@@ -184,6 +186,10 @@
     z_ref[...] = z
 
 
+def mark_kernel(ref, out_ref):
+    out_ref[...] = ref[: out_ref.shape[0]]
+
+
 def in_order(bit, own_ref, other_ref):
     second = (lax.axis_index("leaf") >> bit) & 1 == 1
     own, other = own_ref[...], other_ref[...]
@@ -221,12 +227,12 @@
     for bit in range(len(refs) // 3):
         packet_ref = refs[3 * bit + 2]
         first_z, second_z = in_order(bit, *refs[3 * bit : 3 * bit + 2])
-        u = mt(first_z, packet_ref[2]) + mt(second_z, packet_ref[3])
+        u = mt(first_z, packet_ref[0]) + mt(second_z, packet_ref[1])
         if bit == 0:
-            offset, chain = u, split(packet_ref[4])
+            offset, chain = u, split(packet_ref[2])
         else:
             offset = offset + mt(u, chain)
-            chain = split(mm(chain, packet_ref[4]))
+            chain = split(mm(chain, packet_ref[2]))
     mid_w = mt(pair_y_ref[...], pair_q1) + mt(offset, pair_t)
     leaf_w = mt(mid_y_ref[...], mid_q1) + mt(mid_w, mid_t)
     map_w = mm(mid_t, mm(pair_t, chain))
@@ -240,17 +246,9 @@
         w_out[rows] = mm(t, map_w[part])
 
 
-def last_kernel(low, levels, chunks, base_ref, weight_ref, *refs):
-    *refs, out_ref, result, sems = refs
-    w = None
-    for bit in range(levels - 1, low - 1, -1):
-        packet_ref = refs[3 * (bit - low) + 2]
-        first_z, second_z = in_order(bit, *refs[3 * (bit - low) : 3 * (bit - low) + 2])
-        start = 0 if bit == levels - 1 else 2
-        value = mt(first_z, packet_ref[start]) + mt(second_z, packet_ref[start + 1])
-        if w is not None:
-            value = value + mt(w, packet_ref[4])
-        w = value
+def last_kernel(bit, chunks, base_ref, weight_ref, own_ref, other_ref, top_ref, out_ref, result, sems):
+    first_z, second_z = in_order(bit, own_ref, other_ref)
+    w = mt(first_z, top_ref[0]) + mt(second_z, top_ref[1])
     w = split(w)
     rows = result.shape[0] // chunks
     copies = []
@@ -278,7 +276,6 @@
     count_leaf, cores = lax.axis_size("leaf"), lax.axis_size("panel")
     depth = count_leaf.bit_length() - 1
     assert depth > 2 and cores == 2
-    folded = 2
     rank, columns = up_e.shape[1], rhs.shape[1]
     leaves, count = leaf_e.shape[0], leaf_e.shape[1]
     tile, packet, top_shape = (columns, rank), (5, rank, rank), (2, rank, rank)
@@ -305,10 +302,13 @@
     def home(level):
         return (level - 1) % cores
 
-    first_round = []
-    for level in range(1, depth + 1, cores):
-        masks = [1 << (k - 1) for k in range(level, min(level + cores, depth + 1))]
-        first_round.append(across(low_half, *masks))
+    sides = [[k for k in range(1, depth + 1) if home(k) == c] for c in range(cores)]
+    sides[1].reverse()
+    first_round = {}
+    for i, level in enumerate(sides[0]):
+        pair = [level, *sides[1][i : i + 1]]
+        incoming = across(low_half, *[1 << (k - 1) for k in pair])
+        first_round.update({k: incoming for k in pair})
 
     wait_in = (
         rhs, leaf_q, leaf_e, leaf_f, leaf_g, mid_q, mid_e, mid_f, mid_g, pair_q, pair_e, pair_f, pair_g
@@ -320,49 +320,56 @@
         wait_in=wait_in,
         scratch=[pltpu.VMEM(a.shape, F32) for a in (rhs, leaf_e, leaf_f, mid_e, mid_f)]
         + [dma((4 * leaves + 3,)), dma((6,))],
+        cost=1000,
     )
     leaf_q, leaf_g, mid_q, mid_g, pair_q, pair_e, pair_f, pair_g = kept
     other = swap_cores(z)
-    pair_y, z = call(pair_kernel, [tile, tile], z, other, pair_q, pair_e, pair_f)
-
-    held, full = {}, {}
-
-    def finish(level):
-        c = home(level)
-        swapped = swap_cores(held[level])
-        n = held[level].shape[0]
-        full[level] = choose(n, [(c, None, held[level], 0, 0, n), (1 - c, None, swapped, 0, 0, n)])
+    base, leaf_t = call(
+        leaf_maps_kernel, [rhs.shape, (rhs.shape[0], rank)], leaf_q, leaf_g, y, cost=1000000000
+    )
+    pair_y, z = call(
+        pair_kernel, [tile, tile], z, other, pair_q, pair_e, pair_f, after=(base,), cost=1000
+    )
+
+    up, down, full_up, full_down = {}, {}, {}, {}
+
+    def on_both(level, here, after=()):
+        c, n = home(level), here.shape[0]
+        swapped = swap_cores(here)
+        return choose(n, [(c, None, here, 0, 0, n), (1 - c, None, swapped, 0, 0, n)], after=after)
 
     def receive_first(gate):
         for level in range(1, depth + 1):
-            incoming, _ = lax.optimization_barrier((first_round[(level - 1) // cores], gate))
+            incoming, _ = lax.optimization_barrier((first_round[level], gate))
             if level == depth:
-                (held[level],) = call(top_kernel, [top_shape], low_half, high_half, incoming)
+                (up[level],) = call(top_kernel, [top_shape], low_half, high_half, incoming, cost=1000)
                 continue
-            held[level] = choose(
-                5,
-                [(None, lowest(level - 1), high_half, 0, 0, 5), (None, clear(level), incoming, 0, 0, 5)],
-            )
-        finish(1)
-
-    def start_round(r):
+            owner, below = lowest(level - 1), clear(level)
+            for held, first, n in ((up, 0, 2), (down, 2, 3)):
+                held[level] = choose(
+                    n, [(None, owner, high_half, first, 0, n), (None, below, incoming, first, 0, n)]
+                )
+        full_up[1], full_down[1] = on_both(1, up[1]), on_both(1, down[1])
+
+    def start_round(r, held):
         moves = [[], []]
         for level in range(max(r, 2), depth + 1):
-            moves[home(level)].append((level, level - r))
+            if level in held:
+                moves[home(level)].append((level, level - r))
         groups = []
         for i in range(max(len(side) for side in moves)):
             group = [side[i] for side in moves if i < len(side)]
-            masks = [1 << group[0][1]] * cores
-            size = max(held[level].shape[0] for level, _ in group)
+            masks = [1 << (group[0][1] != 1)] * cores
             choices = []
             for level, bit in group:
                 masks[home(level)] = 1 << bit
                 choices.append((home(level), None, held[level], 0, 0, held[level].shape[0]))
-            operand = held[group[0][0]] if len(group) == 1 else choose(size, choices)
+            n = held[group[0][0]].shape[0]
+            operand = held[group[0][0]] if len(group) == 1 else choose(n, choices)
             groups.append((group, across(operand, *masks)))
         return groups
 
-    def receive(r, groups, gate):
+    def receive(groups, held, full, gate, after=()):
         for group, incoming in groups:
             incoming, _ = lax.optimization_barrier((incoming, gate))
             for level, bit in group:
@@ -372,49 +379,45 @@
                 def stays(position, bit=bit):
                     return position & ((2 << bit) - 1) != 1 << bit
 
-                value = choose(
+                held[level] = choose(
                     n, [(None, stays, before, 0, 0, n), (None, lowest(bit), incoming, 0, 0, n)]
                 )
-                held[level] = value
                 if bit == 0:
-                    finish(level)
+                    full[level] = on_both(level, held[level], after)
 
     exchanged = []
-    flying = None
-    base = weight = None
+    flying_up = flying_down = ()
     for bit in range(depth):
         other = across(z, 1 << bit)
         exchanged += [(z, other)]
         if bit == 0:
             receive_first(z)
-        else:
-            receive(bit + 1, flying, z)
-        if bit + 2 <= depth:
-            flying = start_round(bit + 2)
-        if bit == 1:
-            base, leaf_t = call(
-                leaf_maps_kernel, [rhs.shape, (rhs.shape[0], rank)], leaf_q, leaf_g, y, after=(z,)
-            )
+        mark = call(mark_kernel, [(8, rank)], z, cost=4000000000)
+        if bit != depth - 2:
+            receive(flying_down, down, full_down, z, mark)
         if bit == depth - 1:
             lowest_levels = []
-            for level in range(1, folded + 1):
-                lowest_levels += [*exchanged[level - 1], full[level]]
+            for level in range(1, depth):
+                lowest_levels += [*exchanged[level - 1], full_down[level]]
             base, weight = call(
                 fold_kernel, [base.shape, leaf_t.shape], base, leaf_t,
-                mid_q, mid_g, mid_y, pair_q, pair_g, pair_y, *lowest_levels, after=(z,),
+                mid_q, mid_g, mid_y, pair_q, pair_g, pair_y, *lowest_levels, after=(z,), cost=2000000000,
             )
+            receive(flying_up, up, full_up, z, (weight,))
             break
+        receive(flying_up, up, full_up, z, mark)
+        flying_up = start_round(bit + 2, up) if bit + 2 <= depth else ()
+        if bit + 2 < depth:
+            flying_down = start_round(bit + 2, down)
         (z,) = call(
-            functools.partial(level_kernel, bit), [tile], z, other, full[bit + 1],
-            after=() if bit != 1 else (base,), cost=500000000,
+            functools.partial(level_kernel, bit), [tile], z, other, full_up[bit + 1],
+            cost=LV[bit],
         )
 
-    above = []
-    for level in range(folded + 1, depth + 1):
-        above += [*exchanged[level - 1], full[level]]
     chunks = 2 * leaves
     return last_step(
-        functools.partial(last_kernel, folded, depth, chunks), rhs.shape, chunks, base, weight, *above
+        functools.partial(last_kernel, depth - 1, chunks), rhs.shape, chunks, base, weight,
+        *exchanged[depth - 1], full_up[depth],
     )
 
 

time: 43.6 us -> 39.3 us (0.901)
  waiting for transfers between devices: 11.4 us -> 6.24 us
  starting transfers between devices: 18.6 us -> 19.2 us
    ppermute x10 -> x12, waiting for transfers between devices: 10.4 us -> 4.66 us  [across(): return lax.ppermute(value, ('leaf', 'panel'), pairs)]
    ppermute x10 -> x12, starting transfers between devices: 16.2 us -> 17.8 us  [across(): return lax.ppermute(value, ('leaf', 'panel'), pairs)]
    ppermute x5 -> x8, starting transfers between devices: 2.43 us -> 1.4 us  [swap_cores(): lax.ppermute(value, 'panel', [(i, cores - 1 - i) for i in range(cores)])]
    ppermute x5 -> x8, waiting for transfers between devices: 0.95 us -> 1.58 us  [swap_cores(): lax.ppermute(value, 'panel', [(i, cores - 1 - i) for i in range(cores)])]
    pallas_call x24 -> x37, Pallas kernels: 11.4 us -> 11.8 us  [call(): pl.pallas_call(body, name=getattr(kernel, 'func', kernel).__name__, out_s...]
  transfers between devices with their start and end apart: 15 -> 20, of which waited for: 8 -> 7; matrix products, arithmetic and copies ran while one was open for 0% -> 0% of each run, Pallas kernels for 23% -> 26%
where the time goes in v4:
time: 39.3 us; the launch traced here: 39.1 us
  starting transfers between devices  19.2 us (49%)
  Pallas kernels  13.3 us (34%)
  waiting for transfers between devices  6.24 us (16%)
    ppermute x12, starting transfers between devices, across(): return lax.ppermute(value, ('leaf', 'panel'), pairs)  17.8 us
    pallas_call x37, Pallas kernels, call(): pl.pallas_call(body, name=getattr(kernel, 'func', kernel).__name__, out_s...  11.8 us
    ppermute x12, waiting for transfers between devices, across(): return lax.ppermute(value, ('leaf', 'panel'), pairs)  4.66 us
    ppermute x8, waiting for transfers between devices, swap_cores(): lax.ppermute(value, 'panel', [(i, cores - 1 - i) for i in range(cores)])  1.58 us
    pallas_call x1, Pallas kernels, last_step(): pl.pallas_call(kernel, out_shape=jax.ShapeDtypeStruct(shape, F32), in_spe...  1.49 us
    ppermute x8, starting transfers between devices, swap_cores(): lax.ppermute(value, 'panel', [(i, cores - 1 - i) for i in range(cores)])  1.4 us
  transfers between devices with their start and end apart: 20, of which 7 were waited for; matrix products, arithmetic and copies ran while one was open for 0% of the time, Pallas kernels for 26%

profile of v4, /device:TPU:0, one launch (start us, length us, event | category | flops | bytes accessed | tf_op | source)
XLA Modules:
  0.0 39.1 jit_solution(16044477337715380578)
XLA Ops:
  0.0 1.6 %node_kernel.1 = (f32[5,128,128]{2,1,0:T(8,128)S(1)}, f32[5,128,128]{2,1,0:T(8,128)S(1)}) custom-call(f32[1,256,256]{2,1,0:T(8,128)} %refs_0_.3, f32[1,128,128]{2,1,0:T(8,128)} %refs_1_.3, f32[1,128,128]{2,1,0:T(8,128)} %refs_2_.3, f32[1,128,128]{2,1,0:T(8,128)} %refs_3_.3), custom_call_target="tpu_custom_call" | custom-call | tf_op jit(solution)/shard_map/node_kernel/pallas_call | solution.py:50
  1.6 3.0 %collective-permute-start.2 = (f32[5,128,128]{2,1,0:T(8,128)S(1)}, f32[5,128,128]{2,1,0:T(8,128)S(1)}, u32[]{:S(2)}, u32[]{:S(2)}) collective-permute-start(f32[5,128,128]{2,1,0:T(8,128)S(1)} %get-tuple-element.48.refs_0_), channel_id=1, source_target_pairs={{0,2},{1,17},{2,0},{3,19},{4,6},{5,21},{6,4},{7,23},{8,10},{9,25},... | collective-permute-start | bytes 983048 | tf_op jit(solution)/shard_map/ppermute | solution.py:292
  4.6 1.6 %collective-permute-start.6 = (f32[5,128,128]{2,1,0:T(8,128)S(1)}, f32[5,128,128]{2,1,0:T(8,128)S(1)}, u32[]{:S(2)}, u32[]{:S(2)}) collective-permute-start(f32[5,128,128]{2,1,0:T(8,128)S(1)} %get-tuple-element.48.refs_0_), channel_id=1, source_target_pairs={{0,8},{1,5},{2,10},{3,7},{4,12},{5,1},{6,14},{7,3},{8,0},{9,13},{1... | collective-permute-start | bytes 983048 | tf_op jit(solution)/shard_map/ppermute | solution.py:292
  6.2 4.6 %leaf_kernel.1 = (f32[2,128,384]{2,1,0:T(8,128)S(1)}, f32[128,128]{1,0:T(8,128)S(1)}, f32[128,128]{1,0:T(8,128)S(1)}, f32[2,512,512]{2,1,0:T(8,128)S(1)}, f32[2,...) custom-call(f32[1024,128]{1,0:T(8,128)} %refs_0_.2, ...), custom_call_target="tpu_custom_call" | custom-call | flops 1000 | bytes 1000 | tf_op jit(solution)/shard_map/leaf_kernel/pallas_call | solution.py:50
  10.8 0.4 collective-permute-start
  11.2 1.4 %leaf_maps_kernel.1 = (f32[1024,128]{1,0:T(8,128)S(1)}, f32[1024,128]{1,0:T(8,128)S(1)}) custom-call(f32[2,512,512]{2,1,0:T(8,128)S(1)} %get-tuple-element.32.refs_0_, f32[2,384,128]{2,1,0:T(8,128)S(1)} %get-tuple-element.33.refs_1_, f32[2,128,384]{2,1,0:T(8,128)S(1)} %get-tuple-element.34.refs_2_), custom_call_target="tpu_custom_call" | custom-call | flops 1000000000 | bytes 1000 | tf_op jit(solution)/shard_map/leaf_maps_kernel/pallas_call | solution.py:50
  12.6 0.0 collective-permute-done.refs_1_
  12.6 0.6 %pair_kernel.1 = (f32[128,128]{1,0:T(8,128)S(1)}, f32[128,128]{1,0:T(8,128)S(1)}) custom-call(f32[128,128]{1,0:T(8,128)S(1)} %get-tuple-element.42.refs_0_, f32[128,128]{1,0:T(8,128)S(1)} %collective-permute-done.refs_1_, f32[1,256,256]{2,1,0:T(8,128)S(1)} %get-tuple-element.40.refs_2_.refs_5_, f32[1,128,128]{2,1,0:T(8,128)S(1)} %get-tuple-element.43.refs_3_, ...), custom_call_target="tpu_custom_call" | custom-call | flops 1000 | bytes 1000 | tf_op jit(solution)/shard_map/pair_kernel/pallas_call | solution.py:50
  13.2 0.0 collective-permute-done.2.refs_1_.refs_2_
  13.2 0.3 collective-permute-start.4
  13.5 1.4 %collective-permute-start.1 = (f32[128,128]{1,0:T(8,128)S(1)}, f32[128,128]{1,0:T(8,128)S(1)}, u32[]{:S(2)}, u32[]{:S(2)}) collective-permute-start(f32[128,128]{1,0:T(8,128)S(1)} %get-tuple-element.46.refs_0_.refs_8_), channel_id=1, source_target_pairs={{0,2},{1,3},{2,0},{3,1},{4,6},{5,7},{6,4},{7,5},{8,10},{9,11},{10,... | collective-permute-start | bytes 196616 | tf_op jit(solution)/shard_map/ppermute | solution.py:292
  14.9 0.4 top_kernel.1.refs_0_
  15.2 0.0 collective-permute-done.6.refs_1_
  15.4 1.5 %collective-permute-start.13 = (f32[2,128,128]{2,1,0:T(8,128)S(1)}, f32[2,128,128]{2,1,0:T(8,128)S(1)}, u32[]{:S(2)}, u32[]{:S(2)}) collective-permute-start(f32[2,128,128]{2,1,0:T(8,128)S(1)} %top_kernel.1.refs_0_), channel_id=1, source_target_pairs={{0,4},{1,9},{2,6},{3,11},{4,0},{5,13},{6,2},{7,15},{8,12},{9,1},{1... | collective-permute-start | bytes 393224 | tf_op jit(solution)/shard_map/ppermute | solution.py:292
  17.0 0.6 %collective-permute-start.9 = (f32[2,128,128]{2,1,0:T(8,128)S(1)}, f32[2,128,128]{2,1,0:T(8,128)S(1)}, u32[]{:S(2)}, u32[]{:S(2)}) collective-permute-start(f32[2,128,128]{2,1,0:T(8,128)S(1)} %kernel.36), channel_id=1, source_target_pairs={{0,4},{1,3},{2,6},{3,1},{4,0},{5,7},{6,2},{7,5},{8,12},{9,11},{10,... | collective-permute-start | bytes 393224 | tf_op jit(solution)/shard_map/ppermute | solution.py:292
  17.6 1.5 %collective-permute-start.7 = (f32[3,128,128]{2,1,0:T(8,128)S(1)}, f32[3,128,128]{2,1,0:T(8,128)S(1)}, u32[]{:S(2)}, u32[]{:S(2)}) collective-permute-start(f32[3,128,128]{2,1,0:T(8,128)S(1)} %kernel.31), channel_id=1, source_target_pairs={{0,4},{1,3},{2,6},{3,1},{4,0},{5,7},{6,2},{7,5},{8,12},{9,11},{10,... | collective-permute-start | bytes 589832 | tf_op jit(solution)/shard_map/ppermute | solution.py:292
  19.2 0.0 collective-permute-done.4.refs_1_
  19.2 0.0 collective-permute-start.3
  19.2 0.0 collective-permute-done.1.refs_1_.refs_9_
  19.2 0.3 level_kernel.3.refs_0_.refs_11_
  19.5 2.6 %collective-permute-done.9.refs_1_ = f32[2,128,128]{2,1,0:T(8,128)S(1)} collective-permute-done((f32[2,128,128]{2,1,0:T(8,128)S(1)}, f32[2,128,128]{2,1,0:T(8,128)S(1)}, u32[]{:S(2)}, u32[]{:S(2)}) %collective-permute-start.9) | collective-permute-done | bytes 131104 | tf_op jit(solution)/shard_map/ppermute | solution.py:292
  22.1 1.4 %collective-permute-start.5 = (f32[128,128]{1,0:T(8,128)S(1)}, f32[128,128]{1,0:T(8,128)S(1)}, u32[]{:S(2)}, u32[]{:S(2)}) collective-permute-start(f32[128,128]{1,0:T(8,128)S(1)} %level_kernel.3.refs_0_.refs_11_), channel_id=1, source_target_pairs={{0,4},{1,5},{2,6},{3,7},{4,0},{5,1},{6,2},{7,3},{8,12},{9,13},{10,... | collective-permute-start | bytes 196616 | tf_op jit(solution)/shard_map/ppermute | solution.py:292
  23.5 0.0 collective-permute-done.13.refs_1_
  23.5 0.1 collective-permute-start.10
  23.6 0.7 %collective-permute-start.14 = (f32[2,128,128]{2,1,0:T(8,128)S(1)}, f32[2,128,128]{2,1,0:T(8,128)S(1)}, u32[]{:S(2)}, u32[]{:S(2)}) collective-permute-start(f32[2,128,128]{2,1,0:T(8,128)S(1)} %kernel.42), channel_id=1, source_target_pairs={{0,2},{1,5},{2,0},{3,7},{4,6},{5,1},{6,4},{7,3},{8,10},{9,13},{10,... | collective-permute-start | bytes 393224 | tf_op jit(solution)/shard_map/ppermute | solution.py:292
  24.3 0.0 collective-permute-done.7.refs_1_
  24.4 1.4 %collective-permute-start.12 = (f32[3,128,128]{2,1,0:T(8,128)S(1)}, f32[3,128,128]{2,1,0:T(8,128)S(1)}, u32[]{:S(2)}, u32[]{:S(2)}) collective-permute-start(f32[3,128,128]{2,1,0:T(8,128)S(1)} %kernel.39.refs_0_), channel_id=1, source_target_pairs={{0,2},{1,5},{2,0},{3,7},{4,6},{5,1},{6,4},{7,3},{8,10},{9,13},{10,... | collective-permute-start | bytes 589832 | tf_op jit(solution)/shard_map/ppermute | solution.py:292
  25.8 0.0 collective-permute-done.3.refs_1_
  25.8 0.0 collective-permute-start.8
  25.9 0.0 collective-permute-done.10.refs_1_
  25.9 0.5 %collective-permute-done.5.refs_1_.refs_12_ = f32[128,128]{1,0:T(8,128)S(1)} collective-permute-done((f32[128,128]{1,0:T(8,128)S(1)}, f32[128,128]{1,0:T(8,128)S(1)}, u32[]{:S(2)}, u32[]{:S(2)}) %collective-permute-start.5) | collective-permute-done | bytes 65568 | tf_op jit(solution)/shard_map/ppermute | solution.py:292
  26.4 0.3 level_kernel.4.refs_0_.refs_14_
  26.7 1.7 %collective-permute-start.11 = (f32[128,128]{1,0:T(8,128)S(1)}, f32[128,128]{1,0:T(8,128)S(1)}, u32[]{:S(2)}, u32[]{:S(2)}) collective-permute-start(f32[128,128]{1,0:T(8,128)S(1)} %level_kernel.4.refs_0_.refs_14_), channel_id=1, source_target_pairs={{0,8},{1,9},{2,10},{3,11},{4,12},{5,13},{6,14},{7,15},{8,0},{9,1},... | collective-permute-start | bytes 196616 | tf_op jit(solution)/shard_map/ppermute | solution.py:292
  28.3 0.3 collective-permute-done.14.refs_1_
  28.7 0.1 collective-permute-start.15
  28.8 0.8 %collective-permute-start.18 = (f32[2,128,128]{2,1,0:T(8,128)S(1)}, f32[2,128,128]{2,1,0:T(8,128)S(1)}, u32[]{:S(2)}, u32[]{:S(2)}) collective-permute-start(f32[2,128,128]{2,1,0:T(8,128)S(1)} %kernel.47.refs_0_), channel_id=1, source_target_pairs={{0,4},{1,3},{2,6},{3,1},{4,0},{5,7},{6,2},{7,5},{8,12},{9,11},{10,... | collective-permute-start | bytes 393224 | tf_op jit(solution)/shard_map/ppermute | solution.py:292
  29.6 0.0 collective-permute-done.8.refs_1_
  29.6 0.5 %collective-permute-done.15.refs_1_ = f32[2,128,128]{2,1,0:T(8,128)S(1)} collective-permute-done((f32[2,128,128]{2,1,0:T(8,128)S(1)}, f32[2,128,128]{2,1,0:T(8,128)S(1)}, u32[]{:S(2)}, u32[]{:S(2)}) %collective-permute-start.15) | collective-permute-done | bytes 131104 | tf_op jit(solution)/shard_map/ppermute | solution.py:285
  30.1 0.9 %collective-permute-done.11.refs_1_.refs_15_ = f32[128,128]{1,0:T(8,128)S(1)} collective-permute-done((f32[128,128]{1,0:T(8,128)S(1)}, f32[128,128]{1,0:T(8,128)S(1)}, u32[]{:S(2)}, u32[]{:S(2)}) %collective-permute-start.11) | collective-permute-done | bytes 65568 | tf_op jit(solution)/shard_map/ppermute | solution.py:292
  31.0 0.3 level_kernel.5.refs_0_.refs_17_.own_ref
  31.3 2.2 %collective-permute-start.17 = (f32[128,128]{1,0:T(8,128)S(1)}, f32[128,128]{1,0:T(8,128)S(1)}, u32[]{:S(2)}, u32[]{:S(2)}) collective-permute-start(f32[128,128]{1,0:T(8,128)S(1)} %level_kernel.5.refs_0_.refs_17_.own_ref), channel_id=1, source_target_pairs={{0,16},{1,17},{2,18},{3,19},{4,20},{5,21},{6,22},{7,23},{8,24},{9,... | collective-permute-start | bytes 196616 | tf_op jit(solution)/shard_map/ppermute | solution.py:292
  33.5 0.3 collective-permute-done.18.refs_1_
  33.8 0.1 collective-permute-start.19
  33.9 0.0 collective-permute-done.12.refs_1_
  34.0 0.5 %collective-permute-start.16 = (f32[3,128,128]{2,1,0:T(8,128)S(1)}, f32[3,128,128]{2,1,0:T(8,128)S(1)}, u32[]{:S(2)}, u32[]{:S(2)}) collective-permute-start(f32[3,128,128]{2,1,0:T(8,128)S(1)} %kernel.45.refs_0_), channel_id=1, source_target_pairs={{0,1},{1,0},{2,3},{3,2},{4,5},{5,4},{6,7},{7,6},{8,9},{9,8},{10,11... | collective-permute-start | bytes 589832 | tf_op jit(solution)/shard_map/ppermute | solution.py:285
  34.5 1.1 %collective-permute-done.16.refs_1_ = f32[3,128,128]{2,1,0:T(8,128)S(1)} collective-permute-done((f32[3,128,128]{2,1,0:T(8,128)S(1)}, f32[3,128,128]{2,1,0:T(8,128)S(1)}, u32[]{:S(2)}, u32[]{:S(2)}) %collective-permute-start.16) | collective-permute-done | bytes 196640 | tf_op jit(solution)/shard_map/ppermute | solution.py:285
  35.6 2.0 %fold_kernel.1 = (f32[1024,128]{1,0:T(8,128)S(1)}, f32[1024,128]{1,0:T(8,128)S(1)}) custom-call(f32[1024,128]{1,0:T(8,128)S(1)} %get-tuple-element.35.refs_5_.refs_0_, f32[1024,128]{1,0:T(8,128)S(1)} %get-tuple-element.36.refs_1_, f32[1,256,256]{2,1,0:T(8,128)S(1)} %get-tuple-element.37.refs_2_, f32[1,128,128]{2,1,0:T(8,128)S(1)} %get-tuple-element.38.refs_3_, ...), custom_call_target="tpu_custom_call" | custom-call | flops 2000000000 | bytes 1000 | tf_op jit(solution)/shard_map/fold_kernel/pallas_call | solution.py:50
  37.6 1.5 %shard_map.163 = f32[1024,128]{1,0:T(8,128)} custom-call(f32[1024,128]{1,0:T(8,128)S(1)} %get-tuple-element.56.base_ref, f32[1024,128]{1,0:T(8,128)S(1)} %get-tuple-element.57.refs_2_.weight_ref, f32[128,128]{1,0:T(8,128)S(1)} %level_kernel.5.refs_0_.refs_17_.own_ref, f32[128,128]{1,0:T(8,128)S(1)} %collective-permute-done.17.other_ref, ...), custom_call_target="tpu_custom_call" | custom-call | tf_op jit(solution)/shard_map/pallas_call | solution.py:425
  (30 shorter events, 0.5 us)
Async XLA Ops:
  1.6 11.6 %collective-permute-start.2 = (f32[5,128,128]{2,1,0:T(8,128)S(1)}, f32[5,128,128]{2,1,0:T(8,128)S(1)}, u32[]{:S(2)}, u32[]{:S(2)}) collective-permute-start(f32[5,128,128]{2,1,0:T(8,128)S(1)} %get-tuple-element.48.refs_0_), channel_id=1, source_target_pairs={{0,2},{1,17},{2,0},{3,19},{4,6},{5,21},{6,4},{7,23},{8,10},{9,25},... | collective-permute-start | bytes 983048 | tf_op jit(solution)/shard_map/ppermute | solution.py:292
  4.6 10.7 %collective-permute-start.6 = (f32[5,128,128]{2,1,0:T(8,128)S(1)}, f32[5,128,128]{2,1,0:T(8,128)S(1)}, u32[]{:S(2)}, u32[]{:S(2)}) collective-permute-start(f32[5,128,128]{2,1,0:T(8,128)S(1)} %get-tuple-element.48.refs_0_), channel_id=1, source_target_pairs={{0,8},{1,5},{2,10},{3,7},{4,12},{5,1},{6,14},{7,3},{8,0},{9,13},{1... | collective-permute-start | bytes 983048 | tf_op jit(solution)/shard_map/ppermute | solution.py:292
  10.8 1.8 %collective-permute-start = (f32[128,128]{1,0:T(8,128)S(1)}, f32[128,128]{1,0:T(8,128)S(1)}, u32[]{:S(2)}, u32[]{:S(2)}) collective-permute-start(f32[128,128]{1,0:T(8,128)S(1)} %get-tuple-element.42.refs_0_), channel_id=1, source_target_pairs={{0,1},{1,0},{2,3},{3,2},{4,5},{5,4},{6,7},{7,6},{8,9},{9,8},{10,11... | collective-permute-start | bytes 196616 | tf_op jit(solution)/shard_map/ppermute | solution.py:285
  13.2 5.9 %collective-permute-start.4 = (f32[2,128,128]{2,1,0:T(8,128)S(1)}, f32[2,128,128]{2,1,0:T(8,128)S(1)}, u32[]{:S(2)}, u32[]{:S(2)}) collective-permute-start(f32[2,128,128]{2,1,0:T(8,128)S(1)} %kernel.27.refs_0_), channel_id=1, source_target_pairs={{0,1},{1,0},{2,3},{3,2},{4,5},{5,4},{6,7},{7,6},{8,9},{9,8},{10,11... | collective-permute-start | bytes 393224 | tf_op jit(solution)/shard_map/ppermute | solution.py:285
  13.5 5.7 %collective-permute-start.1 = (f32[128,128]{1,0:T(8,128)S(1)}, f32[128,128]{1,0:T(8,128)S(1)}, u32[]{:S(2)}, u32[]{:S(2)}) collective-permute-start(f32[128,128]{1,0:T(8,128)S(1)} %get-tuple-element.46.refs_0_.refs_8_), channel_id=1, source_target_pairs={{0,2},{1,3},{2,0},{3,1},{4,6},{5,7},{6,4},{7,5},{8,10},{9,11},{10,... | collective-permute-start | bytes 196616 | tf_op jit(solution)/shard_map/ppermute | solution.py:292
  15.4 8.0 %collective-permute-start.13 = (f32[2,128,128]{2,1,0:T(8,128)S(1)}, f32[2,128,128]{2,1,0:T(8,128)S(1)}, u32[]{:S(2)}, u32[]{:S(2)}) collective-permute-start(f32[2,128,128]{2,1,0:T(8,128)S(1)} %top_kernel.1.refs_0_), channel_id=1, source_target_pairs={{0,4},{1,9},{2,6},{3,11},{4,0},{5,13},{6,2},{7,15},{8,12},{9,1},{1... | collective-permute-start | bytes 393224 | tf_op jit(solution)/shard_map/ppermute | solution.py:292
  17.0 5.0 %collective-permute-start.9 = (f32[2,128,128]{2,1,0:T(8,128)S(1)}, f32[2,128,128]{2,1,0:T(8,128)S(1)}, u32[]{:S(2)}, u32[]{:S(2)}) collective-permute-start(f32[2,128,128]{2,1,0:T(8,128)S(1)} %kernel.36), channel_id=1, source_target_pairs={{0,4},{1,3},{2,6},{3,1},{4,0},{5,7},{6,2},{7,5},{8,12},{9,11},{10,... | collective-permute-start | bytes 393224 | tf_op jit(solution)/shard_map/ppermute | solution.py:292
  17.6 6.7 %collective-permute-start.7 = (f32[3,128,128]{2,1,0:T(8,128)S(1)}, f32[3,128,128]{2,1,0:T(8,128)S(1)}, u32[]{:S(2)}, u32[]{:S(2)}) collective-permute-start(f32[3,128,128]{2,1,0:T(8,128)S(1)} %kernel.31), channel_id=1, source_target_pairs={{0,4},{1,3},{2,6},{3,1},{4,0},{5,7},{6,2},{7,5},{8,12},{9,11},{10,... | collective-permute-start | bytes 589832 | tf_op jit(solution)/shard_map/ppermute | solution.py:292
  19.2 6.7 %collective-permute-start.3 = (f32[3,128,128]{2,1,0:T(8,128)S(1)}, f32[3,128,128]{2,1,0:T(8,128)S(1)}, u32[]{:S(2)}, u32[]{:S(2)}) collective-permute-start(f32[3,128,128]{2,1,0:T(8,128)S(1)} %kernel.25.refs_0_), channel_id=1, source_target_pairs={{0,1},{1,0},{2,3},{3,2},{4,5},{5,4},{6,7},{7,6},{8,9},{9,8},{10,11... | collective-permute-start | bytes 589832 | tf_op jit(solution)/shard_map/ppermute | solution.py:285
  22.1 4.3 %collective-permute-start.5 = (f32[128,128]{1,0:T(8,128)S(1)}, f32[128,128]{1,0:T(8,128)S(1)}, u32[]{:S(2)}, u32[]{:S(2)}) collective-permute-start(f32[128,128]{1,0:T(8,128)S(1)} %level_kernel.3.refs_0_.refs_11_), channel_id=1, source_target_pairs={{0,4},{1,5},{2,6},{3,7},{4,0},{5,1},{6,2},{7,3},{8,12},{9,13},{10,... | collective-permute-start | bytes 196616 | tf_op jit(solution)/shard_map/ppermute | solution.py:292
  23.5 2.4 %collective-permute-start.10 = (f32[2,128,128]{2,1,0:T(8,128)S(1)}, f32[2,128,128]{2,1,0:T(8,128)S(1)}, u32[]{:S(2)}, u32[]{:S(2)}) collective-permute-start(f32[2,128,128]{2,1,0:T(8,128)S(1)} %kernel.37.refs_0_), channel_id=1, source_target_pairs={{0,1},{1,0},{2,3},{3,2},{4,5},{5,4},{6,7},{7,6},{8,9},{9,8},{10,11... | collective-permute-start | bytes 393224 | tf_op jit(solution)/shard_map/ppermute | solution.py:285
  23.6 5.0 %collective-permute-start.14 = (f32[2,128,128]{2,1,0:T(8,128)S(1)}, f32[2,128,128]{2,1,0:T(8,128)S(1)}, u32[]{:S(2)}, u32[]{:S(2)}) collective-permute-start(f32[2,128,128]{2,1,0:T(8,128)S(1)} %kernel.42), channel_id=1, source_target_pairs={{0,2},{1,5},{2,0},{3,7},{4,6},{5,1},{6,4},{7,3},{8,10},{9,13},{10,... | collective-permute-start | bytes 393224 | tf_op jit(solution)/shard_map/ppermute | solution.py:292
  24.4 9.5 %collective-permute-start.12 = (f32[3,128,128]{2,1,0:T(8,128)S(1)}, f32[3,128,128]{2,1,0:T(8,128)S(1)}, u32[]{:S(2)}, u32[]{:S(2)}) collective-permute-start(f32[3,128,128]{2,1,0:T(8,128)S(1)} %kernel.39.refs_0_), channel_id=1, source_target_pairs={{0,2},{1,5},{2,0},{3,7},{4,6},{5,1},{6,4},{7,3},{8,10},{9,13},{10,... | collective-permute-start | bytes 589832 | tf_op jit(solution)/shard_map/ppermute | solution.py:292
  25.8 3.7 %collective-permute-start.8 = (f32[3,128,128]{2,1,0:T(8,128)S(1)}, f32[3,128,128]{2,1,0:T(8,128)S(1)}, u32[]{:S(2)}, u32[]{:S(2)}) collective-permute-start(f32[3,128,128]{2,1,0:T(8,128)S(1)} %kernel.32.refs_0_), channel_id=1, source_target_pairs={{0,1},{1,0},{2,3},{3,2},{4,5},{5,4},{6,7},{7,6},{8,9},{9,8},{10,11... | collective-permute-start | bytes 589832 | tf_op jit(solution)/shard_map/ppermute | solution.py:285
  26.7 4.3 %collective-permute-start.11 = (f32[128,128]{1,0:T(8,128)S(1)}, f32[128,128]{1,0:T(8,128)S(1)}, u32[]{:S(2)}, u32[]{:S(2)}) collective-permute-start(f32[128,128]{1,0:T(8,128)S(1)} %level_kernel.4.refs_0_.refs_14_), channel_id=1, source_target_pairs={{0,8},{1,9},{2,10},{3,11},{4,12},{5,13},{6,14},{7,15},{8,0},{9,1},... | collective-permute-start | bytes 196616 | tf_op jit(solution)/shard_map/ppermute | solution.py:292
  28.7 1.4 %collective-permute-start.15 = (f32[2,128,128]{2,1,0:T(8,128)S(1)}, f32[2,128,128]{2,1,0:T(8,128)S(1)}, u32[]{:S(2)}, u32[]{:S(2)}) collective-permute-start(f32[2,128,128]{2,1,0:T(8,128)S(1)} %kernel.43.refs_0_), channel_id=1, source_target_pairs={{0,1},{1,0},{2,3},{3,2},{4,5},{5,4},{6,7},{7,6},{8,9},{9,8},{10,11... | collective-permute-start | bytes 393224 | tf_op jit(solution)/shard_map/ppermute | solution.py:285
  28.8 5.0 %collective-permute-start.18 = (f32[2,128,128]{2,1,0:T(8,128)S(1)}, f32[2,128,128]{2,1,0:T(8,128)S(1)}, u32[]{:S(2)}, u32[]{:S(2)}) collective-permute-start(f32[2,128,128]{2,1,0:T(8,128)S(1)} %kernel.47.refs_0_), channel_id=1, source_target_pairs={{0,4},{1,3},{2,6},{3,1},{4,0},{5,7},{6,2},{7,5},{8,12},{9,11},{10,... | collective-permute-start | bytes 393224 | tf_op jit(solution)/shard_map/ppermute | solution.py:292
  31.3 6.4 %collective-permute-start.17 = (f32[128,128]{1,0:T(8,128)S(1)}, f32[128,128]{1,0:T(8,128)S(1)}, u32[]{:S(2)}, u32[]{:S(2)}) collective-permute-start(f32[128,128]{1,0:T(8,128)S(1)} %level_kernel.5.refs_0_.refs_17_.own_ref), channel_id=1, source_target_pairs={{0,16},{1,17},{2,18},{3,19},{4,20},{5,21},{6,22},{7,23},{8,24},{9,... | collective-permute-start | bytes 196616 | tf_op jit(solution)/shard_map/ppermute | solution.py:292
  33.8 3.8 %collective-permute-start.19 = (f32[2,128,128]{2,1,0:T(8,128)S(1)}, f32[2,128,128]{2,1,0:T(8,128)S(1)}, u32[]{:S(2)}, u32[]{:S(2)}) collective-permute-start(f32[2,128,128]{2,1,0:T(8,128)S(1)} %kernel.48.refs_0_), channel_id=1, source_target_pairs={{0,1},{1,0},{2,3},{3,2},{4,5},{5,4},{6,7},{7,6},{8,9},{9,8},{10,11... | collective-permute-start | bytes 393224 | tf_op jit(solution)/shard_map/ppermute | solution.py:285
  34.0 1.6 %collective-permute-start.16 = (f32[3,128,128]{2,1,0:T(8,128)S(1)}, f32[3,128,128]{2,1,0:T(8,128)S(1)}, u32[]{:S(2)}, u32[]{:S(2)}) collective-permute-start(f32[3,128,128]{2,1,0:T(8,128)S(1)} %kernel.45.refs_0_), channel_id=1, source_target_pairs={{0,1},{1,0},{2,3},{3,2},{4,5},{5,4},{6,7},{7,6},{8,9},{9,8},{10,11... | collective-permute-start | bytes 589832 | tf_op jit(solution)/shard_map/ppermute | solution.py:285

commit v5 on v4

--- a/solution.py
+++ b/solution.py
@@ -25,6 +25,12 @@
     left_high, left_low = left if isinstance(left, tuple) else split(left)
     right_high, right_low = right if isinstance(right, tuple) else split(right)
     dot = functools.partial(lax.dot_general, dimension_numbers=dims, preferred_element_type=F32)
+    if left_high.shape[0] <= right_high.shape[1 - dims[0][1][0]]:
+        axis = dims[0][1][0]
+        return dot(
+            jnp.concatenate([left_high, left_high, left_low], axis=1),
+            jnp.concatenate([right_high, right_low, right_high], axis=axis),
+        )
     return dot(left_high, right_high) + (dot(left_high, right_low) + dot(left_low, right_high))
 
 
@@ -149,17 +155,18 @@
     sources += [mid_q, mid_e, mid_f]
     targets += [mid_q_v, mid_e_v, mid_f_v]
     copies = fetch(sources, targets, sems)
-    ahead = fetch(
-        [pair_q, pair_e, pair_f, pair_g, mid_g, g],
-        [pair_q_v, pair_e_v, pair_f_v, pair_g_v, mid_g_v, g_v],
-        later,
-    )
     reduced = []
     count = e.shape[1]
     for n in range(leaves):
         copies[4 * n].wait()
         block = rhs_v[n * size : (n + 1) * size, :].T
         copies[4 * n + 1].wait()
+        if n == 0:
+            ahead = fetch(
+                [pair_q, pair_e, pair_f, pair_g, mid_g, g],
+                [pair_q_v, pair_e_v, pair_f_v, pair_g_v, mid_g_v, g_v],
+                later,
+            )
         c = mm(block, q_v[n])
         copies[4 * n + 2].wait()
         y = mt(c[:, :count], e_v[n])

time: 39.3 us -> 38.8 us (0.987)
  Pallas kernels: 13.3 us -> 12.5 us
  waiting for transfers between devices: 6.24 us -> 6.88 us
  starting transfers between devices: 19.2 us -> 18.8 us
    ppermute x12, waiting for transfers between devices: 4.66 us -> 5.31 us  [across(): return lax.ppermute(value, ('leaf', 'panel'), pairs)]
    pallas_call x37, Pallas kernels: 11.8 us -> 11.2 us  [call(): pl.pallas_call(body, name=getattr(kernel, 'func', kernel).__name__, out_s...]
    ppermute x12, starting transfers between devices: 17.8 us -> 17.3 us  [across(): return lax.ppermute(value, ('leaf', 'panel'), pairs)]
  transfers between devices with their start and end apart: 20 -> 20, of which waited for: 7 -> 8; matrix products, arithmetic and copies ran while one was open for 0% -> 0% of each run, Pallas kernels for 26% -> 25%
where the time goes in v5:
time: 38.8 us; the launch traced here: 38.6 us
  starting transfers between devices  18.8 us (48%)
  Pallas kernels  12.5 us (32%)
  waiting for transfers between devices  6.88 us (18%)
    ppermute x12, starting transfers between devices, across(): return lax.ppermute(value, ('leaf', 'panel'), pairs)  17.3 us
    pallas_call x37, Pallas kernels, call(): pl.pallas_call(body, name=getattr(kernel, 'func', kernel).__name__, out_s...  11.2 us
    ppermute x12, waiting for transfers between devices, across(): return lax.ppermute(value, ('leaf', 'panel'), pairs)  5.31 us
    ppermute x8, waiting for transfers between devices, swap_cores(): lax.ppermute(value, 'panel', [(i, cores - 1 - i) for i in range(cores)])  1.58 us
    ppermute x8, starting transfers between devices, swap_cores(): lax.ppermute(value, 'panel', [(i, cores - 1 - i) for i in range(cores)])  1.49 us
    pallas_call x1, Pallas kernels, last_step(): pl.pallas_call(kernel, out_shape=jax.ShapeDtypeStruct(shape, F32), in_spe...  1.31 us
  transfers between devices with their start and end apart: 20, of which 8 were waited for; matrix products, arithmetic and copies ran while one was open for 0% of the time, Pallas kernels for 25%

profile of v5, /device:TPU:0, one launch (start us, length us, event | category | flops | bytes accessed | tf_op | source)
XLA Modules:
  0.0 38.6 jit_solution(16480588452384541707)
XLA Ops:
  0.0 1.5 %node_kernel.1 = (f32[5,128,128]{2,1,0:T(8,128)S(1)}, f32[5,128,128]{2,1,0:T(8,128)S(1)}) custom-call(f32[1,256,256]{2,1,0:T(8,128)} %refs_0_.3, f32[1,128,128]{2,1,0:T(8,128)} %refs_1_.3, f32[1,128,128]{2,1,0:T(8,128)} %refs_2_.3, f32[1,128,128]{2,1,0:T(8,128)} %refs_3_.3), custom_call_target="tpu_custom_call" | custom-call | tf_op jit(solution)/shard_map/node_kernel/pallas_call | solution.py:56
  1.5 3.0 %collective-permute-start.2 = (f32[5,128,128]{2,1,0:T(8,128)S(1)}, f32[5,128,128]{2,1,0:T(8,128)S(1)}, u32[]{:S(2)}, u32[]{:S(2)}) collective-permute-start(f32[5,128,128]{2,1,0:T(8,128)S(1)} %get-tuple-element.48.refs_0_), channel_id=1, source_target_pairs={{0,2},{1,17},{2,0},{3,19},{4,6},{5,21},{6,4},{7,23},{8,10},{9,25},... | collective-permute-start | bytes 983048 | tf_op jit(solution)/shard_map/ppermute | solution.py:299
  4.5 1.6 %collective-permute-start.6 = (f32[5,128,128]{2,1,0:T(8,128)S(1)}, f32[5,128,128]{2,1,0:T(8,128)S(1)}, u32[]{:S(2)}, u32[]{:S(2)}) collective-permute-start(f32[5,128,128]{2,1,0:T(8,128)S(1)} %get-tuple-element.48.refs_0_), channel_id=1, source_target_pairs={{0,8},{1,5},{2,10},{3,7},{4,12},{5,1},{6,14},{7,3},{8,0},{9,13},{1... | collective-permute-start | bytes 983048 | tf_op jit(solution)/shard_map/ppermute | solution.py:299
  6.1 4.5 %leaf_kernel.1 = (f32[2,128,384]{2,1,0:T(8,128)S(1)}, f32[128,128]{1,0:T(8,128)S(1)}, f32[128,128]{1,0:T(8,128)S(1)}, f32[2,512,512]{2,1,0:T(8,128)S(1)}, f32[2,...) custom-call(f32[1024,128]{1,0:T(8,128)} %refs_0_.2, ...), custom_call_target="tpu_custom_call" | custom-call | flops 1000 | bytes 1000 | tf_op jit(solution)/shard_map/leaf_kernel/pallas_call | solution.py:56
  10.6 0.4 collective-permute-start
  11.0 1.4 %leaf_maps_kernel.1 = (f32[1024,128]{1,0:T(8,128)S(1)}, f32[1024,128]{1,0:T(8,128)S(1)}) custom-call(f32[2,512,512]{2,1,0:T(8,128)S(1)} %get-tuple-element.32.refs_0_, f32[2,384,128]{2,1,0:T(8,128)S(1)} %get-tuple-element.33.refs_1_, f32[2,128,384]{2,1,0:T(8,128)S(1)} %get-tuple-element.34.refs_2_), custom_call_target="tpu_custom_call" | custom-call | flops 1000000000 | bytes 1000 | tf_op jit(solution)/shard_map/leaf_maps_kernel/pallas_call | solution.py:56
  12.4 0.0 collective-permute-done.refs_1_
  12.4 0.5 %pair_kernel.1 = (f32[128,128]{1,0:T(8,128)S(1)}, f32[128,128]{1,0:T(8,128)S(1)}) custom-call(f32[128,128]{1,0:T(8,128)S(1)} %get-tuple-element.42.refs_0_, f32[128,128]{1,0:T(8,128)S(1)} %collective-permute-done.refs_1_, f32[1,256,256]{2,1,0:T(8,128)S(1)} %get-tuple-element.40.refs_2_.refs_5_, f32[1,128,128]{2,1,0:T(8,128)S(1)} %get-tuple-element.43.refs_3_, ...), custom_call_target="tpu_custom_call" | custom-call | flops 1000 | bytes 1000 | tf_op jit(solution)/shard_map/pair_kernel/pallas_call | solution.py:56
  12.9 0.0 collective-permute-done.2.refs_1_.refs_2_
  13.0 0.4 collective-permute-start.4
  13.3 1.4 %collective-permute-start.1 = (f32[128,128]{1,0:T(8,128)S(1)}, f32[128,128]{1,0:T(8,128)S(1)}, u32[]{:S(2)}, u32[]{:S(2)}) collective-permute-start(f32[128,128]{1,0:T(8,128)S(1)} %get-tuple-element.46.refs_0_.refs_8_), channel_id=1, source_target_pairs={{0,2},{1,3},{2,0},{3,1},{4,6},{5,7},{6,4},{7,5},{8,10},{9,11},{10,... | collective-permute-start | bytes 196616 | tf_op jit(solution)/shard_map/ppermute | solution.py:299
  14.8 0.3 top_kernel.1.refs_0_
  15.1 0.0 collective-permute-done.6.refs_1_
  15.3 1.6 %collective-permute-start.13 = (f32[2,128,128]{2,1,0:T(8,128)S(1)}, f32[2,128,128]{2,1,0:T(8,128)S(1)}, u32[]{:S(2)}, u32[]{:S(2)}) collective-permute-start(f32[2,128,128]{2,1,0:T(8,128)S(1)} %top_kernel.1.refs_0_), channel_id=1, source_target_pairs={{0,4},{1,9},{2,6},{3,11},{4,0},{5,13},{6,2},{7,15},{8,12},{9,1},{1... | collective-permute-start | bytes 393224 | tf_op jit(solution)/shard_map/ppermute | solution.py:299
  16.9 0.6 %collective-permute-start.9 = (f32[2,128,128]{2,1,0:T(8,128)S(1)}, f32[2,128,128]{2,1,0:T(8,128)S(1)}, u32[]{:S(2)}, u32[]{:S(2)}) collective-permute-start(f32[2,128,128]{2,1,0:T(8,128)S(1)} %kernel.36), channel_id=1, source_target_pairs={{0,4},{1,3},{2,6},{3,1},{4,0},{5,7},{6,2},{7,5},{8,12},{9,11},{10,... | collective-permute-start | bytes 393224 | tf_op jit(solution)/shard_map/ppermute | solution.py:299
  17.5 1.6 %collective-permute-start.7 = (f32[3,128,128]{2,1,0:T(8,128)S(1)}, f32[3,128,128]{2,1,0:T(8,128)S(1)}, u32[]{:S(2)}, u32[]{:S(2)}) collective-permute-start(f32[3,128,128]{2,1,0:T(8,128)S(1)} %kernel.31), channel_id=1, source_target_pairs={{0,4},{1,3},{2,6},{3,1},{4,0},{5,7},{6,2},{7,5},{8,12},{9,11},{10,... | collective-permute-start | bytes 589832 | tf_op jit(solution)/shard_map/ppermute | solution.py:299
  19.1 0.0 collective-permute-done.4.refs_1_
  19.1 0.0 collective-permute-start.3
  19.1 0.0 collective-permute-done.1.refs_1_.refs_9_
  19.1 0.2 level_kernel.3.refs_0_.refs_11_
  19.4 2.6 %collective-permute-done.9.refs_1_ = f32[2,128,128]{2,1,0:T(8,128)S(1)} collective-permute-done((f32[2,128,128]{2,1,0:T(8,128)S(1)}, f32[2,128,128]{2,1,0:T(8,128)S(1)}, u32[]{:S(2)}, u32[]{:S(2)}) %collective-permute-start.9) | collective-permute-done | bytes 131104 | tf_op jit(solution)/shard_map/ppermute | solution.py:299
  22.0 1.4 %collective-permute-start.5 = (f32[128,128]{1,0:T(8,128)S(1)}, f32[128,128]{1,0:T(8,128)S(1)}, u32[]{:S(2)}, u32[]{:S(2)}) collective-permute-start(f32[128,128]{1,0:T(8,128)S(1)} %level_kernel.3.refs_0_.refs_11_), channel_id=1, source_target_pairs={{0,4},{1,5},{2,6},{3,7},{4,0},{5,1},{6,2},{7,3},{8,12},{9,13},{10,... | collective-permute-start | bytes 196616 | tf_op jit(solution)/shard_map/ppermute | solution.py:299
  23.4 0.0 collective-permute-done.13.refs_1_
  23.4 0.1 collective-permute-start.10
  23.5 0.7 %collective-permute-start.14 = (f32[2,128,128]{2,1,0:T(8,128)S(1)}, f32[2,128,128]{2,1,0:T(8,128)S(1)}, u32[]{:S(2)}, u32[]{:S(2)}) collective-permute-start(f32[2,128,128]{2,1,0:T(8,128)S(1)} %kernel.42), channel_id=1, source_target_pairs={{0,2},{1,5},{2,0},{3,7},{4,6},{5,1},{6,4},{7,3},{8,10},{9,13},{10,... | collective-permute-start | bytes 393224 | tf_op jit(solution)/shard_map/ppermute | solution.py:299
  24.2 0.2 collective-permute-done.7.refs_1_
  24.5 1.2 %collective-permute-start.12 = (f32[3,128,128]{2,1,0:T(8,128)S(1)}, f32[3,128,128]{2,1,0:T(8,128)S(1)}, u32[]{:S(2)}, u32[]{:S(2)}) collective-permute-start(f32[3,128,128]{2,1,0:T(8,128)S(1)} %kernel.39.refs_0_), channel_id=1, source_target_pairs={{0,2},{1,5},{2,0},{3,7},{4,6},{5,1},{6,4},{7,3},{8,10},{9,13},{10,... | collective-permute-start | bytes 589832 | tf_op jit(solution)/shard_map/ppermute | solution.py:299
  25.7 0.0 collective-permute-done.3.refs_1_
  25.7 0.0 collective-permute-start.8
  25.8 0.0 collective-permute-done.10.refs_1_
  25.8 0.5 %collective-permute-done.5.refs_1_.refs_12_ = f32[128,128]{1,0:T(8,128)S(1)} collective-permute-done((f32[128,128]{1,0:T(8,128)S(1)}, f32[128,128]{1,0:T(8,128)S(1)}, u32[]{:S(2)}, u32[]{:S(2)}) %collective-permute-start.5) | collective-permute-done | bytes 65568 | tf_op jit(solution)/shard_map/ppermute | solution.py:299
  26.3 0.2 level_kernel.4.refs_0_.refs_14_
  26.6 1.3 %collective-permute-start.11 = (f32[128,128]{1,0:T(8,128)S(1)}, f32[128,128]{1,0:T(8,128)S(1)}, u32[]{:S(2)}, u32[]{:S(2)}) collective-permute-start(f32[128,128]{1,0:T(8,128)S(1)} %level_kernel.4.refs_0_.refs_14_), channel_id=1, source_target_pairs={{0,8},{1,9},{2,10},{3,11},{4,12},{5,13},{6,14},{7,15},{8,0},{9,1},... | collective-permute-start | bytes 196616 | tf_op jit(solution)/shard_map/ppermute | solution.py:299
  27.9 0.7 %collective-permute-done.14.refs_1_ = f32[2,128,128]{2,1,0:T(8,128)S(1)} collective-permute-done((f32[2,128,128]{2,1,0:T(8,128)S(1)}, f32[2,128,128]{2,1,0:T(8,128)S(1)}, u32[]{:S(2)}, u32[]{:S(2)}) %collective-permute-start.14) | collective-permute-done | bytes 131104 | tf_op jit(solution)/shard_map/ppermute | solution.py:299
  28.6 0.1 collective-permute-start.15
  28.7 0.8 %collective-permute-start.18 = (f32[2,128,128]{2,1,0:T(8,128)S(1)}, f32[2,128,128]{2,1,0:T(8,128)S(1)}, u32[]{:S(2)}, u32[]{:S(2)}) collective-permute-start(f32[2,128,128]{2,1,0:T(8,128)S(1)} %kernel.47.refs_0_), channel_id=1, source_target_pairs={{0,4},{1,3},{2,6},{3,1},{4,0},{5,7},{6,2},{7,5},{8,12},{9,11},{10,... | collective-permute-start | bytes 393224 | tf_op jit(solution)/shard_map/ppermute | solution.py:299
  29.5 0.5 %collective-permute-done.15.refs_1_ = f32[2,128,128]{2,1,0:T(8,128)S(1)} collective-permute-done((f32[2,128,128]{2,1,0:T(8,128)S(1)}, f32[2,128,128]{2,1,0:T(8,128)S(1)}, u32[]{:S(2)}, u32[]{:S(2)}) %collective-permute-start.15) | collective-permute-done | bytes 131104 | tf_op jit(solution)/shard_map/ppermute | solution.py:292
  30.0 0.9 %collective-permute-done.11.refs_1_.refs_15_ = f32[128,128]{1,0:T(8,128)S(1)} collective-permute-done((f32[128,128]{1,0:T(8,128)S(1)}, f32[128,128]{1,0:T(8,128)S(1)}, u32[]{:S(2)}, u32[]{:S(2)}) %collective-permute-start.11) | collective-permute-done | bytes 65568 | tf_op jit(solution)/shard_map/ppermute | solution.py:299
  30.9 0.2 level_kernel.5.refs_0_.refs_17_.own_ref
  31.1 2.2 %collective-permute-start.17 = (f32[128,128]{1,0:T(8,128)S(1)}, f32[128,128]{1,0:T(8,128)S(1)}, u32[]{:S(2)}, u32[]{:S(2)}) collective-permute-start(f32[128,128]{1,0:T(8,128)S(1)} %level_kernel.5.refs_0_.refs_17_.own_ref), channel_id=1, source_target_pairs={{0,16},{1,17},{2,18},{3,19},{4,20},{5,21},{6,22},{7,23},{8,24},{9,... | collective-permute-start | bytes 196616 | tf_op jit(solution)/shard_map/ppermute | solution.py:299
  33.3 0.4 %collective-permute-done.18.refs_1_ = f32[2,128,128]{2,1,0:T(8,128)S(1)} collective-permute-done((f32[2,128,128]{2,1,0:T(8,128)S(1)}, f32[2,128,128]{2,1,0:T(8,128)S(1)}, u32[]{:S(2)}, u32[]{:S(2)}) %collective-permute-start.18) | collective-permute-done | bytes 131104 | tf_op jit(solution)/shard_map/ppermute | solution.py:299
  33.7 0.1 collective-permute-start.19
  33.9 0.5 %collective-permute-start.16 = (f32[3,128,128]{2,1,0:T(8,128)S(1)}, f32[3,128,128]{2,1,0:T(8,128)S(1)}, u32[]{:S(2)}, u32[]{:S(2)}) collective-permute-start(f32[3,128,128]{2,1,0:T(8,128)S(1)} %kernel.45.refs_0_), channel_id=1, source_target_pairs={{0,1},{1,0},{2,3},{3,2},{4,5},{5,4},{6,7},{7,6},{8,9},{9,8},{10,11... | collective-permute-start | bytes 589832 | tf_op jit(solution)/shard_map/ppermute | solution.py:292
  34.4 1.1 %collective-permute-done.16.refs_1_ = f32[3,128,128]{2,1,0:T(8,128)S(1)} collective-permute-done((f32[3,128,128]{2,1,0:T(8,128)S(1)}, f32[3,128,128]{2,1,0:T(8,128)S(1)}, u32[]{:S(2)}, u32[]{:S(2)}) %collective-permute-start.16) | collective-permute-done | bytes 196640 | tf_op jit(solution)/shard_map/ppermute | solution.py:292
  35.5 1.7 %fold_kernel.1 = (f32[1024,128]{1,0:T(8,128)S(1)}, f32[1024,128]{1,0:T(8,128)S(1)}) custom-call(f32[1024,128]{1,0:T(8,128)S(1)} %get-tuple-element.35.refs_5_.refs_0_, f32[1024,128]{1,0:T(8,128)S(1)} %get-tuple-element.36.refs_1_, f32[1,256,256]{2,1,0:T(8,128)S(1)} %get-tuple-element.37.refs_2_, f32[1,128,128]{2,1,0:T(8,128)S(1)} %get-tuple-element.38.refs_3_, ...), custom_call_target="tpu_custom_call" | custom-call | flops 2000000000 | bytes 1000 | tf_op jit(solution)/shard_map/fold_kernel/pallas_call | solution.py:56
  37.2 0.0 collective-permute-done.19.refs_1_
  37.3 0.0 collective-permute-done.17.other_ref
  37.3 1.3 %shard_map.163 = f32[1024,128]{1,0:T(8,128)} custom-call(f32[1024,128]{1,0:T(8,128)S(1)} %get-tuple-element.56.base_ref, f32[1024,128]{1,0:T(8,128)S(1)} %get-tuple-element.57.refs_2_.weight_ref, f32[128,128]{1,0:T(8,128)S(1)} %level_kernel.5.refs_0_.refs_17_.own_ref, f32[128,128]{1,0:T(8,128)S(1)} %collective-permute-done.17.other_ref, ...), custom_call_target="tpu_custom_call" | custom-call | tf_op jit(solution)/shard_map/pallas_call | solution.py:432
  (30 shorter events, 0.5 us)
Async XLA Ops:
  1.5 11.4 %collective-permute-start.2 = (f32[5,128,128]{2,1,0:T(8,128)S(1)}, f32[5,128,128]{2,1,0:T(8,128)S(1)}, u32[]{:S(2)}, u32[]{:S(2)}) collective-permute-start(f32[5,128,128]{2,1,0:T(8,128)S(1)} %get-tuple-element.48.refs_0_), channel_id=1, source_target_pairs={{0,2},{1,17},{2,0},{3,19},{4,6},{5,21},{6,4},{7,23},{8,10},{9,25},... | collective-permute-start | bytes 983048 | tf_op jit(solution)/shard_map/ppermute | solution.py:299
  4.5 10.6 %collective-permute-start.6 = (f32[5,128,128]{2,1,0:T(8,128)S(1)}, f32[5,128,128]{2,1,0:T(8,128)S(1)}, u32[]{:S(2)}, u32[]{:S(2)}) collective-permute-start(f32[5,128,128]{2,1,0:T(8,128)S(1)} %get-tuple-element.48.refs_0_), channel_id=1, source_target_pairs={{0,8},{1,5},{2,10},{3,7},{4,12},{5,1},{6,14},{7,3},{8,0},{9,13},{1... | collective-permute-start | bytes 983048 | tf_op jit(solution)/shard_map/ppermute | solution.py:299
  10.6 1.8 %collective-permute-start = (f32[128,128]{1,0:T(8,128)S(1)}, f32[128,128]{1,0:T(8,128)S(1)}, u32[]{:S(2)}, u32[]{:S(2)}) collective-permute-start(f32[128,128]{1,0:T(8,128)S(1)} %get-tuple-element.42.refs_0_), channel_id=1, source_target_pairs={{0,1},{1,0},{2,3},{3,2},{4,5},{5,4},{6,7},{7,6},{8,9},{9,8},{10,11... | collective-permute-start | bytes 196616 | tf_op jit(solution)/shard_map/ppermute | solution.py:292
  13.0 6.1 %collective-permute-start.4 = (f32[2,128,128]{2,1,0:T(8,128)S(1)}, f32[2,128,128]{2,1,0:T(8,128)S(1)}, u32[]{:S(2)}, u32[]{:S(2)}) collective-permute-start(f32[2,128,128]{2,1,0:T(8,128)S(1)} %kernel.27.refs_0_), channel_id=1, source_target_pairs={{0,1},{1,0},{2,3},{3,2},{4,5},{5,4},{6,7},{7,6},{8,9},{9,8},{10,11... | collective-permute-start | bytes 393224 | tf_op jit(solution)/shard_map/ppermute | solution.py:292
  13.3 5.8 %collective-permute-start.1 = (f32[128,128]{1,0:T(8,128)S(1)}, f32[128,128]{1,0:T(8,128)S(1)}, u32[]{:S(2)}, u32[]{:S(2)}) collective-permute-start(f32[128,128]{1,0:T(8,128)S(1)} %get-tuple-element.46.refs_0_.refs_8_), channel_id=1, source_target_pairs={{0,2},{1,3},{2,0},{3,1},{4,6},{5,7},{6,4},{7,5},{8,10},{9,11},{10,... | collective-permute-start | bytes 196616 | tf_op jit(solution)/shard_map/ppermute | solution.py:299
  15.3 8.1 %collective-permute-start.13 = (f32[2,128,128]{2,1,0:T(8,128)S(1)}, f32[2,128,128]{2,1,0:T(8,128)S(1)}, u32[]{:S(2)}, u32[]{:S(2)}) collective-permute-start(f32[2,128,128]{2,1,0:T(8,128)S(1)} %top_kernel.1.refs_0_), channel_id=1, source_target_pairs={{0,4},{1,9},{2,6},{3,11},{4,0},{5,13},{6,2},{7,15},{8,12},{9,1},{1... | collective-permute-start | bytes 393224 | tf_op jit(solution)/shard_map/ppermute | solution.py:299
  16.9 5.0 %collective-permute-start.9 = (f32[2,128,128]{2,1,0:T(8,128)S(1)}, f32[2,128,128]{2,1,0:T(8,128)S(1)}, u32[]{:S(2)}, u32[]{:S(2)}) collective-permute-start(f32[2,128,128]{2,1,0:T(8,128)S(1)} %kernel.36), channel_id=1, source_target_pairs={{0,4},{1,3},{2,6},{3,1},{4,0},{5,7},{6,2},{7,5},{8,12},{9,11},{10,... | collective-permute-start | bytes 393224 | tf_op jit(solution)/shard_map/ppermute | solution.py:299
  17.5 6.9 %collective-permute-start.7 = (f32[3,128,128]{2,1,0:T(8,128)S(1)}, f32[3,128,128]{2,1,0:T(8,128)S(1)}, u32[]{:S(2)}, u32[]{:S(2)}) collective-permute-start(f32[3,128,128]{2,1,0:T(8,128)S(1)} %kernel.31), channel_id=1, source_target_pairs={{0,4},{1,3},{2,6},{3,1},{4,0},{5,7},{6,2},{7,5},{8,12},{9,11},{10,... | collective-permute-start | bytes 589832 | tf_op jit(solution)/shard_map/ppermute | solution.py:299
  19.1 6.7 %collective-permute-start.3 = (f32[3,128,128]{2,1,0:T(8,128)S(1)}, f32[3,128,128]{2,1,0:T(8,128)S(1)}, u32[]{:S(2)}, u32[]{:S(2)}) collective-permute-start(f32[3,128,128]{2,1,0:T(8,128)S(1)} %kernel.25.refs_0_), channel_id=1, source_target_pairs={{0,1},{1,0},{2,3},{3,2},{4,5},{5,4},{6,7},{7,6},{8,9},{9,8},{10,11... | collective-permute-start | bytes 589832 | tf_op jit(solution)/shard_map/ppermute | solution.py:292
  22.0 4.3 %collective-permute-start.5 = (f32[128,128]{1,0:T(8,128)S(1)}, f32[128,128]{1,0:T(8,128)S(1)}, u32[]{:S(2)}, u32[]{:S(2)}) collective-permute-start(f32[128,128]{1,0:T(8,128)S(1)} %level_kernel.3.refs_0_.refs_11_), channel_id=1, source_target_pairs={{0,4},{1,5},{2,6},{3,7},{4,0},{5,1},{6,2},{7,3},{8,12},{9,13},{10,... | collective-permute-start | bytes 196616 | tf_op jit(solution)/shard_map/ppermute | solution.py:299
  23.4 2.4 %collective-permute-start.10 = (f32[2,128,128]{2,1,0:T(8,128)S(1)}, f32[2,128,128]{2,1,0:T(8,128)S(1)}, u32[]{:S(2)}, u32[]{:S(2)}) collective-permute-start(f32[2,128,128]{2,1,0:T(8,128)S(1)} %kernel.37.refs_0_), channel_id=1, source_target_pairs={{0,1},{1,0},{2,3},{3,2},{4,5},{5,4},{6,7},{7,6},{8,9},{9,8},{10,11... | collective-permute-start | bytes 393224 | tf_op jit(solution)/shard_map/ppermute | solution.py:292
  23.5 5.0 %collective-permute-start.14 = (f32[2,128,128]{2,1,0:T(8,128)S(1)}, f32[2,128,128]{2,1,0:T(8,128)S(1)}, u32[]{:S(2)}, u32[]{:S(2)}) collective-permute-start(f32[2,128,128]{2,1,0:T(8,128)S(1)} %kernel.42), channel_id=1, source_target_pairs={{0,2},{1,5},{2,0},{3,7},{4,6},{5,1},{6,4},{7,3},{8,10},{9,13},{10,... | collective-permute-start | bytes 393224 | tf_op jit(solution)/shard_map/ppermute | solution.py:299
  24.5 9.3 %collective-permute-start.12 = (f32[3,128,128]{2,1,0:T(8,128)S(1)}, f32[3,128,128]{2,1,0:T(8,128)S(1)}, u32[]{:S(2)}, u32[]{:S(2)}) collective-permute-start(f32[3,128,128]{2,1,0:T(8,128)S(1)} %kernel.39.refs_0_), channel_id=1, source_target_pairs={{0,2},{1,5},{2,0},{3,7},{4,6},{5,1},{6,4},{7,3},{8,10},{9,13},{10,... | collective-permute-start | bytes 589832 | tf_op jit(solution)/shard_map/ppermute | solution.py:299
  25.7 3.7 %collective-permute-start.8 = (f32[3,128,128]{2,1,0:T(8,128)S(1)}, f32[3,128,128]{2,1,0:T(8,128)S(1)}, u32[]{:S(2)}, u32[]{:S(2)}) collective-permute-start(f32[3,128,128]{2,1,0:T(8,128)S(1)} %kernel.32.refs_0_), channel_id=1, source_target_pairs={{0,1},{1,0},{2,3},{3,2},{4,5},{5,4},{6,7},{7,6},{8,9},{9,8},{10,11... | collective-permute-start | bytes 589832 | tf_op jit(solution)/shard_map/ppermute | solution.py:292
  26.6 4.3 %collective-permute-start.11 = (f32[128,128]{1,0:T(8,128)S(1)}, f32[128,128]{1,0:T(8,128)S(1)}, u32[]{:S(2)}, u32[]{:S(2)}) collective-permute-start(f32[128,128]{1,0:T(8,128)S(1)} %level_kernel.4.refs_0_.refs_14_), channel_id=1, source_target_pairs={{0,8},{1,9},{2,10},{3,11},{4,12},{5,13},{6,14},{7,15},{8,0},{9,1},... | collective-permute-start | bytes 196616 | tf_op jit(solution)/shard_map/ppermute | solution.py:299
  28.6 1.4 %collective-permute-start.15 = (f32[2,128,128]{2,1,0:T(8,128)S(1)}, f32[2,128,128]{2,1,0:T(8,128)S(1)}, u32[]{:S(2)}, u32[]{:S(2)}) collective-permute-start(f32[2,128,128]{2,1,0:T(8,128)S(1)} %kernel.43.refs_0_), channel_id=1, source_target_pairs={{0,1},{1,0},{2,3},{3,2},{4,5},{5,4},{6,7},{7,6},{8,9},{9,8},{10,11... | collective-permute-start | bytes 393224 | tf_op jit(solution)/shard_map/ppermute | solution.py:292
  28.7 5.0 %collective-permute-start.18 = (f32[2,128,128]{2,1,0:T(8,128)S(1)}, f32[2,128,128]{2,1,0:T(8,128)S(1)}, u32[]{:S(2)}, u32[]{:S(2)}) collective-permute-start(f32[2,128,128]{2,1,0:T(8,128)S(1)} %kernel.47.refs_0_), channel_id=1, source_target_pairs={{0,4},{1,3},{2,6},{3,1},{4,0},{5,7},{6,2},{7,5},{8,12},{9,11},{10,... | collective-permute-start | bytes 393224 | tf_op jit(solution)/shard_map/ppermute | solution.py:299
  31.1 6.2 %collective-permute-start.17 = (f32[128,128]{1,0:T(8,128)S(1)}, f32[128,128]{1,0:T(8,128)S(1)}, u32[]{:S(2)}, u32[]{:S(2)}) collective-permute-start(f32[128,128]{1,0:T(8,128)S(1)} %level_kernel.5.refs_0_.refs_17_.own_ref), channel_id=1, source_target_pairs={{0,16},{1,17},{2,18},{3,19},{4,20},{5,21},{6,22},{7,23},{8,24},{9,... | collective-permute-start | bytes 196616 | tf_op jit(solution)/shard_map/ppermute | solution.py:299
  33.7 3.5 %collective-permute-start.19 = (f32[2,128,128]{2,1,0:T(8,128)S(1)}, f32[2,128,128]{2,1,0:T(8,128)S(1)}, u32[]{:S(2)}, u32[]{:S(2)}) collective-permute-start(f32[2,128,128]{2,1,0:T(8,128)S(1)} %kernel.48.refs_0_), channel_id=1, source_target_pairs={{0,1},{1,0},{2,3},{3,2},{4,5},{5,4},{6,7},{7,6},{8,9},{9,8},{10,11... | collective-permute-start | bytes 393224 | tf_op jit(solution)/shard_map/ppermute | solution.py:292
  33.9 1.6 %collective-permute-start.16 = (f32[3,128,128]{2,1,0:T(8,128)S(1)}, f32[3,128,128]{2,1,0:T(8,128)S(1)}, u32[]{:S(2)}, u32[]{:S(2)}) collective-permute-start(f32[3,128,128]{2,1,0:T(8,128)S(1)} %kernel.45.refs_0_), channel_id=1, source_target_pairs={{0,1},{1,0},{2,3},{3,2},{4,5},{5,4},{6,7},{7,6},{8,9},{9,8},{10,11... | collective-permute-start | bytes 589832 | tf_op jit(solution)/shard_map/ppermute | solution.py:292
